TPU v7x, 512 devices: a whole 4x8x8 slice. The times are simulated.
512 devices in a mesh: dp: 32 (over x_hi, z, core), cuts: 16 (over x_lo, y).
Axes of the slice: x: 4 (x_hi: 2, x_lo: 2; x = x_hi * 2 + x_lo), y: 8, z: 8, core: 2. Of those that a mesh axis runs over, the one named last changes fastest.
Arguments:
- tokens: bfloat16 [4096, 2048], P('dp', 'cuts'), may hold values from -6 to 6
- cotangent: bfloat16 [4096, 2048], P('dp', 'cuts'), may hold values from -6 to 6
- gates: float32 [4096, 2], P('dp'), may hold values from 0.1 to 1
- routes: int32 [4096, 2], P('dp'), may hold values from 0 to 31, all different within a row; in each aligned block of 128 rows (0 to 127, 128 to 255, ...) at most 12 rows name the same one
- w_in: bfloat16 [32, 2048, 4096], P('dp', None, 'cuts'), may hold values from -0.125 to 0.125
- w_out: bfloat16 [32, 4096, 2048], P('dp', 'cuts'), may hold values from -0.09375 to 0.09375
Outputs:
- mixed: bfloat16 [4096, 2048], P('dp', 'cuts')
- token_grad: bfloat16 [4096, 2048], P('dp', 'cuts')
- grad_in: bfloat16 [32, 2048, 4096], P('dp', None, 'cuts')
- grad_out: bfloat16 [32, 4096, 2048], P('dp', 'cuts')
Inputs may be any that keep to these rules, and one draw needn't show every extreme that they name: `routes`: each row names 2 different experts. Within the rows of one device (aligned blocks of 128 rows) no expert is named by more than 12 rows, a bound that some block reaches.
All inputs are finite; a program needn't handle non-finite values.
Results may differ from a plain program's by a relative error of at most 0.024.
Values may be sent and summed in bfloat16 or wider, within the bound.
No kernel may reach another device: no remote copies, remote signals or barrier semaphores. Data moves between devices by JAX's collectives and lax.ppermute only.
A program may use at most 64 MiB of HBM per device.

v0:
```python
import math

import jax
import jax.numpy as jnp
from jax import lax
from jax.sharding import PartitionSpec as P


def gelu_parts(pre):
    coef = math.sqrt(2.0 / math.pi)
    inner = coef * (pre + 0.044715 * pre * pre * pre)
    tangent = jnp.tanh(inner)
    value = 0.5 * pre * (1.0 + tangent)
    slope = 0.5 * (1.0 + tangent) + 0.5 * pre * (1.0 - tangent * tangent) * coef * (
        1.0 + 3.0 * 0.044715 * pre * pre
    )
    return (value, slope)


def slot_targets(routes, capacity, experts):
    flat = routes.reshape(-1)
    onehot = (flat[:, None] == jnp.arange(experts, dtype=jnp.int32)[None, :]).astype(jnp.int32)
    before = jnp.cumsum(onehot, axis=0) - onehot
    position = jnp.sum(before * onehot, axis=1)
    return flat * capacity + position


def contract_last(left, right):
    return lax.dot_general(
        left, right, (((1,), (1,)), ((), ())), preferred_element_type=jnp.float32
    )


def contract_first(left, right):
    return lax.dot_general(
        left, right, (((0,), (0,)), ((), ())), preferred_element_type=jnp.float32
    )


def body(tokens, cotangent, gates, routes, w_in, w_out):
    experts = lax.axis_size("dp")
    tok_rows = routes.shape[0]
    chosen = routes.shape[1]
    capacity = 3 * chosen * tok_rows // (2 * experts)
    slots = experts * capacity
    target = slot_targets(routes, capacity, experts)
    placing = (jnp.arange(slots, dtype=jnp.int32)[:, None] == target[None, :]).astype(jnp.bfloat16)
    weights = gates.reshape(-1, 1)
    full_x, full_g = (
        lax.all_gather(tokens, "cuts", axis=1, tiled=True),
        lax.all_gather(cotangent, "cuts", axis=1, tiled=True),
    )
    rep_x = jnp.repeat(full_x, chosen, axis=0)
    scaled = (weights * jnp.repeat(full_g, chosen, axis=0).astype(jnp.float32)).astype(jnp.bfloat16)
    sent_x = jnp.dot(placing, rep_x, preferred_element_type=jnp.float32).astype(jnp.bfloat16)
    sent_g = jnp.dot(placing, scaled, preferred_element_type=jnp.float32).astype(jnp.bfloat16)
    send_x = sent_x.reshape(experts, capacity, -1)
    send_g = sent_g.reshape(experts, capacity, -1)
    recv_x, recv_g = (
        lax.all_to_all(send_x, "dp", split_axis=0, concat_axis=0, tiled=True),
        lax.all_to_all(send_g, "dp", split_axis=0, concat_axis=0, tiled=True),
    )
    width = recv_x.shape[2]
    rows_x = recv_x.reshape(slots, width)
    rows_g = recv_g.reshape(slots, width)
    first = w_in[0]
    second = w_out[0]
    pre = jnp.dot(rows_x, first, preferred_element_type=jnp.float32)
    value, slope = gelu_parts(pre)
    active = value.astype(jnp.bfloat16)
    dpre = (contract_last(rows_g, second) * slope).astype(jnp.bfloat16)
    out_part = jnp.dot(active, second, preferred_element_type=jnp.float32)
    back_part = contract_last(dpre, first)
    grad_in = contract_first(rows_x, dpre).astype(jnp.bfloat16)[None]
    grad_out = contract_first(active, rows_g).astype(jnp.bfloat16)[None]
    sum_out, sum_back = (
        lax.psum_scatter(
            out_part.reshape(experts, capacity, width).astype(jnp.bfloat16),
            "cuts",
            scatter_dimension=2,
            tiled=True,
        ).astype(jnp.float32),
        lax.psum_scatter(
            back_part.reshape(experts, capacity, width).astype(jnp.bfloat16),
            "cuts",
            scatter_dimension=2,
            tiled=True,
        ).astype(jnp.float32),
    )
    home_out, home_back = (
        lax.all_to_all(
            sum_out.astype(jnp.bfloat16), "dp", split_axis=0, concat_axis=0, tiled=True
        ).astype(sum_out.dtype),
        lax.all_to_all(
            sum_back.astype(jnp.bfloat16), "dp", split_axis=0, concat_axis=0, tiled=True
        ).astype(sum_back.dtype),
    )
    narrow = home_out.shape[2]
    picked_out = home_out.reshape(slots, narrow)[target]
    picked_back = home_back.reshape(slots, narrow)[target]
    mixed = (
        (weights * picked_out).reshape(tok_rows, chosen, narrow).sum(axis=1).astype(jnp.bfloat16)
    )
    token_grad = picked_back.reshape(tok_rows, chosen, narrow).sum(axis=1).astype(jnp.bfloat16)
    return (mixed, token_grad, grad_in, grad_out)


def solution(mesh):
    in_specs = (
        P("dp", "cuts"),
        P("dp", "cuts"),
        P("dp", None),
        P("dp", None),
        P("dp", None, "cuts"),
        P("dp", "cuts", None),
    )
    out_specs = (P("dp", "cuts"), P("dp", "cuts"), P("dp", None, "cuts"), P("dp", "cuts", None))
    return jax.shard_map(body, mesh=mesh, in_specs=in_specs, out_specs=out_specs, check_vma=False)
```

profile of v0, /device:TPU:1, one launch (start us, length us, event | category | flops | bytes accessed | tf_op | source)
XLA Modules:
  0.0 375.3 jit_solution(84646023119937118)
XLA Ops:
  9.3 30.6 %all_gather.6 = bf16[128,2048]{1,0:T(8,128)(2,1)S(1)} all-gather(bf16[128,128]{1,0:T(8,128)(2,1)} %param.6), channel_id=1, replica_groups=mesh['dp'=32,'cuts'=16] {'cuts'}, dimensions={1}, use_global_device_ids=true | all-gather | bytes 557056 | tf_op jit(solution)/shard_map/all_gather | solution.py:50
  40.5 1.2 reshape.111
  41.7 1.8 convolution_convert_fusion.3
  43.5 1.5 reshape.112
  45.1 20.6 %all-to-all-start = ((bf16[32,12,2048]{2,1,0:T(8,128)(2,1)}), bf16[32,12,2048]{2,1,0:T(8,128)(2,1)S(1)}, u32[]{:S(2)}, u32[]{:S(2)}) async-start(bf16[32,12,2048]{2,1,0:T(8,128)(2,1)} %reshape.112), calls=%async_computation | async-start | bytes 4194304 | tf_op jit(solution)/shard_map/all_to_all | solution.py:60
  66.0 28.6 %all_gather.7 = bf16[128,2048]{1,0:T(8,128)(2,1)S(1)} all-gather(bf16[128,128]{1,0:T(8,128)(2,1)S(1)} %copy-done.2), channel_id=1, replica_groups=mesh['dp'=32,'cuts'=16] {'cuts'}, dimensions={1}, use_global_device_ids=true | all-gather | bytes 557056 | tf_op jit(solution)/shard_map/all_gather | solution.py:51
  94.6 2.4 broadcast_in_dim.18
  97.0 3.7 convert_element_type.61
  100.6 3.4 convolution_convert_fusion.1
  104.1 3.6 reshape.116
  107.7 8.9 %all-to-all-done = bf16[32,12,2048]{2,1,0:T(8,128)(2,1)S(1)} async-done(((bf16[32,12,2048]{2,1,0:T(8,128)(2,1)}), bf16[32,12,2048]{2,1,0:T(8,128)(2,1)S(1)}, u32[]{:S(2)}, u32[]{:S(2)}) %all-to-all-start) | async-done | bytes 1572896 | tf_op jit(solution)/shard_map/all_to_all | solution.py:60
  116.6 5.8 %all-to-all-start.2 = ((bf16[32,12,2048]{2,1,0:T(8,128)(2,1)}), bf16[32,12,2048]{2,1,0:T(8,128)(2,1)}, u32[]{:S(2)}, u32[]{:S(2)}) async-start(bf16[32,12,2048]{2,1,0:T(8,128)(2,1)} %reshape.116), calls=%async_computation.2 | async-start | bytes 4194304 | tf_op jit(solution)/shard_map/all_to_all | solution.py:61
  122.5 1.4 reshape.113
  123.9 2.8 multiply_convert_fusion.2
  126.7 46.7 %all-to-all-done.2 = bf16[32,12,2048]{2,1,0:T(8,128)(2,1)} async-done(((bf16[32,12,2048]{2,1,0:T(8,128)(2,1)}), bf16[32,12,2048]{2,1,0:T(8,128)(2,1)}, u32[]{:S(2)}, u32[]{:S(2)}) %all-to-all-start.2) | async-done | bytes 1572896 | tf_op jit(solution)/shard_map/all_to_all | solution.py:61
  173.4 2.5 reshape.117
  175.9 2.0 fusion.2
  178.0 1.8 convolution_convert_fusion
  179.7 10.0 %copy.35 = bf16[32,12,2048]{0,1,2:T(8,128)(2,1)} copy(bf16[32,12,2048]{2,0,1:T(8,128)(2,1)} %convolution_convert_fusion) | data formatting | bytes 3145728
  189.7 10.3 %reshape.145 = bf16[2048,384]{1,0:T(8,128)(2,1)} reshape(bf16[2048,12,32]{2,1,0:T(8,128)(2,1)} %bitcast.54) | data formatting | bytes 3145728
  200.3 3.0 convolution_convert_fusion.2
  203.3 10.0 %copy.33 = bf16[32,12,2048]{0,1,2:T(8,128)(2,1)} copy(bf16[32,12,2048]{2,0,1:T(8,128)(2,1)} %convolution_convert_fusion.2) | data formatting | bytes 3145728
  213.3 10.3 %reshape.143 = bf16[2048,384]{1,0:T(8,128)(2,1)} reshape(bf16[2048,12,32]{2,1,0:T(8,128)(2,1)} %bitcast.55) | data formatting | bytes 3145728
  224.6 32.8 %reduce-scatter.9.cloned.1.call-done = bf16[128,384]{1,0:T(8,128)(2,1)} async-done(((bf16[2048,384]{1,0:T(8,128)(2,1)}), bf16[128,384]{1,0:T(8,128)(2,1)}) %reduce-scatter.9.cloned.1.call-update) | async-done | bytes 98320
  257.3 1.3 reshape.146
  259.8 21.2 %all-to-all-start.3 = ((bf16[32,12,128]{2,1,0:T(8,128)(2,1)}), bf16[32,12,128]{2,1,0:T(8,128)(2,1)S(1)}, u32[]{:S(2)}, u32[]{:S(2)}) async-start(bf16[32,12,128]{2,1,0:T(8,128)(2,1)} %copy.32), calls=%async_computation.3 | async-start | bytes 262144 | tf_op jit(solution)/shard_map/all_to_all | solution.py:94
  281.0 3.2 fusion
  284.2 47.8 %reduce-scatter.7.cloned.1.call-done = bf16[128,384]{1,0:T(8,128)(2,1)} async-done(((bf16[2048,384]{1,0:T(8,128)(2,1)}), bf16[128,384]{1,0:T(8,128)(2,1)}) %reduce-scatter.7.cloned.1.call-update) | async-done | bytes 98320
  332.0 1.3 reshape.144
  334.4 21.1 %all-to-all-start.1 = ((bf16[32,12,128]{2,1,0:T(8,128)(2,1)}), bf16[32,12,128]{2,1,0:T(8,128)(2,1)S(1)}, u32[]{:S(2)}, u32[]{:S(2)}) async-start(bf16[32,12,128]{2,1,0:T(8,128)(2,1)} %copy.28), calls=%async_computation.1 | async-start | bytes 262144 | tf_op jit(solution)/shard_map/all_to_all | solution.py:91
  355.5 1.7 fusion.1
  357.9 8.1 %all-to-all-done.1 = bf16[32,12,128]{2,1,0:T(8,128)(2,1)S(1)} async-done(((bf16[32,12,128]{2,1,0:T(8,128)(2,1)}), bf16[32,12,128]{2,1,0:T(8,128)(2,1)S(1)}, u32[]{:S(2)}, u32[]{:S(2)}) %all-to-all-start.1) | async-done | bytes 98336 | tf_op jit(solution)/shard_map/all_to_all | solution.py:91
  (43 shorter events, 9.7 us)
Async XLA Ops:
  7.2 116.7 %copy-start = (bf16[1,2048,256]{2,1,0:T(8,128)(2,1)S(1)}, bf16[1,2048,256]{2,1,0:T(8,128)(2,1)}, u32[]{:S(2)}) copy-start(bf16[1,2048,256]{2,1,0:T(8,128)(2,1)} %param.10) | copy-start | bytes 3145732
  45.1 20.7 %copy-start.4 = (f32[128,2]{0,1:T(2,128)S(1)}, f32[128,2]{0,1:T(2,128)}, u32[]{:S(2)}) copy-start(f32[128,2]{0,1:T(2,128)} %param.8) | copy-start | bytes 3076
  45.1 20.9 %copy-start.2 = (bf16[128,128]{1,0:T(8,128)(2,1)S(1)}, bf16[128,128]{1,0:T(8,128)(2,1)}, u32[]{:S(2)}) copy-start(bf16[128,128]{1,0:T(8,128)(2,1)} %param.7) | copy-start | bytes 98308
  45.1 71.5 %all-to-all-start = ((bf16[32,12,2048]{2,1,0:T(8,128)(2,1)}), bf16[32,12,2048]{2,1,0:T(8,128)(2,1)S(1)}, u32[]{:S(2)}, u32[]{:S(2)}) async-start(bf16[32,12,2048]{2,1,0:T(8,128)(2,1)} %reshape.112), calls=%async_computation | async-start | bytes 4194304 | tf_op jit(solution)/shard_map/all_to_all | solution.py:60
  116.6 56.8 %all-to-all-start.2 = ((bf16[32,12,2048]{2,1,0:T(8,128)(2,1)}), bf16[32,12,2048]{2,1,0:T(8,128)(2,1)}, u32[]{:S(2)}, u32[]{:S(2)}) async-start(bf16[32,12,2048]{2,1,0:T(8,128)(2,1)} %reshape.116), calls=%async_computation.2 | async-start | bytes 4194304 | tf_op jit(solution)/shard_map/all_to_all | solution.py:61
  122.4 134.9 %reduce-scatter.9.cloned.1.call-start = ((), (), s32[]{:S(2)}) async-start(), calls=%async_computation.7 | async-start | bytes 1671168
  177.9 1.8 copy-start.1
  200.0 131.9 %reduce-scatter.7.cloned.1.call-start = ((), (), s32[]{:S(2)}) async-start(), calls=%async_computation.6 | async-start | bytes 1671168
  223.6 0.7 copy-start.3
  259.8 74.6 %all-to-all-start.3 = ((bf16[32,12,128]{2,1,0:T(8,128)(2,1)}), bf16[32,12,128]{2,1,0:T(8,128)(2,1)S(1)}, u32[]{:S(2)}, u32[]{:S(2)}) async-start(bf16[32,12,128]{2,1,0:T(8,128)(2,1)} %copy.32), calls=%async_computation.3 | async-start | bytes 262144 | tf_op jit(solution)/shard_map/all_to_all | solution.py:94
  334.4 31.7 %all-to-all-start.1 = ((bf16[32,12,128]{2,1,0:T(8,128)(2,1)}), bf16[32,12,128]{2,1,0:T(8,128)(2,1)S(1)}, u32[]{:S(2)}, u32[]{:S(2)}) async-start(bf16[32,12,128]{2,1,0:T(8,128)(2,1)} %copy.28), calls=%async_computation.1 | async-start | bytes 262144 | tf_op jit(solution)/shard_map/all_to_all | solution.py:91
Sparse Core Ops, SparseCore 0:
  200.2 57.1 reduce-scatter.8
  260.4 71.5 reduce-scatter.6
where the time goes:
time: 377 us; the launch traced here: 375 us
  waiting for transfers between devices  144 us (38%)
  starting transfers between devices  69.1 us (18%)
  local copies, waits for them, and re-layouts  66.4 us (18%)
  blocking collectives  59.2 us (16%)
  matrix products  19.6 us (5%)
  between operations  14.2 us (4%)
    unnamed x4, waiting for transfers between devices  80.6 us
    all_to_all x1, waiting for transfers between devices, body(): lax.all_to_all(send_g, 'dp', split_axis=0, concat_axis=0, tiled=True)  46.7 us
    unnamed x18, local copies, waits for them, and re-layouts  44.7 us
    all_gather x1, blocking collectives, body(): lax.all_gather(tokens, 'cuts', axis=1, tiled=True)  30.6 us
    all_gather x1, blocking collectives, body(): lax.all_gather(cotangent, 'cuts', axis=1, tiled=True)  28.6 us
    all_to_all x1, starting transfers between devices, body(): lax.all_to_all(sum_back.astype(jnp.bfloat16), 'dp', split_axis=0, concat_...  21.2 us
    all_to_all x1, starting transfers between devices, body(): lax.all_to_all(sum_out.astype(jnp.bfloat16), 'dp', split_axis=0, concat_a...  21.1 us
    all_to_all x1, starting transfers between devices, body(): lax.all_to_all(send_x, 'dp', split_axis=0, concat_axis=0, tiled=True)  20.6 us
  transfers between devices with their start and end apart: 6, of which 5 were waited for; matrix products, arithmetic and copies ran while one was open for 14% of the time, Pallas kernels for 0%

commit v1 on v0

v1 whole, which is shorter than its diff:
```python
import functools
import math

import jax
import jax.numpy as jnp
from jax import lax
from jax.experimental import pallas as pl
from jax.experimental.pallas import tpu as pltpu
from jax.sharding import PartitionSpec as P

BF16 = jnp.bfloat16
F32 = jnp.float32
HALVES = 2
PAD = 8


def gelu_parts(pre):
    coef = math.sqrt(2.0 / math.pi)
    inner = coef * (pre + 0.044715 * pre * pre * pre)
    tangent = jnp.tanh(inner)
    value = 0.5 * pre * (1.0 + tangent)
    slope = 0.5 * (1.0 + tangent) + 0.5 * pre * (1.0 - tangent * tangent) * coef * (
        1.0 + 3.0 * 0.044715 * pre * pre
    )
    return (value, slope)


def dot(left, right, dims=((1,), (0,))):
    return lax.dot_general(left, right, (dims, ((), ())), preferred_element_type=F32)


def iota(shape, axis):
    return lax.broadcasted_iota(jnp.int32, shape, axis)


def place_kernel(experts, cap, routes_ref, gates_ref, tok_ref, cot_ref, sent_ref, rows_ref):
    tok_rows, width = tok_ref.shape
    routes = routes_ref[...]
    first, second = routes[0:1, :], routes[1:2, :]
    names = iota((experts, tok_rows), 0)
    hit0, hit1 = names == first, names == second
    either = jnp.where(hit0 | hit1, 1.0, 0.0).astype(BF16)
    earlier = iota((tok_rows, tok_rows), 0) < iota((tok_rows, tok_rows), 1)
    count = dot(either, jnp.where(earlier, 1.0, 0.0).astype(BF16))
    half_cap = cap // HALVES

    def row_of(hit, expert):
        position = jnp.sum(jnp.where(hit, count, 0.0), axis=0, keepdims=True).astype(jnp.int32)
        upper = jnp.where(position >= half_cap, 1, 0)
        return (expert * HALVES + upper) * PAD + position - upper * half_cap

    row0, row1 = row_of(hit0, first), row_of(hit1, second)
    rows_ref[0:1, :] = row0
    rows_ref[1:2, :] = row1
    chunks = experts * HALVES
    slot = iota((chunks * PAD, tok_rows), 0)
    at0, at1 = slot == row0, slot == row1
    gates = gates_ref[...]
    gate = jnp.sum(
        jnp.where(at0, gates[0:1, :], 0.0) + jnp.where(at1, gates[1:2, :], 0.0),
        axis=1,
        keepdims=True,
    )
    select = jnp.where(at0 | at1, 1.0, 0.0).astype(BF16)
    both = dot(select, jnp.concatenate([tok_ref[...], cot_ref[...]], axis=1))
    held_x = both[:, :width].reshape(chunks, PAD, width)
    held_g = (both[:, width:] * gate).reshape(chunks, PAD, width)
    sent_ref[...] = jnp.concatenate([held_x, held_g], axis=1).astype(BF16)


def packing(sources, used):
    shape = (sources * used, sources * PAD)
    at = iota(shape, 1)
    inner = lax.bitwise_and(at, PAD - 1)
    outer = lax.shift_right_logical(at, 3)
    hit = (iota(shape, 0) == outer * used + inner) & (inner < used)
    return jnp.where(hit, 1.0, 0.0).astype(BF16)


def pack_kernel(sources, used, recv_ref, out_ref):
    width = recv_ref.shape[2]
    pick = packing(sources, used)
    held = recv_ref[...].astype(F32).reshape(sources, HALVES, 2, PAD, width)
    rows = sources * used
    for kind in range(2):
        for part in range(HALVES):
            piece = held[:, part, kind].reshape(sources * PAD, width).astype(BF16)
            start = (kind * HALVES + part) * rows
            out_ref[start : start + rows, :] = dot(pick, piece).astype(BF16)


def sum_kernel(sources, used, recv_ref, out_ref):
    groups, _, width = recv_ref.shape
    pick = packing(sources, used)
    rows = sources * used
    kinds = []
    for kind in range(2):
        parts = []
        for part in range(HALVES):
            start = (kind * HALVES + part) * rows
            total = recv_ref[0, start : start + rows, :].astype(F32)
            for group in range(1, groups):
                total = total + recv_ref[group, start : start + rows, :].astype(F32)
            spread = dot(pick, total.astype(BF16), ((0,), (0,)))
            parts.append(spread.reshape(sources, 1, PAD, width))
        kinds.append(jnp.concatenate(parts, axis=1))
    whole = jnp.concatenate(kinds, axis=2)
    out_ref[...] = whole.reshape(sources * HALVES, 2 * PAD, width).astype(BF16)


def expert_kernel(
    recv_ref, in0_ref, in1_ref, out0_ref, out1_ref, ret_ref, x_ref, g_ref, act_ref, dpre_ref
):
    peers, all_rows, width = recv_ref.shape
    rows = all_rows // (2 * HALVES)
    for kind, ref in ((0, x_ref), (1, g_ref)):
        for part in range(HALVES):
            start = (kind * HALVES + part) * rows
            for peer in range(peers):
                at = (part * peers + peer) * width
                ref[:, at : at + width] = recv_ref[peer, start : start + rows, :]
    ins, outs = (in0_ref, in1_ref), (out0_ref, out1_ref)
    acts, dpres = [], []
    for group in range(2):
        pre = dot(x_ref[...], ins[group][...])
        value, slope = gelu_parts(pre)
        backed = dot(g_ref[...], outs[group][...], ((1,), (1,)))
        acts.append(value.astype(BF16))
        dpres.append((backed * slope).astype(BF16))
        act_ref[group] = acts[group]
        dpre_ref[group] = dpres[group]
    for part in range(HALVES):
        for pair in range(peers // 2):
            at = (part * peers + 2 * pair) * width
            cols = slice(at, at + 2 * width)
            given = dot(acts[0], outs[0][:, cols]) + dot(acts[1], outs[1][:, cols])
            back = dot(dpres[0], ins[0][cols, :], ((1,), (1,))) + dot(
                dpres[1], ins[1][cols, :], ((1,), (1,))
            )
            for kind, block in ((0, given), (1, back)):
                block = block.astype(BF16)
                start = (kind * HALVES + part) * rows
                ret_ref[2 * pair, start : start + rows, :] = block[:, :width]
                ret_ref[2 * pair + 1, start : start + rows, :] = block[:, width:]


def combine_kernel(rows_ref, gates_ref, home_ref, mixed_ref, grad_ref):
    chunks, _, width = home_ref.shape
    tok_rows = mixed_ref.shape[0]
    held = home_ref[...].astype(F32)
    given = held[:, :PAD].reshape(chunks * PAD, width).astype(BF16)
    back = held[:, PAD:].reshape(chunks * PAD, width).astype(BF16)
    slot = iota((chunks * PAD, tok_rows), 0)
    at0, at1 = slot == rows_ref[0:1, :], slot == rows_ref[1:2, :]
    diagonal = iota((tok_rows, tok_rows), 0) == iota((tok_rows, tok_rows), 1)

    def mask(hit):
        return jnp.where(hit, 1.0, 0.0).astype(BF16)

    def column(row):
        return jnp.sum(jnp.where(diagonal, row, 0.0), axis=1, keepdims=True)

    over_rows = ((0,), (0,))
    mixed = column(gates_ref[0:1, :]) * dot(mask(at0), given, over_rows) + column(
        gates_ref[1:2, :]
    ) * dot(mask(at1), given, over_rows)
    mixed_ref[...] = mixed.astype(BF16)
    grad_ref[...] = dot(mask(at0 | at1), back, over_rows).astype(BF16)


def call(kernel, shapes, flops, moved, *args):
    return pl.pallas_call(
        kernel,
        out_shape=shapes,
        cost_estimate=pl.CostEstimate(flops=flops, bytes_accessed=moved, transcendentals=0),
        compiler_params=pltpu.CompilerParams(vmem_limit_bytes=40 * 1024 * 1024),
    )(*args)


def struct(*shape, dtype=BF16):
    return jax.ShapeDtypeStruct(shape, dtype)


def body(tokens, cotangent, gates, routes, w_in, w_out):
    experts = lax.axis_size("dp")
    cuts = lax.axis_size("cuts")
    peers = cuts // HALVES
    tok_rows, width = tokens.shape
    chosen = routes.shape[1]
    cap = 3 * chosen * tok_rows // (2 * experts)
    used = cap // HALVES
    chunks = experts * HALVES
    rows = experts * used
    model = width * cuts
    swap = [(c, (c + peers) % cuts) for c in range(cuts)]
    line = [[h * peers + y for y in range(peers)] for h in range(HALVES)]
    plane = [
        [d * cuts + h * peers + y for d in range(experts) for h in range(HALVES)]
        for y in range(peers)
    ]

    def to_partner(value):
        return lax.ppermute(value, "cuts", swap)

    def over_plane(value):
        return lax.all_to_all(value, ("dp", "cuts"), 0, 0, tiled=True, axis_index_groups=plane)

    def over_line(value):
        return lax.all_to_all(value, "cuts", 0, 0, tiled=True, axis_index_groups=line)

    in_own, out_own = w_in[0], w_out[0]
    hidden = in_own.shape[1]
    in_other, out_other = to_partner(in_own), to_partner(out_own)
    routes_t, gates_t = routes.T, gates.T

    sent, places = call(
        functools.partial(place_kernel, experts, cap),
        (struct(chunks, 2 * PAD, width), struct(chosen, tok_rows, dtype=jnp.int32)),
        4 * chunks * PAD * tok_rows * width,
        8 * chunks * PAD * width,
        routes_t,
        gates_t,
        tokens,
        cotangent,
    )
    recv = over_plane(sent)
    packed = call(
        functools.partial(pack_kernel, experts, used),
        struct(4 * rows, width),
        8 * rows * experts * PAD * width,
        8 * rows * 4 * width,
        recv,
    )
    lined = over_line(jnp.broadcast_to(packed[None], (peers, 4 * rows, width)))
    ret, held_x, held_g, active, dpre = call(
        expert_kernel,
        (
            struct(peers, 4 * rows, width),
            struct(rows, model),
            struct(rows, model),
            struct(2, rows, hidden),
            struct(2, rows, hidden),
        ),
        16 * rows * model * hidden,
        24 * rows * model,
        lined,
        in_own,
        in_other,
        out_own,
        out_other,
    )
    returned = over_line(ret)
    over_rows = ((0,), (0,))
    sent_in = to_partner(dot(held_x, dpre[1], over_rows).astype(BF16))
    sent_out = to_partner(dot(active[1], held_g, over_rows).astype(BF16))
    summed = call(
        functools.partial(sum_kernel, experts, used),
        struct(chunks, 2 * PAD, width),
        8 * rows * experts * PAD * width,
        8 * rows * peers * width,
        returned,
    )
    home = over_plane(summed)
    grad_in = (dot(held_x, dpre[0], over_rows) + sent_in.astype(F32)).astype(BF16)[None]
    grad_out = (dot(active[0], held_g, over_rows) + sent_out.astype(F32)).astype(BF16)[None]
    mixed, token_grad = call(
        combine_kernel,
        (struct(tok_rows, width), struct(tok_rows, width)),
        6 * chunks * PAD * tok_rows * width,
        8 * chunks * PAD * width,
        places,
        gates_t,
        home,
    )
    return (mixed, token_grad, grad_in, grad_out)


def solution(mesh):
    in_specs = (
        P("dp", "cuts"),
        P("dp", "cuts"),
        P("dp", None),
        P("dp", None),
        P("dp", None, "cuts"),
        P("dp", "cuts", None),
    )
    out_specs = (P("dp", "cuts"), P("dp", "cuts"), P("dp", None, "cuts"), P("dp", "cuts", None))
    return jax.shard_map(body, mesh=mesh, in_specs=in_specs, out_specs=out_specs, check_vma=False)
```

time: 377 us -> 168 us (0.45)
  waiting for transfers between devices: 144 us -> 83.7 us
  local copies, waits for them, and re-layouts: 66.4 us -> 12.2 us
  starting transfers between devices: 69.1 us -> 28.4 us
  blocking collectives: 59.2 us -> 28.6 us
  between operations: 14.2 us -> 0.74 us
  matrix products: 19.6 us -> 8.24 us
  Pallas kernels: 0 us -> 5.35 us
    unnamed x4 -> x0, waiting for transfers between devices: 80.6 us -> none
    all_gather x2 -> x0, blocking collectives: 59.2 us -> none  [the longest x1 30.6 us: body(): lax.all_gather(tokens, 'cuts', axis=1, tiled=True)]
    all_to_all x4 -> x3, starting transfers between devices: 68.8 us -> 17.9 us  [the longest x2 13.3 us: over_line(): lax.all_to_all(value, 'cuts', 0, 0, tiled=True, axis_index_groups=line)]
    ppermute x0 -> x4, waiting for transfers between devices: none -> 42.9 us  [to_partner(): return lax.ppermute(value, 'cuts', swap)]
    unnamed x18 -> x26, local copies, waits for them, and re-layouts: 44.7 us -> 10.9 us
    all_to_all x0 -> x1, blocking collectives: none -> 28.6 us  [over_plane(): lax.all_to_all(value, ('dp', 'cuts'), 0, 0, tiled=True, axis_index_groups...]
    all_to_all x4 -> x3, waiting for transfers between devices: 63.7 us -> 40.7 us  [the longest x2 32.3 us: over_line(): lax.all_to_all(value, 'cuts', 0, 0, tiled=True, axis_index_groups=line)]
    dot_general x8 -> x4, matrix products: 19.6 us -> 8.24 us  [dot(): lax.dot_general(left, right, (dims, ((), ())), preferred_element_type=F32)]
  transfers between devices with their start and end apart: 6 -> 7, of which waited for: 5 -> 5; matrix products, arithmetic and copies ran while one was open for 14% -> 5% of each run, Pallas kernels for 0% -> 1%
where the time goes in v1:
time: 168 us; the launch traced here: 167 us
  waiting for transfers between devices  83.7 us (50%)
  blocking collectives  28.6 us (17%)
  starting transfers between devices  28.4 us (17%)
  local copies, waits for them, and re-layouts  12.2 us (7%)
  matrix products  8.24 us (5%)
  Pallas kernels  5.35 us (3%)
    ppermute x4, waiting for transfers between devices, to_partner(): return lax.ppermute(value, 'cuts', swap)  42.9 us
    all_to_all x2, waiting for transfers between devices, over_line(): lax.all_to_all(value, 'cuts', 0, 0, tiled=True, axis_index_groups=line)  32.3 us
    all_to_all x1, blocking collectives, over_plane(): lax.all_to_all(value, ('dp', 'cuts'), 0, 0, tiled=True, axis_index_groups...  28.6 us
    all_to_all x2, starting transfers between devices, over_line(): lax.all_to_all(value, 'cuts', 0, 0, tiled=True, axis_index_groups=line)  13.3 us
    unnamed x26, local copies, waits for them, and re-layouts  10.9 us
    ppermute x4, starting transfers between devices, to_partner(): return lax.ppermute(value, 'cuts', swap)  10.5 us
    all_to_all x1, waiting for transfers between devices, over_plane(): lax.all_to_all(value, ('dp', 'cuts'), 0, 0, tiled=True, axis_index_groups...  8.42 us
    dot_general x4, matrix products, dot(): lax.dot_general(left, right, (dims, ((), ())), preferred_element_type=F32)  8.24 us
  transfers between devices with their start and end apart: 7, of which 5 were waited for; matrix products, arithmetic and copies ran while one was open for 5% of the time, Pallas kernels for 1%

profile of v1, /device:TPU:1, one launch (start us, length us, event | category | flops | bytes accessed | tf_op | source)
XLA Modules:
  0.0 167.2 jit_solution(17987340410138830934)
XLA Ops:
  0.6 0.7 copy-done.1
  1.3 0.8 copy-done.10
  2.1 0.8 copy-done.11
  2.8 0.7 copy-done.12
  3.5 0.4 shard_map.93
  3.9 28.6 %all_to_all.20.recv_ref = bf16[64,16,128]{2,1,0:T(8,128)(2,1)S(1)} all-to-all(bf16[64,16,128]{2,1,0:T(8,128)(2,1)S(1)} %get-tuple-element.14), channel_id=1, replica_groups={{0,8,16,24,32,40,48,56,64,72,80,88,96,104,112,120,128,136,144,152,160,1..., dimensions={0} | all-to-all | bytes 524288 | tf_op jit(solution)/shard_map/all_to_all | solution.py:206
  32.7 1.4 broadcast_in_dim.12
  34.1 6.9 %all-to-all-start.1 = ((bf16[8,768,128]{2,1,0:T(8,128)(2,1)}), bf16[8,768,128]{2,1,0:T(8,128)(2,1)S(1)}, u32[]{:S(2)}, u32[]{:S(2)}) async-start(bf16[8,768,128]{2,1,0:T(8,128)(2,1)} %broadcast_in_dim.12), calls=%async_computation.1 | async-start | bytes 3145728 | tf_op jit(solution)/shard_map/all_to_all | solution.py:209
  41.0 2.2 %collective-permute-start = (bf16[2048,256]{1,0:T(8,128)(2,1)S(1)}, bf16[2048,256]{1,0:T(8,128)(2,1)S(1)}, u32[]{:S(2)}, u32[]{:S(2)}) collective-permute-start(bf16[2048,256]{1,0:T(8,128)(2,1)S(1)} %bitcast.26), channel_id=1, source_target_pairs={{0,8},{1,9},{2,10},{3,11},{4,12},{5,13},{6,14},{7,15},{8,0},{9,1},... | collective-permute-start | bytes 3145736 | tf_op jit(solution)/shard_map/ppermute | solution.py:203
  43.3 3.1 %collective-permute-start.1 = (bf16[256,2048]{1,0:T(8,128)(2,1)}, bf16[256,2048]{1,0:T(8,128)(2,1)S(1)}, u32[]{:S(2)}, u32[]{:S(2)}) collective-permute-start(bf16[256,2048]{1,0:T(8,128)(2,1)} %bitcast.28), channel_id=1, source_target_pairs={{0,8},{1,9},{2,10},{3,11},{4,12},{5,13},{6,14},{7,15},{8,0},{9,1},... | collective-permute-start | bytes 3145736 | tf_op jit(solution)/shard_map/ppermute | solution.py:203
  46.3 21.2 %collective-permute-done.in1_ref = bf16[2048,256]{1,0:T(8,128)(2,1)S(1)} collective-permute-done((bf16[2048,256]{1,0:T(8,128)(2,1)S(1)}, bf16[2048,256]{1,0:T(8,128)(2,1)S(1)}, u32[]{:S(2)}, u32[]{:S(2)}) %collective-permute-start) | collective-permute-done | bytes 1048608 | tf_op jit(solution)/shard_map/ppermute | solution.py:203
  67.5 1.0 copy-done.6
  68.5 21.5 %collective-permute-done.1.out1_ref = bf16[256,2048]{1,0:T(8,128)(2,1)S(1)} collective-permute-done((bf16[256,2048]{1,0:T(8,128)(2,1)}, bf16[256,2048]{1,0:T(8,128)(2,1)S(1)}, u32[]{:S(2)}, u32[]{:S(2)}) %collective-permute-start.1) | collective-permute-done | bytes 1048608 | tf_op jit(solution)/shard_map/ppermute | solution.py:203
  90.0 1.0 copy-done.8
  91.0 1.2 copy-done.4
  92.2 1.2 copy-done.5
  93.4 1.2 copy-done.7
  94.6 1.2 copy-done.9
  95.9 2.6 %shard_map.95 = (bf16[8,768,128]{2,1,0:T(8,128)(2,1)S(1)}, bf16[192,2048]{1,0:T(8,128)(2,1)S(1)}, bf16[192,2048]{1,0:T(8,128)(2,1)S(1)}, bf16[2,192,256]{2,1,0:T(8,128)(2,1)S(1)}, bf16[2,192,256]{2,1,0:T(8,128)(2,1)S(1)}) custom-call(bf16[8,768,128]{2,1,0:T(8,128)(2,1)S(1)} %all-to-all-done.1.recv_ref, bf16[2048,256]{1,0:T(8,128)(2,1)S(1)} %bitcast.27, ...), custom_call_target="tpu_custom_call" | custom-call | flops 1610612736 | bytes 9437184 | tf_op jit(solution)/shard_map/pallas_call | solution.py:172
  98.5 1.2 copy-done
  99.6 6.3 %all-to-all-start.2 = ((bf16[8,768,128]{2,1,0:T(8,128)(2,1)}), bf16[8,768,128]{2,1,0:T(8,128)(2,1)S(1)}, u32[]{:S(2)}, u32[]{:S(2)}) async-start(bf16[8,768,128]{2,1,0:T(8,128)(2,1)} %copy-done), calls=%async_computation.2 | async-start | bytes 3145728 | tf_op jit(solution)/shard_map/all_to_all | solution.py:209
  105.9 1.4 convolution_convert_fusion
  107.4 2.2 %collective-permute-start.3 = (bf16[256,2048]{1,0:T(8,128)(2,1)}, bf16[256,2048]{1,0:T(8,128)(2,1)}, u32[]{:S(2)}, u32[]{:S(2)}) collective-permute-start(bf16[256,2048]{1,0:T(8,128)(2,1)} %convolution_convert_fusion), channel_id=1, source_target_pairs={{0,8},{1,9},{2,10},{3,11},{4,12},{5,13},{6,14},{7,15},{8,0},{9,1},... | collective-permute-start | bytes 3145736 | tf_op jit(solution)/shard_map/ppermute | solution.py:203
  109.5 1.5 convolution_convert_fusion.1
  111.0 3.1 %collective-permute-start.2 = (bf16[2048,256]{1,0:T(8,128)(2,1)}, bf16[2048,256]{1,0:T(8,128)(2,1)}, u32[]{:S(2)}, u32[]{:S(2)}) collective-permute-start(bf16[2048,256]{1,0:T(8,128)(2,1)} %convolution_convert_fusion.1), channel_id=1, source_target_pairs={{0,8},{1,9},{2,10},{3,11},{4,12},{5,13},{6,14},{7,15},{8,0},{9,1},... | collective-permute-start | bytes 3145736 | tf_op jit(solution)/shard_map/ppermute | solution.py:203
  114.1 32.3 %all-to-all-done.2.recv_ref = bf16[8,768,128]{2,1,0:T(8,128)(2,1)S(1)} async-done(((bf16[8,768,128]{2,1,0:T(8,128)(2,1)}), bf16[8,768,128]{2,1,0:T(8,128)(2,1)S(1)}, u32[]{:S(2)}, u32[]{:S(2)}) %all-to-all-start.2) | async-done | bytes 1572896 | tf_op jit(solution)/shard_map/all_to_all | solution.py:209
  146.4 1.1 shard_map.96
  147.6 4.6 %all-to-all-start.3 = ((bf16[64,16,128]{2,1,0:T(8,128)(2,1)}), bf16[64,16,128]{2,1,0:T(8,128)(2,1)S(1)}, u32[]{:S(2)}, u32[]{:S(2)}) async-start(bf16[64,16,128]{2,1,0:T(8,128)(2,1)} %shard_map.96), calls=%async_computation.3 | async-start | bytes 524288 | tf_op jit(solution)/shard_map/all_to_all | solution.py:206
  152.2 2.7 %fusion.2 = bf16[1,256,2048]{2,1,0:T(8,128)(2,1)} fusion(bf16[192,2048]{1,0:T(8,128)(2,1)S(1)} %get-tuple-element.21, bf16[256,2048]{1,0:T(8,128)(2,1)} %collective-permute-done.3, bf16[2,192,256]{2,1,0:T(8,128)(2,1)S(1)} %get-tuple-element.20), kind=kOutput, calls=%fused_computation.6 | convolution fusion | flops 202899456 | bytes 2981888 | tf_op jit(solution)/shard_map/dot_general | solution.py:29
  155.1 2.7 %fusion.3 = bf16[1,2048,256]{2,1,0:T(8,128)(2,1)} fusion(bf16[192,2048]{1,0:T(8,128)(2,1)S(1)} %get-tuple-element.18, bf16[2048,256]{1,0:T(8,128)(2,1)} %collective-permute-done.2, bf16[2,192,256]{2,1,0:T(8,128)(2,1)S(1)} %get-tuple-element.19), kind=kOutput, calls=%fused_computation.7 | convolution fusion | flops 202899456 | bytes 2981888 | tf_op jit(solution)/shard_map/dot_general | solution.py:29
  157.8 8.4 %all-to-all-done.3.home_ref = bf16[64,16,128]{2,1,0:T(8,128)(2,1)S(1)} async-done(((bf16[64,16,128]{2,1,0:T(8,128)(2,1)}), bf16[64,16,128]{2,1,0:T(8,128)(2,1)S(1)}, u32[]{:S(2)}, u32[]{:S(2)}) %all-to-all-start.3) | async-done | bytes 262176 | tf_op jit(solution)/shard_map/all_to_all | solution.py:206
  166.2 1.0 shard_map.97
  (19 shorter events, 0.5 us)
Async XLA Ops:
  0.6 0.7 copy-start.1
  1.3 0.8 copy-start.10
  2.1 0.8 copy-start.11
  2.8 0.7 copy-start.12
  34.1 7.0 %copy-start.3 = (bf16[1,2048,256]{2,1,0:T(8,128)(2,1)S(1)}, bf16[1,2048,256]{2,1,0:T(8,128)(2,1)}, u32[]{:S(2)}) copy-start(bf16[1,2048,256]{2,1,0:T(8,128)(2,1)} %param.10) | copy-start | bytes 3145732
  34.1 56.9 %all-to-all-start.1 = ((bf16[8,768,128]{2,1,0:T(8,128)(2,1)}), bf16[8,768,128]{2,1,0:T(8,128)(2,1)S(1)}, u32[]{:S(2)}, u32[]{:S(2)}) async-start(bf16[8,768,128]{2,1,0:T(8,128)(2,1)} %broadcast_in_dim.12), calls=%async_computation.1 | async-start | bytes 3145728 | tf_op jit(solution)/shard_map/all_to_all | solution.py:209
  41.0 26.5 %collective-permute-start = (bf16[2048,256]{1,0:T(8,128)(2,1)S(1)}, bf16[2048,256]{1,0:T(8,128)(2,1)S(1)}, u32[]{:S(2)}, u32[]{:S(2)}) collective-permute-start(bf16[2048,256]{1,0:T(8,128)(2,1)S(1)} %bitcast.26), channel_id=1, source_target_pairs={{0,8},{1,9},{2,10},{3,11},{4,12},{5,13},{6,14},{7,15},{8,0},{9,1},... | collective-permute-start | bytes 3145736 | tf_op jit(solution)/shard_map/ppermute | solution.py:203
  43.3 46.7 %collective-permute-start.1 = (bf16[256,2048]{1,0:T(8,128)(2,1)}, bf16[256,2048]{1,0:T(8,128)(2,1)S(1)}, u32[]{:S(2)}, u32[]{:S(2)}) collective-permute-start(bf16[256,2048]{1,0:T(8,128)(2,1)} %bitcast.28), channel_id=1, source_target_pairs={{0,8},{1,9},{2,10},{3,11},{4,12},{5,13},{6,14},{7,15},{8,0},{9,1},... | collective-permute-start | bytes 3145736 | tf_op jit(solution)/shard_map/ppermute | solution.py:203
  67.5 1.0 copy-start.6
  90.0 1.0 copy-start.8
  91.0 1.2 copy-start.4
  92.2 1.2 copy-start.5
  93.4 1.2 copy-start.7
  94.6 1.2 copy-start.9
  98.5 1.2 copy-start
  99.6 46.8 %all-to-all-start.2 = ((bf16[8,768,128]{2,1,0:T(8,128)(2,1)}), bf16[8,768,128]{2,1,0:T(8,128)(2,1)S(1)}, u32[]{:S(2)}, u32[]{:S(2)}) async-start(bf16[8,768,128]{2,1,0:T(8,128)(2,1)} %copy-done), calls=%async_computation.2 | async-start | bytes 3145728 | tf_op jit(solution)/shard_map/all_to_all | solution.py:209
  107.4 44.8 %collective-permute-start.3 = (bf16[256,2048]{1,0:T(8,128)(2,1)}, bf16[256,2048]{1,0:T(8,128)(2,1)}, u32[]{:S(2)}, u32[]{:S(2)}) collective-permute-start(bf16[256,2048]{1,0:T(8,128)(2,1)} %convolution_convert_fusion), channel_id=1, source_target_pairs={{0,8},{1,9},{2,10},{3,11},{4,12},{5,13},{6,14},{7,15},{8,0},{9,1},... | collective-permute-start | bytes 3145736 | tf_op jit(solution)/shard_map/ppermute | solution.py:203
  111.0 44.1 %collective-permute-start.2 = (bf16[2048,256]{1,0:T(8,128)(2,1)}, bf16[2048,256]{1,0:T(8,128)(2,1)}, u32[]{:S(2)}, u32[]{:S(2)}) collective-permute-start(bf16[2048,256]{1,0:T(8,128)(2,1)} %convolution_convert_fusion.1), channel_id=1, source_target_pairs={{0,8},{1,9},{2,10},{3,11},{4,12},{5,13},{6,14},{7,15},{8,0},{9,1},... | collective-permute-start | bytes 3145736 | tf_op jit(solution)/shard_map/ppermute | solution.py:203
  147.6 18.6 %all-to-all-start.3 = ((bf16[64,16,128]{2,1,0:T(8,128)(2,1)}), bf16[64,16,128]{2,1,0:T(8,128)(2,1)S(1)}, u32[]{:S(2)}, u32[]{:S(2)}) async-start(bf16[64,16,128]{2,1,0:T(8,128)(2,1)} %shard_map.96), calls=%async_computation.3 | async-start | bytes 524288 | tf_op jit(solution)/shard_map/all_to_all | solution.py:206
  154.8 11.4 %copy-start.2 = (f32[128,2]{0,1:T(2,128)S(1)}, f32[128,2]{0,1:T(2,128)}, u32[]{:S(2)}) copy-start(f32[128,2]{0,1:T(2,128)} %param.8) | copy-start | bytes 3076

commit v2 on v1

v2 whole, which is shorter than its diff:
```python
import functools
import math

import jax
import jax.numpy as jnp
from jax import lax
from jax.experimental import pallas as pl
from jax.experimental.pallas import tpu as pltpu
from jax.sharding import PartitionSpec as P

BF16 = jnp.bfloat16
F32 = jnp.float32
HALVES = 2
PAD = 8


def gelu_parts(pre):
    coef = math.sqrt(2.0 / math.pi)
    inner = coef * (pre + 0.044715 * pre * pre * pre)
    tangent = jnp.tanh(inner)
    value = 0.5 * pre * (1.0 + tangent)
    slope = 0.5 * (1.0 + tangent) + 0.5 * pre * (1.0 - tangent * tangent) * coef * (
        1.0 + 3.0 * 0.044715 * pre * pre
    )
    return (value, slope)


def dot(left, right, dims=((1,), (0,))):
    return lax.dot_general(left, right, (dims, ((), ())), preferred_element_type=F32)


def iota(shape, axis):
    return lax.broadcasted_iota(jnp.int32, shape, axis)


def place_kernel(experts, cap, routes_in, gates_in, tok_in, cot_in, sent_ref, rows_ref, *scratch):
    routes_ref, gates_ref, both_ref, sems = scratch
    tok_rows, width = tok_in.shape
    copies = [
        pltpu.make_async_copy(routes_in, routes_ref, sems.at[0]),
        pltpu.make_async_copy(gates_in, gates_ref, sems.at[1]),
        pltpu.make_async_copy(tok_in, both_ref.at[:, pl.ds(0, width)], sems.at[2]),
        pltpu.make_async_copy(cot_in, both_ref.at[:, pl.ds(width, width)], sems.at[3]),
    ]
    for copy in copies:
        copy.start()
    copies[0].wait()
    routes = routes_ref[...]
    first, second = routes[0:1, :], routes[1:2, :]
    names = iota((experts, tok_rows), 0)
    hit0, hit1 = names == first, names == second
    either = jnp.where(hit0 | hit1, 1.0, 0.0).astype(BF16)
    earlier = iota((tok_rows, tok_rows), 0) < iota((tok_rows, tok_rows), 1)
    count = dot(either, jnp.where(earlier, 1.0, 0.0).astype(BF16))
    half_cap = cap // HALVES

    def row_of(hit, expert):
        position = jnp.sum(jnp.where(hit, count, 0.0), axis=0, keepdims=True).astype(jnp.int32)
        upper = jnp.where(position >= half_cap, 1, 0)
        return (expert * HALVES + upper) * PAD + position - upper * half_cap

    row0, row1 = row_of(hit0, first), row_of(hit1, second)
    rows_ref[0:1, :] = row0
    rows_ref[1:2, :] = row1
    chunks = experts * HALVES
    slot = iota((chunks * PAD, tok_rows), 0)
    at0, at1 = slot == row0, slot == row1
    copies[1].wait()
    gates = gates_ref[...]
    gate = jnp.sum(
        jnp.where(at0, gates[0:1, :], 0.0) + jnp.where(at1, gates[1:2, :], 0.0),
        axis=1,
        keepdims=True,
    )
    select = jnp.where(at0 | at1, 1.0, 0.0).astype(BF16)
    copies[2].wait()
    copies[3].wait()
    both = dot(select, both_ref[...])
    held_x = both[:, :width].reshape(chunks, PAD, width)
    held_g = (both[:, width:] * gate).reshape(chunks, PAD, width)
    sent_ref[...] = jnp.concatenate([held_x, held_g], axis=1).astype(BF16)


def packing(sources, used):
    shape = (sources * used, sources * PAD)
    at = iota(shape, 1)
    inner = lax.bitwise_and(at, PAD - 1)
    outer = lax.shift_right_logical(at, 3)
    hit = (iota(shape, 0) == outer * used + inner) & (inner < used)
    return jnp.where(hit, 1.0, 0.0).astype(BF16)


def pack_kernel(sources, used, recv_ref, x_out, g_out, x_ref, g_ref, sems):
    width = recv_ref.shape[2]
    pick = packing(sources, used)
    held = recv_ref[...].astype(F32).reshape(sources, HALVES, 2, PAD, width)
    rows = sources * used
    copies = []
    for kind, ref, out in ((0, x_ref, x_out), (1, g_ref, g_out)):
        for part in range(HALVES):
            piece = held[:, part, kind].reshape(sources * PAD, width).astype(BF16)
            ref[part * rows : (part + 1) * rows, :] = dot(pick, piece).astype(BF16)
        for peer in range(out.shape[0]):
            copies.append(pltpu.make_async_copy(ref, out.at[peer], sems.at[kind, peer]))
            copies[-1].start()
    for copy in copies:
        copy.wait()


def sum_kernel(sources, used, given_ref, back_ref, out_ref):
    groups, _, width = given_ref.shape
    pick = packing(sources, used)
    rows = sources * used
    kinds = []
    for ref in (given_ref, back_ref):
        parts = []
        for part in range(HALVES):
            start = part * rows
            total = ref[0, start : start + rows, :].astype(F32)
            for group in range(1, groups):
                total = total + ref[group, start : start + rows, :].astype(F32)
            spread = dot(pick, total.astype(BF16), ((0,), (0,)))
            parts.append(spread.reshape(sources, 1, PAD, width))
        kinds.append(jnp.concatenate(parts, axis=1))
    whole = jnp.concatenate(kinds, axis=2)
    out_ref[...] = whole.reshape(sources * HALVES, 2 * PAD, width).astype(BF16)


def fetch_rows(recv, held_ref, sems):
    peers, both_rows, width = recv.shape
    rows = both_rows // HALVES
    copies = []
    for part in range(HALVES):
        for peer in range(peers):
            at = (part * peers + peer) * width
            copies.append(
                pltpu.make_async_copy(
                    recv.at[peer, pl.ds(part * rows, rows), :],
                    held_ref.at[:, pl.ds(at, width)],
                    sems.at[part * peers + peer],
                )
            )
            copies[-1].start()
    return copies


def fetch_weights(own, head, tail, other, refs, sems):
    in0_ref, in1_ref, out0_ref, out1_ref = refs
    cut = head.shape[0]
    return {
        "in0": [pltpu.make_async_copy(own[0], in0_ref, sems.at[0])],
        "in1": [
            pltpu.make_async_copy(head, in1_ref.at[pl.ds(0, cut), :], sems.at[1]),
            pltpu.make_async_copy(tail, in1_ref.at[pl.ds(cut, tail.shape[0]), :], sems.at[2]),
        ],
        "out0": [pltpu.make_async_copy(own[1], out0_ref, sems.at[3])],
        "out1": [pltpu.make_async_copy(other, out1_ref, sems.at[4])],
    }


def send_blocks(ret_ref, ret_out, sems, product):
    peers, both_rows, width = ret_ref.shape
    rows = both_rows // HALVES
    copies = []
    for part in range(HALVES):
        at_rows = pl.ds(part * rows, rows)
        for pair in range(peers // 2):
            at = (part * peers + 2 * pair) * width
            block = product(slice(at, at + 2 * width)).astype(BF16)
            for side in range(2):
                peer = 2 * pair + side
                ret_ref[peer, at_rows, :] = block[:, side * width : (side + 1) * width]
                copies.append(
                    pltpu.make_async_copy(
                        ret_ref.at[peer, at_rows, :],
                        ret_out.at[peer, at_rows, :],
                        sems.at[part * peers + peer],
                    )
                )
                copies[-1].start()
    return copies


def forward_kernel(
    recv, in_own, in_head, in_tail, out_own, out_other, ret_out, x_out, act_ref, slope_ref, *scratch
):
    x_ref, in0, in1, out0, out1, ret_ref, row_sems, weight_sems, ret_sems, x_sem = scratch
    rows = fetch_rows(recv, x_ref, row_sems)
    weights = fetch_weights(
        (in_own, out_own), in_head, in_tail, out_other, (in0, in1, out0, out1), weight_sems
    )
    for name in ("in0", "in1", "out0", "out1"):
        for copy in weights[name]:
            copy.start()
    for copy in rows:
        copy.wait()
    kept = pltpu.make_async_copy(x_ref, x_out, x_sem.at[0])
    kept.start()
    acts = []
    for group, (name, ref) in enumerate((("in0", in0), ("in1", in1))):
        for copy in weights[name]:
            copy.wait()
        value, slope = gelu_parts(dot(x_ref[...], ref[...]))
        acts.append(value.astype(BF16))
        act_ref[group] = acts[group]
        slope_ref[group] = slope
    for name in ("out0", "out1"):
        for copy in weights[name]:
            copy.wait()
    sent = send_blocks(
        ret_ref,
        ret_out,
        ret_sems,
        lambda cols: dot(acts[0], out0[:, cols]) + dot(acts[1], out1[:, cols]),
    )
    for copy in sent + [kept]:
        copy.wait()


def backward_kernel(
    recv, in_own, in_head, in_tail, out_own, out_other, slope_ref, ret_out, g_out, dpre_ref, *scratch
):
    g_ref, in0, in1, out0, out1, ret_ref, row_sems, weight_sems, ret_sems, g_sem = scratch
    rows = fetch_rows(recv, g_ref, row_sems)
    weights = fetch_weights(
        (in_own, out_own), in_head, in_tail, out_other, (in0, in1, out0, out1), weight_sems
    )
    for name in ("out0", "out1", "in0", "in1"):
        for copy in weights[name]:
            copy.start()
    for copy in rows:
        copy.wait()
    kept = pltpu.make_async_copy(g_ref, g_out, g_sem.at[0])
    kept.start()
    dpres = []
    by_last = ((1,), (1,))
    for group, (name, ref) in enumerate((("out0", out0), ("out1", out1))):
        for copy in weights[name]:
            copy.wait()
        backed = dot(g_ref[...], ref[...], by_last)
        dpres.append((backed * slope_ref[group]).astype(BF16))
        dpre_ref[group] = dpres[group]
    for name in ("in0", "in1"):
        for copy in weights[name]:
            copy.wait()
    sent = send_blocks(
        ret_ref,
        ret_out,
        ret_sems,
        lambda cols: dot(dpres[0], in0[cols, :], by_last) + dot(dpres[1], in1[cols, :], by_last),
    )
    for copy in sent + [kept]:
        copy.wait()


def combine_kernel(rows_ref, gates_ref, home_ref, mixed_ref, grad_ref):
    chunks, _, width = home_ref.shape
    tok_rows = mixed_ref.shape[0]
    held = home_ref[...].astype(F32)
    given = held[:, :PAD].reshape(chunks * PAD, width).astype(BF16)
    back = held[:, PAD:].reshape(chunks * PAD, width).astype(BF16)
    slot = iota((chunks * PAD, tok_rows), 0)
    at0, at1 = slot == rows_ref[0:1, :], slot == rows_ref[1:2, :]
    diagonal = iota((tok_rows, tok_rows), 0) == iota((tok_rows, tok_rows), 1)

    def mask(hit):
        return jnp.where(hit, 1.0, 0.0).astype(BF16)

    def column(row):
        return jnp.sum(jnp.where(diagonal, row, 0.0), axis=1, keepdims=True)

    over_rows = ((0,), (0,))
    mixed = column(gates_ref[0:1, :]) * dot(mask(at0), given, over_rows) + column(
        gates_ref[1:2, :]
    ) * dot(mask(at1), given, over_rows)
    mixed_ref[...] = mixed.astype(BF16)
    grad_ref[...] = dot(mask(at0 | at1), back, over_rows).astype(BF16)


def call(kernel, shapes, cost, places, limit, scratch, *args):
    ins, outs = places
    flops, moved = cost
    return pl.pallas_call(
        kernel,
        out_shape=shapes,
        in_specs=[pl.BlockSpec(memory_space=place) for place in ins],
        out_specs=tuple(pl.BlockSpec(memory_space=place) for place in outs),
        scratch_shapes=scratch,
        cost_estimate=pl.CostEstimate(flops=flops, bytes_accessed=moved, transcendentals=0),
        compiler_params=pltpu.CompilerParams(vmem_limit_bytes=limit * 1024 * 1024),
    )(*args)


def struct(*shape, dtype=BF16):
    return jax.ShapeDtypeStruct(shape, dtype)


def body(tokens, cotangent, gates, routes, w_in, w_out):
    experts = lax.axis_size("dp")
    cuts = lax.axis_size("cuts")
    peers = cuts // HALVES
    tok_rows, width = tokens.shape
    chosen = routes.shape[1]
    cap = 3 * chosen * tok_rows // (2 * experts)
    used = cap // HALVES
    chunks = experts * HALVES
    rows = experts * used
    both_rows = HALVES * rows
    model = width * cuts
    near, far = pltpu.VMEM, pltpu.HBM
    dma = pltpu.SemaphoreType.DMA
    swap = [(c, (c + peers) % cuts) for c in range(cuts)]
    line = [[h * peers + y for y in range(peers)] for h in range(HALVES)]
    plane = [
        [d * cuts + h * peers + y for d in range(experts) for h in range(HALVES)]
        for y in range(peers)
    ]

    def to_partner(value):
        return lax.ppermute(value, "cuts", swap)

    def over_plane(value):
        return lax.all_to_all(value, ("dp", "cuts"), 0, 0, tiled=True, axis_index_groups=plane)

    def over_line(value):
        return lax.all_to_all(value, "cuts", 0, 0, tiled=True, axis_index_groups=line)

    in_own, out_own = w_in[0], w_out[0]
    hidden = in_own.shape[1]
    cut = model * 3 // 4
    in_head = to_partner(in_own[:cut])
    in_tail, out_other = to_partner(in_own[cut:]), to_partner(out_own)
    routes_t, gates_t = routes.T, gates.T

    sent, places = call(
        functools.partial(place_kernel, experts, cap),
        (struct(chunks, 2 * PAD, width), struct(chosen, tok_rows, dtype=jnp.int32)),
        (4 * chunks * PAD * tok_rows * width, 8 * chunks * PAD * width),
        ([far] * 4, [near] * 2),
        16,
        [
            pltpu.VMEM((chosen, tok_rows), jnp.int32),
            pltpu.VMEM((chosen, tok_rows), F32),
            pltpu.VMEM((tok_rows, 2 * width), BF16),
            dma((4,)),
        ],
        routes_t,
        gates_t,
        tokens,
        cotangent,
    )
    recv = over_plane(sent)
    spread_x, spread_g = call(
        functools.partial(pack_kernel, experts, used),
        (struct(peers, both_rows, width), struct(peers, both_rows, width)),
        (8 * rows * experts * PAD * width, 8 * both_rows * peers * width),
        ([near], [far] * 2),
        16,
        [
            pltpu.VMEM((both_rows, width), BF16),
            pltpu.VMEM((both_rows, width), BF16),
            dma((2, peers)),
        ],
        recv,
    )
    spread_x, spread_g, in_head = lax.optimization_barrier((spread_x, spread_g, in_head))
    lined_x, lined_g = over_line(spread_x), over_line(spread_g)
    blocks = [
        pltpu.VMEM((rows, model), BF16),
        pltpu.VMEM((model, hidden), BF16),
        pltpu.VMEM((model, hidden), BF16),
        pltpu.VMEM((hidden, model), BF16),
        pltpu.VMEM((hidden, model), BF16),
        pltpu.VMEM((peers, both_rows, width), BF16),
        dma((cuts,)),
        dma((5,)),
        dma((cuts,)),
        dma((1,)),
    ]
    work = (8 * rows * model * hidden, 4 * rows * model + 8 * model * hidden)
    given, held_x, active, slope = call(
        forward_kernel,
        (
            struct(peers, both_rows, width),
            struct(rows, model),
            struct(2, rows, hidden),
            struct(2, rows, hidden, dtype=F32),
        ),
        work,
        ([far] * 6, [far, far, near, near]),
        32,
        blocks,
        lined_x,
        in_own,
        in_head,
        in_tail,
        out_own,
        out_other,
    )
    back_given = over_line(given)
    back, held_g, dpre = call(
        backward_kernel,
        (
            struct(peers, both_rows, width),
            struct(rows, model),
            struct(2, rows, hidden),
        ),
        work,
        ([far] * 6 + [near], [far, far, near]),
        32,
        blocks,
        lined_g,
        in_own,
        in_head,
        in_tail,
        out_own,
        out_other,
        slope,
    )
    back_back = over_line(back)
    over_rows = ((0,), (0,))
    sent_in = to_partner(dot(held_x, dpre[1], over_rows).astype(BF16))
    sent_out = to_partner(dot(active[1], held_g, over_rows).astype(BF16))
    summed = call(
        functools.partial(sum_kernel, experts, used),
        (struct(chunks, 2 * PAD, width),),
        (8 * rows * experts * PAD * width, 8 * rows * peers * width),
        ([near] * 2, [near]),
        16,
        [],
        back_given,
        back_back,
    )[0]
    home = over_plane(summed)
    grad_in = (dot(held_x, dpre[0], over_rows) + sent_in.astype(F32)).astype(BF16)[None]
    grad_out = (dot(active[0], held_g, over_rows) + sent_out.astype(F32)).astype(BF16)[None]
    mixed, token_grad = call(
        combine_kernel,
        (struct(tok_rows, width), struct(tok_rows, width)),
        (6 * chunks * PAD * tok_rows * width, 8 * chunks * PAD * width),
        ([near] * 3, [near] * 2),
        16,
        [],
        places,
        gates_t,
        home,
    )
    return (mixed, token_grad, grad_in, grad_out)


def solution(mesh):
    in_specs = (
        P("dp", "cuts"),
        P("dp", "cuts"),
        P("dp", None),
        P("dp", None),
        P("dp", None, "cuts"),
        P("dp", "cuts", None),
    )
    out_specs = (P("dp", "cuts"), P("dp", "cuts"), P("dp", None, "cuts"), P("dp", "cuts", None))
    return jax.shard_map(body, mesh=mesh, in_specs=in_specs, out_specs=out_specs, check_vma=False)
```

time: 168 us -> 209 us (1.24)
  blocking collectives: 28.6 us -> 84.5 us
  waiting for transfers between devices: 83.7 us -> 57.6 us
  Pallas kernels: 5.35 us -> 15 us
  local copies, waits for them, and re-layouts: 12.2 us -> 9.78 us
  starting transfers between devices: 28.4 us -> 30.6 us
    all_to_all x0 -> x2, blocking collectives: none -> 56.8 us  [over_line(): lax.all_to_all(value, 'cuts', 0, 0, tiled=True, axis_index_groups=line)]
    all_to_all x2, waiting for transfers between devices: 32.3 us -> 11.8 us  [over_line(): lax.all_to_all(value, 'cuts', 0, 0, tiled=True, axis_index_groups=line)]
    pallas_call x5 -> x6, Pallas kernels: 5.35 us -> 15 us  [call(): pl.pallas_call(kernel, out_shape=shapes, in_specs=[pl.BlockSpec(memory_sp...]
    all_to_all x1, waiting for transfers between devices: 8.42 us -> 1.77 us  [over_plane(): lax.all_to_all(value, ('dp', 'cuts'), 0, 0, tiled=True, axis_index_groups...]
    all_to_all x2, starting transfers between devices: 13.3 us -> 8.03 us  [over_line(): lax.all_to_all(value, 'cuts', 0, 0, tiled=True, axis_index_groups=line)]
    ppermute x4 -> x5, starting transfers between devices: 10.5 us -> 14.5 us  [to_partner(): return lax.ppermute(value, 'cuts', swap)]
    all_to_all x1, starting transfers between devices: 4.6 us -> 8.06 us  [over_plane(): lax.all_to_all(value, ('dp', 'cuts'), 0, 0, tiled=True, axis_index_groups...]
    unnamed x26 -> x40, local copies, waits for them, and re-layouts: 10.9 us -> 8.55 us
  transfers between devices with their start and end apart: 7 -> 8, of which waited for: 5 -> 4; matrix products, arithmetic and copies ran while one was open for 5% -> 4% of each run, Pallas kernels for 1% -> 4%
where the time goes in v2:
time: 209 us; the launch traced here: 207 us
  blocking collectives  84.5 us (40%)
  waiting for transfers between devices  57.6 us (28%)
  starting transfers between devices  30.6 us (15%)
  Pallas kernels  15 us (7%)
  local copies, waits for them, and re-layouts  9.78 us (5%)
  matrix products  8.24 us (4%)
    all_to_all x2, blocking collectives, over_line(): lax.all_to_all(value, 'cuts', 0, 0, tiled=True, axis_index_groups=line)  56.8 us
    ppermute x5, waiting for transfers between devices, to_partner(): return lax.ppermute(value, 'cuts', swap)  44.1 us
    all_to_all x1, blocking collectives, over_plane(): lax.all_to_all(value, ('dp', 'cuts'), 0, 0, tiled=True, axis_index_groups...  27.7 us
    pallas_call x6, Pallas kernels, call(): pl.pallas_call(kernel, out_shape=shapes, in_specs=[pl.BlockSpec(memory_sp...  15 us
    ppermute x5, starting transfers between devices, to_partner(): return lax.ppermute(value, 'cuts', swap)  14.5 us
    all_to_all x2, waiting for transfers between devices, over_line(): lax.all_to_all(value, 'cuts', 0, 0, tiled=True, axis_index_groups=line)  11.8 us
    unnamed x40, local copies, waits for them, and re-layouts  8.55 us
    dot_general x4, matrix products, dot(): lax.dot_general(left, right, (dims, ((), ())), preferred_element_type=F32)  8.24 us
  transfers between devices with their start and end apart: 8, of which 4 were waited for; matrix products, arithmetic and copies ran while one was open for 4% of the time, Pallas kernels for 4%

profile of v2, /device:TPU:1, one launch (start us, length us, event | category | flops | bytes accessed | tf_op | source)
XLA Modules:
  0.0 206.7 jit_solution(4444368123902480956)
XLA Ops:
  0.7 1.2 slice_bitcast_fusion
  1.9 3.9 %collective-permute-start = (bf16[1536,256]{1,0:T(8,128)(2,1)S(1)}, bf16[1536,256]{1,0:T(8,128)(2,1)S(1)}, u32[]{:S(2)}, u32[]{:S(2)}) collective-permute-start(bf16[1536,256]{1,0:T(8,128)(2,1)S(1)} %slice_bitcast_fusion), channel_id=1, source_target_pairs={{0,8},{1,9},{2,10},{3,11},{4,12},{5,13},{6,14},{7,15},{8,0},{9,1},... | collective-permute-start | bytes 2359304 | tf_op jit(solution)/shard_map/ppermute | solution.py:320
  6.5 27.7 %all_to_all.30.recv_ref = bf16[64,16,128]{2,1,0:T(8,128)(2,1)S(1)} all-to-all(bf16[64,16,128]{2,1,0:T(8,128)(2,1)S(1)} %get-tuple-element.21), channel_id=1, replica_groups={{0,8,16,24,32,40,48,56,64,72,80,88,96,104,112,120,128,136,144,152,160,1..., dimensions={0} | all-to-all | bytes 524288 | tf_op jit(solution)/shard_map/all_to_all | solution.py:323
  34.3 2.4 %shard_map.94 = (bf16[8,384,128]{2,1,0:T(8,128)(2,1)S(1)}, bf16[8,384,128]{2,1,0:T(8,128)(2,1)}) custom-call(bf16[64,16,128]{2,1,0:T(8,128)(2,1)S(1)} %all_to_all.30.recv_ref), custom_call_target="tpu_custom_call" | custom-call | flops 50331648 | bytes 3145728 | tf_op jit(solution)/shard_map/pallas_call | solution.py:283
  36.7 0.9 copy-done.5
  37.6 30.5 %all_to_all.31.recv = bf16[8,384,128]{2,1,0:T(8,128)(2,1)} all-to-all(bf16[8,384,128]{2,1,0:T(8,128)(2,1)S(1)} %get-tuple-element.24), channel_id=1, replica_groups={{0,1,2,3,4,5,6,7},{8,9,10,11,12,13,14,15},{16,17,18,19,20,21,22,23},{24..., dimensions={0} | all-to-all | bytes 1572864 | tf_op jit(solution)/shard_map/all_to_all | solution.py:326
  68.1 4.3 %all-to-all-start.3 = ((bf16[8,384,128]{2,1,0:T(8,128)(2,1)}), bf16[8,384,128]{2,1,0:T(8,128)(2,1)}, u32[]{:S(2)}, u32[]{:S(2)}) async-start(bf16[8,384,128]{2,1,0:T(8,128)(2,1)} %get-tuple-element.27), calls=%async_computation.3 | async-start | bytes 1572864 | tf_op jit(solution)/shard_map/all_to_all | solution.py:326
  72.4 2.2 %collective-permute-start.2 = (bf16[256,2048]{1,0:T(8,128)(2,1)S(1)}, bf16[256,2048]{1,0:T(8,128)(2,1)S(1)}, u32[]{:S(2)}, u32[]{:S(2)}) collective-permute-start(bf16[256,2048]{1,0:T(8,128)(2,1)S(1)} %bitcast.30), channel_id=1, source_target_pairs={{0,8},{1,9},{2,10},{3,11},{4,12},{5,13},{6,14},{7,15},{8,0},{9,1},... | collective-permute-start | bytes 3145736 | tf_op jit(solution)/shard_map/ppermute | solution.py:320
  74.7 3.1 %collective-permute-start.1 = (bf16[512,256]{1,0:T(8,128)(2,1)S(1)}, bf16[512,256]{1,0:T(8,128)(2,1)S(1)}, u32[]{:S(2)}, u32[]{:S(2)}) collective-permute-start(bf16[512,256]{1,0:T(8,128)(2,1)S(1)} %slice_bitcast_fusion.1), channel_id=1, source_target_pairs={{0,8},{1,9},{2,10},{3,11},{4,12},{5,13},{6,14},{7,15},{8,0},{9,1},... | collective-permute-start | bytes 786440 | tf_op jit(solution)/shard_map/ppermute | solution.py:320
  77.8 26.5 %collective-permute-done.1.in_tail = bf16[512,256]{1,0:T(8,128)(2,1)S(1)} collective-permute-done((bf16[512,256]{1,0:T(8,128)(2,1)S(1)}, bf16[512,256]{1,0:T(8,128)(2,1)S(1)}, u32[]{:S(2)}, u32[]{:S(2)}) %collective-permute-start.1) | collective-permute-done | bytes 262176 | tf_op jit(solution)/shard_map/ppermute | solution.py:320
  104.2 1.1 copy-done.2
  105.4 1.1 copy-done.6
  106.5 3.5 %shard_map.95 = (bf16[8,384,128]{2,1,0:T(8,128)(2,1)}, bf16[192,2048]{1,0:T(8,128)(2,1)S(1)}, bf16[2,192,256]{2,1,0:T(8,128)(2,1)S(1)}, f32[2,192,256]{2,1,0:T(8,128)S(1)}) custom-call(bf16[8,384,128]{2,1,0:T(8,128)(2,1)S(1)} %copy-done.2, bf16[2048,256]{1,0:T(8,128)(2,1)S(1)} %bitcast.28, bf16[1536,256]{1,0:T(8,128)(2,1)S(1)} %copy-done.6, ...), custom_call_target="tpu_custom_call" | custom-call | flops 805306368 | bytes 5767168 | tf_op jit(solution)/shard_map/pallas_call | solution.py:283
  110.0 0.9 copy-done.3
  112.4 1.1 copy-done.7
  113.5 1.0 copy-done.11
  114.5 6.4 %shard_map.96 = (bf16[8,384,128]{2,1,0:T(8,128)(2,1)S(1)}, bf16[192,2048]{1,0:T(8,128)(2,1)S(1)}, bf16[2,192,256]{2,1,0:T(8,128)(2,1)S(1)}) custom-call(bf16[8,384,128]{2,1,0:T(8,128)(2,1)} %all-to-all-done.3.recv, bf16[2048,256]{1,0:T(8,128)(2,1)S(1)} %bitcast.29, bf16[1536,256]{1,0:T(8,128)(2,1)S(1)} %copy-done.7, ...), custom_call_target="tpu_custom_call" | custom-call | flops 805306368 | bytes 5767168 | tf_op jit(solution)/shard_map/pallas_call | solution.py:283
  120.9 0.9 copy-done.8
  121.7 26.3 %all_to_all.32.back_ref = bf16[8,384,128]{2,1,0:T(8,128)(2,1)S(1)} all-to-all(bf16[8,384,128]{2,1,0:T(8,128)(2,1)S(1)} %get-tuple-element.29), channel_id=1, replica_groups={{0,1,2,3,4,5,6,7},{8,9,10,11,12,13,14,15},{16,17,18,19,20,21,22,23},{24..., dimensions={0} | all-to-all | bytes 1572864 | tf_op jit(solution)/shard_map/all_to_all | solution.py:326
  148.1 3.7 %all-to-all-start.2 = ((bf16[8,384,128]{2,1,0:T(8,128)(2,1)}), bf16[8,384,128]{2,1,0:T(8,128)(2,1)S(1)}, u32[]{:S(2)}, u32[]{:S(2)}) async-start(bf16[8,384,128]{2,1,0:T(8,128)(2,1)} %get-tuple-element.26), calls=%async_computation.2 | async-start | bytes 1572864 | tf_op jit(solution)/shard_map/all_to_all | solution.py:326
  151.8 1.4 convolution_convert_fusion
  153.2 2.2 %collective-permute-start.4 = (bf16[256,2048]{1,0:T(8,128)(2,1)}, bf16[256,2048]{1,0:T(8,128)(2,1)}, u32[]{:S(2)}, u32[]{:S(2)}) collective-permute-start(bf16[256,2048]{1,0:T(8,128)(2,1)} %convolution_convert_fusion), channel_id=1, source_target_pairs={{0,8},{1,9},{2,10},{3,11},{4,12},{5,13},{6,14},{7,15},{8,0},{9,1},... | collective-permute-start | bytes 3145736 | tf_op jit(solution)/shard_map/ppermute | solution.py:320
  155.5 1.5 convolution_convert_fusion.1
  156.9 3.0 %collective-permute-start.3 = (bf16[2048,256]{1,0:T(8,128)(2,1)}, bf16[2048,256]{1,0:T(8,128)(2,1)}, u32[]{:S(2)}, u32[]{:S(2)}) collective-permute-start(bf16[2048,256]{1,0:T(8,128)(2,1)} %convolution_convert_fusion.1), channel_id=1, source_target_pairs={{0,8},{1,9},{2,10},{3,11},{4,12},{5,13},{6,14},{7,15},{8,0},{9,1},... | collective-permute-start | bytes 3145736 | tf_op jit(solution)/shard_map/ppermute | solution.py:320
  160.0 11.8 %all-to-all-done.2.given_ref = bf16[8,384,128]{2,1,0:T(8,128)(2,1)S(1)} async-done(((bf16[8,384,128]{2,1,0:T(8,128)(2,1)}), bf16[8,384,128]{2,1,0:T(8,128)(2,1)S(1)}, u32[]{:S(2)}, u32[]{:S(2)}) %all-to-all-start.2) | async-done | bytes 786464 | tf_op jit(solution)/shard_map/all_to_all | solution.py:326
  171.8 1.1 shard_map.97
  172.9 8.1 %all-to-all-start.5 = ((bf16[64,16,128]{2,1,0:T(8,128)(2,1)}), bf16[64,16,128]{2,1,0:T(8,128)(2,1)S(1)}, u32[]{:S(2)}, u32[]{:S(2)}) async-start(bf16[64,16,128]{2,1,0:T(8,128)(2,1)} %shard_map.97), calls=%async_computation.5 | async-start | bytes 524288 | tf_op jit(solution)/shard_map/all_to_all | solution.py:323
  181.0 2.7 %fusion.2 = bf16[1,256,2048]{2,1,0:T(8,128)(2,1)} fusion(bf16[192,2048]{1,0:T(8,128)(2,1)S(1)} %copy-done.9, bf16[256,2048]{1,0:T(8,128)(2,1)} %collective-permute-done.4, bf16[2,192,256]{2,1,0:T(8,128)(2,1)S(1)} %copy-done.13), kind=kOutput, calls=%fused_computation.6 | convolution fusion | flops 202899456 | bytes 2981888 | tf_op jit(solution)/shard_map/dot_general | solution.py:29
  183.6 17.6 %collective-permute-done.3 = bf16[2048,256]{1,0:T(8,128)(2,1)} collective-permute-done((bf16[2048,256]{1,0:T(8,128)(2,1)}, bf16[2048,256]{1,0:T(8,128)(2,1)}, u32[]{:S(2)}, u32[]{:S(2)}) %collective-permute-start.3) | collective-permute-done | bytes 1048608 | tf_op jit(solution)/shard_map/ppermute | solution.py:320
  201.3 2.7 %fusion.3 = bf16[1,2048,256]{2,1,0:T(8,128)(2,1)} fusion(bf16[192,2048]{1,0:T(8,128)(2,1)S(1)} %copy-done.4, bf16[2048,256]{1,0:T(8,128)(2,1)} %collective-permute-done.3, bf16[2,192,256]{2,1,0:T(8,128)(2,1)S(1)} %copy-done.15), kind=kOutput, calls=%fused_computation.7 | convolution fusion | flops 202899456 | bytes 2981888 | tf_op jit(solution)/shard_map/dot_general | solution.py:29
  203.9 1.8 all-to-all-done.5.home_ref
  205.7 1.0 shard_map.98
  (39 shorter events, 2.2 us)
Async XLA Ops:
  0.6 5.2 %copy-start.19 = (s32[128,2]{0,1:T(2,128)S(1)}, s32[128,2]{0,1:T(2,128)}, u32[]{:S(2)}) copy-start(s32[128,2]{0,1:T(2,128)} %param.9) | copy-start | bytes 3076
  0.6 5.2 %copy-start.16 = (f32[128,2]{0,1:T(2,128)S(1)}, f32[128,2]{0,1:T(2,128)}, u32[]{:S(2)}) copy-start(f32[128,2]{0,1:T(2,128)} %param.8) | copy-start | bytes 3076
  0.7 5.2 %copy-start.18 = (bf16[128,128]{1,0:T(8,128)(2,1)S(1)}, bf16[128,128]{1,0:T(8,128)(2,1)}, u32[]{:S(2)}) copy-start(bf16[128,128]{1,0:T(8,128)(2,1)} %cot_in.1) | copy-start | bytes 98308
  0.7 5.2 %copy-start.17 = (bf16[128,128]{1,0:T(8,128)(2,1)S(1)}, bf16[128,128]{1,0:T(8,128)(2,1)}, u32[]{:S(2)}) copy-start(bf16[128,128]{1,0:T(8,128)(2,1)} %tok_in.1) | copy-start | bytes 98308
  1.9 34.8 %collective-permute-start = (bf16[1536,256]{1,0:T(8,128)(2,1)S(1)}, bf16[1536,256]{1,0:T(8,128)(2,1)S(1)}, u32[]{:S(2)}, u32[]{:S(2)}) collective-permute-start(bf16[1536,256]{1,0:T(8,128)(2,1)S(1)} %slice_bitcast_fusion), channel_id=1, source_target_pairs={{0,8},{1,9},{2,10},{3,11},{4,12},{5,13},{6,14},{7,15},{8,0},{9,1},... | collective-permute-start | bytes 2359304 | tf_op jit(solution)/shard_map/ppermute | solution.py:320
  36.7 0.9 copy-start.5
  37.6 34.8 %copy-start.1 = (bf16[1,256,2048]{2,1,0:T(8,128)(2,1)S(1)}, bf16[1,256,2048]{2,1,0:T(8,128)(2,1)}, u32[]{:S(2)}) copy-start(bf16[1,256,2048]{2,1,0:T(8,128)(2,1)} %param.11) | copy-start | bytes 3145732
  68.1 6.6 %copy-start = (bf16[1,2048,256]{2,1,0:T(8,128)(2,1)S(1)}, bf16[1,2048,256]{2,1,0:T(8,128)(2,1)}, u32[]{:S(2)}) copy-start(bf16[1,2048,256]{2,1,0:T(8,128)(2,1)} %param.10) | copy-start | bytes 3145732
  68.1 44.3 %all-to-all-start.3 = ((bf16[8,384,128]{2,1,0:T(8,128)(2,1)}), bf16[8,384,128]{2,1,0:T(8,128)(2,1)}, u32[]{:S(2)}, u32[]{:S(2)}) async-start(bf16[8,384,128]{2,1,0:T(8,128)(2,1)} %get-tuple-element.27), calls=%async_computation.3 | async-start | bytes 1572864 | tf_op jit(solution)/shard_map/all_to_all | solution.py:326
  72.4 31.8 %collective-permute-start.2 = (bf16[256,2048]{1,0:T(8,128)(2,1)S(1)}, bf16[256,2048]{1,0:T(8,128)(2,1)S(1)}, u32[]{:S(2)}, u32[]{:S(2)}) collective-permute-start(bf16[256,2048]{1,0:T(8,128)(2,1)S(1)} %bitcast.30), channel_id=1, source_target_pairs={{0,8},{1,9},{2,10},{3,11},{4,12},{5,13},{6,14},{7,15},{8,0},{9,1},... | collective-permute-start | bytes 3145736 | tf_op jit(solution)/shard_map/ppermute | solution.py:320
  74.7 29.5 %collective-permute-start.1 = (bf16[512,256]{1,0:T(8,128)(2,1)S(1)}, bf16[512,256]{1,0:T(8,128)(2,1)S(1)}, u32[]{:S(2)}, u32[]{:S(2)}) collective-permute-start(bf16[512,256]{1,0:T(8,128)(2,1)S(1)} %slice_bitcast_fusion.1), channel_id=1, source_target_pairs={{0,8},{1,9},{2,10},{3,11},{4,12},{5,13},{6,14},{7,15},{8,0},{9,1},... | collective-permute-start | bytes 786440 | tf_op jit(solution)/shard_map/ppermute | solution.py:320
  104.2 1.1 copy-start.2
  105.3 1.1 copy-start.6
  110.0 0.9 copy-start.3
  110.9 0.8 copy-start.10
  111.7 0.7 copy-start.12
  112.4 1.1 copy-start.7
  113.5 1.0 copy-start.11
  120.9 0.9 copy-start.8
  121.7 26.3 %copy-start.14 = (bf16[2,192,256]{2,1,0:T(8,128)(2,1)}, bf16[2,192,256]{2,1,0:T(8,128)(2,1)S(1)}, u32[]{:S(2)}) copy-start(bf16[2,192,256]{2,1,0:T(8,128)(2,1)S(1)} %get-tuple-element.33) | copy-start | bytes 589828
  148.0 3.7 %copy-start.9 = (bf16[192,2048]{1,0:T(8,128)(2,1)S(1)}, bf16[192,2048]{1,0:T(8,128)(2,1)}, u32[]{:S(2)}) copy-start(bf16[192,2048]{1,0:T(8,128)(2,1)} %copy-done.8) | copy-start | bytes 2359300
  148.0 3.7 %copy-start.13 = (bf16[2,192,256]{2,1,0:T(8,128)(2,1)S(1)}, bf16[2,192,256]{2,1,0:T(8,128)(2,1)}, u32[]{:S(2)}) copy-start(bf16[2,192,256]{2,1,0:T(8,128)(2,1)} %copy-done.12) | copy-start | bytes 589828
  148.1 23.7 %all-to-all-start.2 = ((bf16[8,384,128]{2,1,0:T(8,128)(2,1)}), bf16[8,384,128]{2,1,0:T(8,128)(2,1)S(1)}, u32[]{:S(2)}, u32[]{:S(2)}) async-start(bf16[8,384,128]{2,1,0:T(8,128)(2,1)} %get-tuple-element.26), calls=%async_computation.2 | async-start | bytes 1572864 | tf_op jit(solution)/shard_map/all_to_all | solution.py:326
  151.7 3.7 %copy-start.4 = (bf16[192,2048]{1,0:T(8,128)(2,1)S(1)}, bf16[192,2048]{1,0:T(8,128)(2,1)}, u32[]{:S(2)}) copy-start(bf16[192,2048]{1,0:T(8,128)(2,1)} %copy-done.3) | copy-start | bytes 2359300
  151.7 3.7 %copy-start.15 = (bf16[2,192,256]{2,1,0:T(8,128)(2,1)S(1)}, bf16[2,192,256]{2,1,0:T(8,128)(2,1)}, u32[]{:S(2)}) copy-start(bf16[2,192,256]{2,1,0:T(8,128)(2,1)} %copy-done.14) | copy-start | bytes 589828
  153.2 27.8 %collective-permute-start.4 = (bf16[256,2048]{1,0:T(8,128)(2,1)}, bf16[256,2048]{1,0:T(8,128)(2,1)}, u32[]{:S(2)}, u32[]{:S(2)}) collective-permute-start(bf16[256,2048]{1,0:T(8,128)(2,1)} %convolution_convert_fusion), channel_id=1, source_target_pairs={{0,8},{1,9},{2,10},{3,11},{4,12},{5,13},{6,14},{7,15},{8,0},{9,1},... | collective-permute-start | bytes 3145736 | tf_op jit(solution)/shard_map/ppermute | solution.py:320
  156.9 44.3 %collective-permute-start.3 = (bf16[2048,256]{1,0:T(8,128)(2,1)}, bf16[2048,256]{1,0:T(8,128)(2,1)}, u32[]{:S(2)}, u32[]{:S(2)}) collective-permute-start(bf16[2048,256]{1,0:T(8,128)(2,1)} %convolution_convert_fusion.1), channel_id=1, source_target_pairs={{0,8},{1,9},{2,10},{3,11},{4,12},{5,13},{6,14},{7,15},{8,0},{9,1},... | collective-permute-start | bytes 3145736 | tf_op jit(solution)/shard_map/ppermute | solution.py:320
  172.9 32.8 %all-to-all-start.5 = ((bf16[64,16,128]{2,1,0:T(8,128)(2,1)}), bf16[64,16,128]{2,1,0:T(8,128)(2,1)S(1)}, u32[]{:S(2)}, u32[]{:S(2)}) async-start(bf16[64,16,128]{2,1,0:T(8,128)(2,1)} %shard_map.97), calls=%async_computation.5 | async-start | bytes 524288 | tf_op jit(solution)/shard_map/all_to_all | solution.py:323

commit v3 on v1

--- a/solution.py
+++ b/solution.py
@@ -33,8 +33,18 @@
     return lax.broadcasted_iota(jnp.int32, shape, axis)
 
 
-def place_kernel(experts, cap, routes_ref, gates_ref, tok_ref, cot_ref, sent_ref, rows_ref):
-    tok_rows, width = tok_ref.shape
+def place_kernel(experts, cap, routes_in, gates_in, tok_in, cot_in, sent_ref, rows_ref, *scratch):
+    routes_ref, gates_ref, both_ref, sems = scratch
+    tok_rows, width = tok_in.shape
+    copies = [
+        pltpu.make_async_copy(routes_in, routes_ref, sems.at[0]),
+        pltpu.make_async_copy(gates_in, gates_ref, sems.at[1]),
+        pltpu.make_async_copy(tok_in, both_ref.at[:, pl.ds(0, width)], sems.at[2]),
+        pltpu.make_async_copy(cot_in, both_ref.at[:, pl.ds(width, width)], sems.at[3]),
+    ]
+    for copy in copies:
+        copy.start()
+    copies[0].wait()
     routes = routes_ref[...]
     first, second = routes[0:1, :], routes[1:2, :]
     names = iota((experts, tok_rows), 0)
@@ -55,6 +65,7 @@
     chunks = experts * HALVES
     slot = iota((chunks * PAD, tok_rows), 0)
     at0, at1 = slot == row0, slot == row1
+    copies[1].wait()
     gates = gates_ref[...]
     gate = jnp.sum(
         jnp.where(at0, gates[0:1, :], 0.0) + jnp.where(at1, gates[1:2, :], 0.0),
@@ -62,7 +73,9 @@
         keepdims=True,
     )
     select = jnp.where(at0 | at1, 1.0, 0.0).astype(BF16)
-    both = dot(select, jnp.concatenate([tok_ref[...], cot_ref[...]], axis=1))
+    copies[2].wait()
+    copies[3].wait()
+    both = dot(select, both_ref[...])
     held_x = both[:, :width].reshape(chunks, PAD, width)
     held_g = (both[:, width:] * gate).reshape(chunks, PAD, width)
     sent_ref[...] = jnp.concatenate([held_x, held_g], axis=1).astype(BF16)
@@ -77,16 +90,25 @@
     return jnp.where(hit, 1.0, 0.0).astype(BF16)
 
 
-def pack_kernel(sources, used, recv_ref, out_ref):
+def pack_kernel(sources, used, recv_ref, out, held_ref, sems):
     width = recv_ref.shape[2]
     pick = packing(sources, used)
     held = recv_ref[...].astype(F32).reshape(sources, HALVES, 2, PAD, width)
     rows = sources * used
+    copies = []
     for kind in range(2):
         for part in range(HALVES):
             piece = held[:, part, kind].reshape(sources * PAD, width).astype(BF16)
             start = (kind * HALVES + part) * rows
-            out_ref[start : start + rows, :] = dot(pick, piece).astype(BF16)
+            held_ref[start : start + rows, :] = dot(pick, piece).astype(BF16)
+        at = pl.ds(kind * HALVES * rows, HALVES * rows)
+        for peer in range(out.shape[0]):
+            copies.append(
+                pltpu.make_async_copy(held_ref.at[at, :], out.at[peer, at, :], sems.at[kind, peer])
+            )
+            copies[-1].start()
+    for copy in copies:
+        copy.wait()
 
 
 def sum_kernel(sources, used, recv_ref, out_ref):
@@ -109,39 +131,101 @@
 
 
 def expert_kernel(
-    recv_ref, in0_ref, in1_ref, out0_ref, out1_ref, ret_ref, x_ref, g_ref, act_ref, dpre_ref
+    recv, in_own, in_head, in_tail, out_own, out_other, ret_out, x_out, g_out, act_ref, dpre_ref, *scratch
 ):
-    peers, all_rows, width = recv_ref.shape
+    x_ref, g_ref, in0, in1, out0, out1, ret_ref, row_sems, weight_sems, ret_sems, kept_sems = scratch
+    peers, all_rows, width = recv.shape
     rows = all_rows // (2 * HALVES)
-    for kind, ref in ((0, x_ref), (1, g_ref)):
+    cut = in_head.shape[0]
+
+    def fetch_rows(kind, ref):
+        copies = []
         for part in range(HALVES):
             start = (kind * HALVES + part) * rows
             for peer in range(peers):
-                at = (part * peers + peer) * width
-                ref[:, at : at + width] = recv_ref[peer, start : start + rows, :]
-    ins, outs = (in0_ref, in1_ref), (out0_ref, out1_ref)
-    acts, dpres = [], []
-    for group in range(2):
-        pre = dot(x_ref[...], ins[group][...])
-        value, slope = gelu_parts(pre)
-        backed = dot(g_ref[...], outs[group][...], ((1,), (1,)))
+                index = part * peers + peer
+                copies.append(
+                    pltpu.make_async_copy(
+                        recv.at[peer, pl.ds(start, rows), :],
+                        ref.at[:, pl.ds(index * width, width)],
+                        row_sems.at[kind, index],
+                    )
+                )
+                copies[-1].start()
+        return copies
+
+    rows_x = fetch_rows(0, x_ref)
+    load_in = [
+        [pltpu.make_async_copy(in_own, in0, weight_sems.at[0])],
+        [
+            pltpu.make_async_copy(in_head, in1.at[pl.ds(0, cut), :], weight_sems.at[1]),
+            pltpu.make_async_copy(
+                in_tail, in1.at[pl.ds(cut, in1.shape[0] - cut), :], weight_sems.at[2]
+            ),
+        ],
+    ]
+    load_out = [
+        [pltpu.make_async_copy(out_own, out0, weight_sems.at[3])],
+        [pltpu.make_async_copy(out_other, out1, weight_sems.at[4])],
+    ]
+    for copies in load_in:
+        for copy in copies:
+            copy.start()
+    rows_g = fetch_rows(1, g_ref)
+    for copies in load_out:
+        for copy in copies:
+            copy.start()
+    sent = []
+
+    def send(kind, product):
+        for part in range(HALVES):
+            at_rows = pl.ds((kind * HALVES + part) * rows, rows)
+            for pair in range(peers // 2):
+                at = (part * peers + 2 * pair) * width
+                block = product(slice(at, at + 2 * width)).astype(BF16)
+                for side in range(2):
+                    peer = 2 * pair + side
+                    ret_ref[peer, at_rows, :] = block[:, side * width : (side + 1) * width]
+                    sent.append(
+                        pltpu.make_async_copy(
+                            ret_ref.at[peer, at_rows, :],
+                            ret_out.at[peer, at_rows, :],
+                            ret_sems.at[kind, part * peers + peer],
+                        )
+                    )
+                    sent[-1].start()
+
+    def keep(ref, out, index):
+        sent.append(pltpu.make_async_copy(ref, out, kept_sems.at[index]))
+        sent[-1].start()
+
+    by_last = ((1,), (1,))
+    for copy in rows_x:
+        copy.wait()
+    keep(x_ref, x_out, 0)
+    acts, slopes, dpres = [], [], []
+    for group, ref in enumerate((in0, in1)):
+        for copy in load_in[group]:
+            copy.wait()
+        value, slope = gelu_parts(dot(x_ref[...], ref[...]))
         acts.append(value.astype(BF16))
-        dpres.append((backed * slope).astype(BF16))
+        slopes.append(slope)
         act_ref[group] = acts[group]
+    for copy in rows_g:
+        copy.wait()
+    keep(g_ref, g_out, 1)
+    for group, ref in enumerate((out0, out1)):
+        for copy in load_out[group]:
+            copy.wait()
+        dpres.append((dot(g_ref[...], ref[...], by_last) * slopes[group]).astype(BF16))
         dpre_ref[group] = dpres[group]
-    for part in range(HALVES):
-        for pair in range(peers // 2):
-            at = (part * peers + 2 * pair) * width
-            cols = slice(at, at + 2 * width)
-            given = dot(acts[0], outs[0][:, cols]) + dot(acts[1], outs[1][:, cols])
-            back = dot(dpres[0], ins[0][cols, :], ((1,), (1,))) + dot(
-                dpres[1], ins[1][cols, :], ((1,), (1,))
-            )
-            for kind, block in ((0, given), (1, back)):
-                block = block.astype(BF16)
-                start = (kind * HALVES + part) * rows
-                ret_ref[2 * pair, start : start + rows, :] = block[:, :width]
-                ret_ref[2 * pair + 1, start : start + rows, :] = block[:, width:]
+    send(0, lambda cols: dot(acts[0], out0[:, cols]) + dot(acts[1], out1[:, cols]))
+    send(
+        1,
+        lambda cols: dot(dpres[0], in0[cols, :], by_last) + dot(dpres[1], in1[cols, :], by_last),
+    )
+    for copy in sent:
+        copy.wait()
 
 
 def combine_kernel(rows_ref, gates_ref, home_ref, mixed_ref, grad_ref):
@@ -168,12 +252,17 @@
     grad_ref[...] = dot(mask(at0 | at1), back, over_rows).astype(BF16)
 
 
-def call(kernel, shapes, flops, moved, *args):
+def call(kernel, shapes, cost, places, limit, scratch, *args):
+    ins, outs = places
+    flops, moved = cost
     return pl.pallas_call(
         kernel,
         out_shape=shapes,
+        in_specs=[pl.BlockSpec(memory_space=place) for place in ins],
+        out_specs=tuple(pl.BlockSpec(memory_space=place) for place in outs),
+        scratch_shapes=scratch,
         cost_estimate=pl.CostEstimate(flops=flops, bytes_accessed=moved, transcendentals=0),
-        compiler_params=pltpu.CompilerParams(vmem_limit_bytes=40 * 1024 * 1024),
+        compiler_params=pltpu.CompilerParams(vmem_limit_bytes=limit * 1024 * 1024),
     )(*args)
 
 
@@ -191,7 +280,10 @@
     used = cap // HALVES
     chunks = experts * HALVES
     rows = experts * used
+    both_rows = HALVES * rows
     model = width * cuts
+    near, far = pltpu.VMEM, pltpu.HBM
+    dma = pltpu.SemaphoreType.DMA
     swap = [(c, (c + peers) % cuts) for c in range(cuts)]
     line = [[h * peers + y for y in range(peers)] for h in range(HALVES)]
     plane = [
@@ -210,28 +302,40 @@
 
     in_own, out_own = w_in[0], w_out[0]
     hidden = in_own.shape[1]
-    in_other, out_other = to_partner(in_own), to_partner(out_own)
+    cut = model * 3 // 4
+    in_head = to_partner(in_own[:cut])
+    in_tail, out_other = to_partner(in_own[cut:]), to_partner(out_own)
     routes_t, gates_t = routes.T, gates.T
 
     sent, places = call(
         functools.partial(place_kernel, experts, cap),
         (struct(chunks, 2 * PAD, width), struct(chosen, tok_rows, dtype=jnp.int32)),
-        4 * chunks * PAD * tok_rows * width,
-        8 * chunks * PAD * width,
+        (4 * chunks * PAD * tok_rows * width, 8 * chunks * PAD * width),
+        ([far] * 4, [near] * 2),
+        16,
+        [
+            pltpu.VMEM((chosen, tok_rows), jnp.int32),
+            pltpu.VMEM((chosen, tok_rows), F32),
+            pltpu.VMEM((tok_rows, 2 * width), BF16),
+            dma((4,)),
+        ],
         routes_t,
         gates_t,
         tokens,
         cotangent,
     )
     recv = over_plane(sent)
-    packed = call(
+    spread = call(
         functools.partial(pack_kernel, experts, used),
-        struct(4 * rows, width),
-        8 * rows * experts * PAD * width,
-        8 * rows * 4 * width,
+        (struct(peers, 4 * rows, width),),
+        (8 * rows * experts * PAD * width, 8 * both_rows * peers * width),
+        ([near], [far]),
+        56,
+        [pltpu.VMEM((4 * rows, width), BF16), dma((2, peers))],
         recv,
-    )
-    lined = over_line(jnp.broadcast_to(packed[None], (peers, 4 * rows, width)))
+    )[0]
+    spread, in_head = lax.optimization_barrier((spread, in_head))
+    lined = over_line(spread)
     ret, held_x, held_g, active, dpre = call(
         expert_kernel,
         (
@@ -241,11 +345,26 @@
             struct(2, rows, hidden),
             struct(2, rows, hidden),
         ),
-        16 * rows * model * hidden,
-        24 * rows * model,
+        (16 * rows * model * hidden, 12 * rows * model + 8 * model * hidden),
+        ([far] * 6, [far] * 3 + [near] * 2),
+        60,
+        [
+            pltpu.VMEM((rows, model), BF16),
+            pltpu.VMEM((rows, model), BF16),
+            pltpu.VMEM((model, hidden), BF16),
+            pltpu.VMEM((model, hidden), BF16),
+            pltpu.VMEM((hidden, model), BF16),
+            pltpu.VMEM((hidden, model), BF16),
+            pltpu.VMEM((peers, 4 * rows, width), BF16),
+            dma((2, cuts)),
+            dma((5,)),
+            dma((2, cuts)),
+            dma((2,)),
+        ],
         lined,
         in_own,
-        in_other,
+        in_head,
+        in_tail,
         out_own,
         out_other,
     )
@@ -255,19 +374,23 @@
     sent_out = to_partner(dot(active[1], held_g, over_rows).astype(BF16))
     summed = call(
         functools.partial(sum_kernel, experts, used),
-        struct(chunks, 2 * PAD, width),
-        8 * rows * experts * PAD * width,
-        8 * rows * peers * width,
+        (struct(chunks, 2 * PAD, width),),
+        (8 * rows * experts * PAD * width, 8 * rows * peers * width),
+        ([near], [near]),
+        16,
+        [],
         returned,
-    )
+    )[0]
     home = over_plane(summed)
     grad_in = (dot(held_x, dpre[0], over_rows) + sent_in.astype(F32)).astype(BF16)[None]
     grad_out = (dot(active[0], held_g, over_rows) + sent_out.astype(F32)).astype(BF16)[None]
     mixed, token_grad = call(
         combine_kernel,
         (struct(tok_rows, width), struct(tok_rows, width)),
-        6 * chunks * PAD * tok_rows * width,
-        8 * chunks * PAD * width,
+        (6 * chunks * PAD * tok_rows * width, 8 * chunks * PAD * width),
+        ([near] * 3, [near] * 2),
+        16,
+        [],
         places,
         gates_t,
         home,

time: 168 us -> 159 us (0.946)
  waiting for transfers between devices: 83.7 us -> 72.8 us
  local copies, waits for them, and re-layouts: 12.2 us -> 4.24 us
  Pallas kernels: 5.35 us -> 12.8 us
  starting transfers between devices: 28.4 us -> 31.8 us
    ppermute x4 -> x5, waiting for transfers between devices: 42.9 us -> 27.6 us  [to_partner(): return lax.ppermute(value, 'cuts', swap)]
    unnamed x26 -> x24, local copies, waits for them, and re-layouts: 10.9 us -> 2.06 us
    pallas_call x5, Pallas kernels: 5.35 us -> 12.8 us  [call(): pl.pallas_call(kernel, out_shape=shapes, in_specs=[pl.BlockSpec(memory_sp...]
    all_to_all x2, waiting for transfers between devices: 32.3 us -> 38.3 us  [over_line(): lax.all_to_all(value, 'cuts', 0, 0, tiled=True, axis_index_groups=line)]
    ppermute x4 -> x5, starting transfers between devices: 10.5 us -> 14.5 us  [to_partner(): return lax.ppermute(value, 'cuts', swap)]
    all_to_all x2, starting transfers between devices: 13.3 us -> 10.5 us  [over_line(): lax.all_to_all(value, 'cuts', 0, 0, tiled=True, axis_index_groups=line)]
    slice x0 -> x2, local copies, waits for them, and re-layouts: none -> 2.18 us  [the longest x1 1.21 us: body(): in_head = to_partner(in_own[:cut])]
    all_to_all x1, starting transfers between devices: 4.6 us -> 6.73 us  [over_plane(): lax.all_to_all(value, ('dp', 'cuts'), 0, 0, tiled=True, axis_index_groups...]
  transfers between devices with their start and end apart: 7 -> 8, of which waited for: 5 -> 5; matrix products, arithmetic and copies ran while one was open for 5% -> 6% of each run, Pallas kernels for 1% -> 3%
where the time goes in v3:
time: 159 us
  waiting for transfers between devices  72.8 us (46%)
  starting transfers between devices  31.8 us (20%)
  blocking collectives  27.8 us (17%)
  Pallas kernels  12.8 us (8%)
  matrix products  8.25 us (5%)
  local copies, waits for them, and re-layouts  4.24 us (3%)
    all_to_all x2, waiting for transfers between devices, over_line(): lax.all_to_all(value, 'cuts', 0, 0, tiled=True, axis_index_groups=line)  38.3 us
    all_to_all x1, blocking collectives, over_plane(): lax.all_to_all(value, ('dp', 'cuts'), 0, 0, tiled=True, axis_index_groups...  27.8 us
    ppermute x5, waiting for transfers between devices, to_partner(): return lax.ppermute(value, 'cuts', swap)  27.6 us
    ppermute x5, starting transfers between devices, to_partner(): return lax.ppermute(value, 'cuts', swap)  14.5 us
    pallas_call x5, Pallas kernels, call(): pl.pallas_call(kernel, out_shape=shapes, in_specs=[pl.BlockSpec(memory_sp...  12.8 us
    all_to_all x2, starting transfers between devices, over_line(): lax.all_to_all(value, 'cuts', 0, 0, tiled=True, axis_index_groups=line)  10.5 us
    dot_general x4, matrix products, dot(): lax.dot_general(left, right, (dims, ((), ())), preferred_element_type=F32)  8.25 us
    all_to_all x1, waiting for transfers between devices, over_plane(): lax.all_to_all(value, ('dp', 'cuts'), 0, 0, tiled=True, axis_index_groups...  6.87 us
  transfers between devices with their start and end apart: 8, of which 5 were waited for; matrix products, arithmetic and copies ran while one was open for 6% of the time, Pallas kernels for 3%

profile of v3, /device:TPU:1, one launch (start us, length us, event | category | flops | bytes accessed | tf_op | source)
XLA Modules:
  0.0 158.6 jit_solution(15131296496986509901)
XLA Ops:
  0.7 1.2 slice_bitcast_fusion
  1.9 3.9 %collective-permute-start = (bf16[1536,256]{1,0:T(8,128)(2,1)S(1)}, bf16[1536,256]{1,0:T(8,128)(2,1)S(1)}, u32[]{:S(2)}, u32[]{:S(2)}) collective-permute-start(bf16[1536,256]{1,0:T(8,128)(2,1)S(1)} %slice_bitcast_fusion), channel_id=1, source_target_pairs={{0,8},{1,9},{2,10},{3,11},{4,12},{5,13},{6,14},{7,15},{8,0},{9,1},... | collective-permute-start | bytes 2359304 | tf_op jit(solution)/shard_map/ppermute | solution.py:295
  5.9 0.7 shard_map.93
  6.5 27.8 %all_to_all.20.recv_ref = bf16[64,16,128]{2,1,0:T(8,128)(2,1)} all-to-all(bf16[64,16,128]{2,1,0:T(8,128)(2,1)S(1)} %get-tuple-element.16), channel_id=1, replica_groups={{0,8,16,24,32,40,48,56,64,72,80,88,96,104,112,120,128,136,144,152,160,1..., dimensions={0} | all-to-all | bytes 524288 | tf_op jit(solution)/shard_map/all_to_all | solution.py:298
  34.4 2.4 %shard_map.94 = bf16[8,768,128]{2,1,0:T(8,128)(2,1)} custom-call(bf16[64,16,128]{2,1,0:T(8,128)(2,1)} %all_to_all.20.recv_ref), custom_call_target="tpu_custom_call" | custom-call | flops 50331648 | bytes 3145728 | tf_op jit(solution)/shard_map/pallas_call | solution.py:258
  36.8 0.0 copy-start.9
  36.8 0.0 collective-permute-done.in_head
  36.9 0.0 copy-start.10
  36.9 0.9 copy-done.10
  37.7 6.8 %all-to-all-start.1 = ((bf16[8,768,128]{2,1,0:T(8,128)(2,1)}), bf16[8,768,128]{2,1,0:T(8,128)(2,1)S(1)}, u32[]{:S(2)}, u32[]{:S(2)}) async-start(bf16[8,768,128]{2,1,0:T(8,128)(2,1)} %shard_map.94), calls=%async_computation.1 | async-start | bytes 3145728 | tf_op jit(solution)/shard_map/all_to_all | solution.py:301
  44.6 2.2 %collective-permute-start.2 = (bf16[256,2048]{1,0:T(8,128)(2,1)S(1)}, bf16[256,2048]{1,0:T(8,128)(2,1)}, u32[]{:S(2)}, u32[]{:S(2)}) collective-permute-start(bf16[256,2048]{1,0:T(8,128)(2,1)S(1)} %bitcast.33), channel_id=1, source_target_pairs={{0,8},{1,9},{2,10},{3,11},{4,12},{5,13},{6,14},{7,15},{8,0},{9,1},... | collective-permute-start | bytes 3145736 | tf_op jit(solution)/shard_map/ppermute | solution.py:295
  46.8 1.0 slice_bitcast_fusion.1
  47.8 3.0 %collective-permute-start.1 = (bf16[512,256]{1,0:T(8,128)(2,1)S(1)}, bf16[512,256]{1,0:T(8,128)(2,1)S(1)}, u32[]{:S(2)}, u32[]{:S(2)}) collective-permute-start(bf16[512,256]{1,0:T(8,128)(2,1)S(1)} %slice_bitcast_fusion.1), channel_id=1, source_target_pairs={{0,8},{1,9},{2,10},{3,11},{4,12},{5,13},{6,14},{7,15},{8,0},{9,1},... | collective-permute-start | bytes 786440 | tf_op jit(solution)/shard_map/ppermute | solution.py:295
  50.8 25.8 %collective-permute-done.1.in_tail = bf16[512,256]{1,0:T(8,128)(2,1)S(1)} collective-permute-done((bf16[512,256]{1,0:T(8,128)(2,1)S(1)}, bf16[512,256]{1,0:T(8,128)(2,1)S(1)}, u32[]{:S(2)}, u32[]{:S(2)}) %collective-permute-start.1) | collective-permute-done | bytes 262176 | tf_op jit(solution)/shard_map/ppermute | solution.py:295
  76.7 0.0 collective-permute-done.2.out_other
  76.7 8.4 %all-to-all-done.1.recv = bf16[8,768,128]{2,1,0:T(8,128)(2,1)S(1)} async-done(((bf16[8,768,128]{2,1,0:T(8,128)(2,1)}), bf16[8,768,128]{2,1,0:T(8,128)(2,1)S(1)}, u32[]{:S(2)}, u32[]{:S(2)}) %all-to-all-start.1) | async-done | bytes 1572896 | tf_op jit(solution)/shard_map/all_to_all | solution.py:301
  85.0 1.1 copy-done.6
  86.2 7.6 %shard_map.95 = (bf16[8,768,128]{2,1,0:T(8,128)(2,1)}, bf16[192,2048]{1,0:T(8,128)(2,1)}, bf16[192,2048]{1,0:T(8,128)(2,1)}, bf16[2,192,256]{2,1,0:T(8,128)(2,1)}, bf16[2,192,256]{2,1,0:T(8,128)(2,1)}) custom-call(bf16[8,768,128]{2,1,0:T(8,128)(2,1)} %copy-done.6, bf16[2048,256]{1,0:T(8,128)(2,1)} %bitcast.31, bf16[1536,256]{1,0:T(8,128)(2,1)} %copy-done.10, ...), custom_call_target="tpu_custom_call" | custom-call | flops 1610612736 | bytes 8912896 | tf_op jit(solution)/shard_map/pallas_call | solution.py:258
  93.8 3.7 %all-to-all-start.2 = ((bf16[8,768,128]{2,1,0:T(8,128)(2,1)}), bf16[8,768,128]{2,1,0:T(8,128)(2,1)S(1)}, u32[]{:S(2)}, u32[]{:S(2)}) async-start(bf16[8,768,128]{2,1,0:T(8,128)(2,1)} %get-tuple-element.19), calls=%async_computation.2 | async-start | bytes 3145728 | tf_op jit(solution)/shard_map/all_to_all | solution.py:301
  97.5 0.0 copy-start.4
  97.6 1.4 convolution_convert_fusion
  99.0 2.2 %collective-permute-start.4 = (bf16[256,2048]{1,0:T(8,128)(2,1)}, bf16[256,2048]{1,0:T(8,128)(2,1)}, u32[]{:S(2)}, u32[]{:S(2)}) collective-permute-start(bf16[256,2048]{1,0:T(8,128)(2,1)} %convolution_convert_fusion), channel_id=1, source_target_pairs={{0,8},{1,9},{2,10},{3,11},{4,12},{5,13},{6,14},{7,15},{8,0},{9,1},... | collective-permute-start | bytes 3145736 | tf_op jit(solution)/shard_map/ppermute | solution.py:295
  101.2 1.5 convolution_convert_fusion.1
  102.7 3.0 %collective-permute-start.3 = (bf16[2048,256]{1,0:T(8,128)(2,1)}, bf16[2048,256]{1,0:T(8,128)(2,1)}, u32[]{:S(2)}, u32[]{:S(2)}) collective-permute-start(bf16[2048,256]{1,0:T(8,128)(2,1)} %convolution_convert_fusion.1), channel_id=1, source_target_pairs={{0,8},{1,9},{2,10},{3,11},{4,12},{5,13},{6,14},{7,15},{8,0},{9,1},... | collective-permute-start | bytes 3145736 | tf_op jit(solution)/shard_map/ppermute | solution.py:295
  105.8 29.9 %all-to-all-done.2.recv_ref = bf16[8,768,128]{2,1,0:T(8,128)(2,1)S(1)} async-done(((bf16[8,768,128]{2,1,0:T(8,128)(2,1)}), bf16[8,768,128]{2,1,0:T(8,128)(2,1)S(1)}, u32[]{:S(2)}, u32[]{:S(2)}) %all-to-all-start.2) | async-done | bytes 1572896 | tf_op jit(solution)/shard_map/all_to_all | solution.py:301
  135.7 1.1 shard_map.96
  136.8 6.7 %all-to-all-start.3 = ((bf16[64,16,128]{2,1,0:T(8,128)(2,1)}), bf16[64,16,128]{2,1,0:T(8,128)(2,1)S(1)}, u32[]{:S(2)}, u32[]{:S(2)}) async-start(bf16[64,16,128]{2,1,0:T(8,128)(2,1)} %shard_map.96), calls=%async_computation.3 | async-start | bytes 524288 | tf_op jit(solution)/shard_map/all_to_all | solution.py:298
  143.6 2.7 %fusion.2 = bf16[1,256,2048]{2,1,0:T(8,128)(2,1)} fusion(bf16[192,2048]{1,0:T(8,128)(2,1)S(1)} %copy-done.5, bf16[256,2048]{1,0:T(8,128)(2,1)} %collective-permute-done.4, bf16[2,192,256]{2,1,0:T(8,128)(2,1)S(1)} %copy-done.8), kind=kOutput, calls=%fused_computation.6 | convolution fusion | flops 202899456 | bytes 2981888 | tf_op jit(solution)/shard_map/dot_general | solution.py:29
  146.2 1.8 %collective-permute-done.3 = bf16[2048,256]{1,0:T(8,128)(2,1)} collective-permute-done((bf16[2048,256]{1,0:T(8,128)(2,1)}, bf16[2048,256]{1,0:T(8,128)(2,1)}, u32[]{:S(2)}, u32[]{:S(2)}) %collective-permute-start.3) | collective-permute-done | bytes 1048608 | tf_op jit(solution)/shard_map/ppermute | solution.py:295
  148.0 2.7 %fusion.3 = bf16[1,2048,256]{2,1,0:T(8,128)(2,1)} fusion(bf16[192,2048]{1,0:T(8,128)(2,1)S(1)} %copy-done.4, bf16[2048,256]{1,0:T(8,128)(2,1)} %collective-permute-done.3, bf16[2,192,256]{2,1,0:T(8,128)(2,1)S(1)} %copy-done.7), kind=kOutput, calls=%fused_computation.7 | convolution fusion | flops 202899456 | bytes 2981888 | tf_op jit(solution)/shard_map/dot_general | solution.py:29
  150.7 6.9 %all-to-all-done.3.home_ref = bf16[64,16,128]{2,1,0:T(8,128)(2,1)S(1)} async-done(((bf16[64,16,128]{2,1,0:T(8,128)(2,1)}), bf16[64,16,128]{2,1,0:T(8,128)(2,1)S(1)}, u32[]{:S(2)}, u32[]{:S(2)}) %all-to-all-start.3) | async-done | bytes 262176 | tf_op jit(solution)/shard_map/all_to_all | solution.py:298
  157.6 1.0 shard_map.97
  (20 shorter events, 0.0 us)
Async XLA Ops:
  0.6 5.2 %copy-start.3 = (s32[128,2]{0,1:T(2,128)S(1)}, s32[128,2]{0,1:T(2,128)}, u32[]{:S(2)}) copy-start(s32[128,2]{0,1:T(2,128)} %param.9) | copy-start | bytes 3076
  0.6 5.2 %copy-start = (f32[128,2]{0,1:T(2,128)S(1)}, f32[128,2]{0,1:T(2,128)}, u32[]{:S(2)}) copy-start(f32[128,2]{0,1:T(2,128)} %param.8) | copy-start | bytes 3076
  0.7 5.2 %copy-start.2 = (bf16[128,128]{1,0:T(8,128)(2,1)S(1)}, bf16[128,128]{1,0:T(8,128)(2,1)}, u32[]{:S(2)}) copy-start(bf16[128,128]{1,0:T(8,128)(2,1)} %cot_in.1) | copy-start | bytes 98308
  0.7 5.2 %copy-start.1 = (bf16[128,128]{1,0:T(8,128)(2,1)S(1)}, bf16[128,128]{1,0:T(8,128)(2,1)}, u32[]{:S(2)}) copy-start(bf16[128,128]{1,0:T(8,128)(2,1)} %tok_in.1) | copy-start | bytes 98308
  1.9 35.0 %collective-permute-start = (bf16[1536,256]{1,0:T(8,128)(2,1)S(1)}, bf16[1536,256]{1,0:T(8,128)(2,1)S(1)}, u32[]{:S(2)}, u32[]{:S(2)}) collective-permute-start(bf16[1536,256]{1,0:T(8,128)(2,1)S(1)} %slice_bitcast_fusion), channel_id=1, source_target_pairs={{0,8},{1,9},{2,10},{3,11},{4,12},{5,13},{6,14},{7,15},{8,0},{9,1},... | collective-permute-start | bytes 2359304 | tf_op jit(solution)/shard_map/ppermute | solution.py:295
  36.8 7.7 %copy-start.9 = (bf16[1,256,2048]{2,1,0:T(8,128)(2,1)S(1)}, bf16[1,256,2048]{2,1,0:T(8,128)(2,1)}, u32[]{:S(2)}) copy-start(bf16[1,256,2048]{2,1,0:T(8,128)(2,1)} %param.11) | copy-start | bytes 3145732
  36.9 0.9 copy-start.10
  37.7 47.3 %all-to-all-start.1 = ((bf16[8,768,128]{2,1,0:T(8,128)(2,1)}), bf16[8,768,128]{2,1,0:T(8,128)(2,1)S(1)}, u32[]{:S(2)}, u32[]{:S(2)}) async-start(bf16[8,768,128]{2,1,0:T(8,128)(2,1)} %shard_map.94), calls=%async_computation.1 | async-start | bytes 3145728 | tf_op jit(solution)/shard_map/all_to_all | solution.py:301
  44.6 32.1 %collective-permute-start.2 = (bf16[256,2048]{1,0:T(8,128)(2,1)S(1)}, bf16[256,2048]{1,0:T(8,128)(2,1)}, u32[]{:S(2)}, u32[]{:S(2)}) collective-permute-start(bf16[256,2048]{1,0:T(8,128)(2,1)S(1)} %bitcast.33), channel_id=1, source_target_pairs={{0,8},{1,9},{2,10},{3,11},{4,12},{5,13},{6,14},{7,15},{8,0},{9,1},... | collective-permute-start | bytes 3145736 | tf_op jit(solution)/shard_map/ppermute | solution.py:295
  47.8 28.9 %collective-permute-start.1 = (bf16[512,256]{1,0:T(8,128)(2,1)S(1)}, bf16[512,256]{1,0:T(8,128)(2,1)S(1)}, u32[]{:S(2)}, u32[]{:S(2)}) collective-permute-start(bf16[512,256]{1,0:T(8,128)(2,1)S(1)} %slice_bitcast_fusion.1), channel_id=1, source_target_pairs={{0,8},{1,9},{2,10},{3,11},{4,12},{5,13},{6,14},{7,15},{8,0},{9,1},... | collective-permute-start | bytes 786440 | tf_op jit(solution)/shard_map/ppermute | solution.py:295
  76.6 8.4 %copy-start.11 = (bf16[512,256]{1,0:T(8,128)(2,1)}, bf16[512,256]{1,0:T(8,128)(2,1)S(1)}, u32[]{:S(2)}) copy-start(bf16[512,256]{1,0:T(8,128)(2,1)S(1)} %collective-permute-done.1.in_tail) | copy-start | bytes 786436
  85.0 1.1 copy-start.6
  93.8 3.8 %copy-start.5 = (bf16[192,2048]{1,0:T(8,128)(2,1)S(1)}, bf16[192,2048]{1,0:T(8,128)(2,1)}, u32[]{:S(2)}) copy-start(bf16[192,2048]{1,0:T(8,128)(2,1)} %get-tuple-element.25) | copy-start | bytes 2359300
  93.8 3.8 %copy-start.8 = (bf16[2,192,256]{2,1,0:T(8,128)(2,1)S(1)}, bf16[2,192,256]{2,1,0:T(8,128)(2,1)}, u32[]{:S(2)}) copy-start(bf16[2,192,256]{2,1,0:T(8,128)(2,1)} %get-tuple-element.24) | copy-start | bytes 589828
  93.8 41.9 %all-to-all-start.2 = ((bf16[8,768,128]{2,1,0:T(8,128)(2,1)}), bf16[8,768,128]{2,1,0:T(8,128)(2,1)S(1)}, u32[]{:S(2)}, u32[]{:S(2)}) async-start(bf16[8,768,128]{2,1,0:T(8,128)(2,1)} %get-tuple-element.19), calls=%async_computation.2 | async-start | bytes 3145728 | tf_op jit(solution)/shard_map/all_to_all | solution.py:301
  97.5 3.7 %copy-start.4 = (bf16[192,2048]{1,0:T(8,128)(2,1)S(1)}, bf16[192,2048]{1,0:T(8,128)(2,1)}, u32[]{:S(2)}) copy-start(bf16[192,2048]{1,0:T(8,128)(2,1)} %get-tuple-element.22) | copy-start | bytes 2359300
  97.5 3.7 %copy-start.7 = (bf16[2,192,256]{2,1,0:T(8,128)(2,1)S(1)}, bf16[2,192,256]{2,1,0:T(8,128)(2,1)}, u32[]{:S(2)}) copy-start(bf16[2,192,256]{2,1,0:T(8,128)(2,1)} %get-tuple-element.23) | copy-start | bytes 589828
  99.0 44.6 %collective-permute-start.4 = (bf16[256,2048]{1,0:T(8,128)(2,1)}, bf16[256,2048]{1,0:T(8,128)(2,1)}, u32[]{:S(2)}, u32[]{:S(2)}) collective-permute-start(bf16[256,2048]{1,0:T(8,128)(2,1)} %convolution_convert_fusion), channel_id=1, source_target_pairs={{0,8},{1,9},{2,10},{3,11},{4,12},{5,13},{6,14},{7,15},{8,0},{9,1},... | collective-permute-start | bytes 3145736 | tf_op jit(solution)/shard_map/ppermute | solution.py:295
  102.7 45.3 %collective-permute-start.3 = (bf16[2048,256]{1,0:T(8,128)(2,1)}, bf16[2048,256]{1,0:T(8,128)(2,1)}, u32[]{:S(2)}, u32[]{:S(2)}) collective-permute-start(bf16[2048,256]{1,0:T(8,128)(2,1)} %convolution_convert_fusion.1), channel_id=1, source_target_pairs={{0,8},{1,9},{2,10},{3,11},{4,12},{5,13},{6,14},{7,15},{8,0},{9,1},... | collective-permute-start | bytes 3145736 | tf_op jit(solution)/shard_map/ppermute | solution.py:295
  136.8 20.8 %all-to-all-start.3 = ((bf16[64,16,128]{2,1,0:T(8,128)(2,1)}), bf16[64,16,128]{2,1,0:T(8,128)(2,1)S(1)}, u32[]{:S(2)}, u32[]{:S(2)}) async-start(bf16[64,16,128]{2,1,0:T(8,128)(2,1)} %shard_map.96), calls=%async_computation.3 | async-start | bytes 524288 | tf_op jit(solution)/shard_map/all_to_all | solution.py:298

commit v4 on v3

v4 whole, which is shorter than its diff:
```python
import functools
import math

import jax
import jax.numpy as jnp
from jax import lax
from jax.experimental import pallas as pl
from jax.experimental.pallas import tpu as pltpu
from jax.sharding import PartitionSpec as P

BF16 = jnp.bfloat16
F32 = jnp.float32
HALVES = 2
FOUR = 4


def gelu_parts(pre):
    coef = math.sqrt(2.0 / math.pi)
    inner = coef * (pre + 0.044715 * pre * pre * pre)
    tangent = jnp.tanh(inner)
    value = 0.5 * pre * (1.0 + tangent)
    slope = 0.5 * (1.0 + tangent) + 0.5 * pre * (1.0 - tangent * tangent) * coef * (
        1.0 + 3.0 * 0.044715 * pre * pre
    )
    return (value, slope)


def dot(left, right, dims=((1,), (0,))):
    return lax.dot_general(left, right, (dims, ((), ())), preferred_element_type=F32)


def iota(shape, axis):
    return lax.broadcasted_iota(jnp.int32, shape, axis)


def mask(hit):
    return jnp.where(hit, 1.0, 0.0).astype(BF16)


def place_kernel(experts, cap, routes_in, gates_in, tok_in, cot_in, sent, rows_ref, *scratch):
    routes_ref, gates_ref, tok_ref, cot_ref, held_ref, sems, sent_sems = scratch
    tok_rows = tok_in.shape[0]
    copies = [
        pltpu.make_async_copy(routes_in, routes_ref, sems.at[0]),
        pltpu.make_async_copy(gates_in, gates_ref, sems.at[1]),
        pltpu.make_async_copy(tok_in, tok_ref, sems.at[2]),
        pltpu.make_async_copy(cot_in, cot_ref, sems.at[3]),
    ]
    for copy in copies:
        copy.start()
    copies[0].wait()
    routes = routes_ref[...]
    first, second = routes[0:1, :], routes[1:2, :]
    names = iota((experts, tok_rows), 0)
    hit0, hit1 = names == first, names == second
    either = jnp.where(hit0 | hit1, 1.0, 0.0).astype(BF16)
    earlier = iota((tok_rows, tok_rows), 0) < iota((tok_rows, tok_rows), 1)
    count = dot(either, jnp.where(earlier, 1.0, 0.0).astype(BF16))
    used = cap // HALVES

    def row_of(hit, expert):
        position = jnp.sum(jnp.where(hit, count, 0.0), axis=0, keepdims=True).astype(jnp.int32)
        upper = jnp.where(position >= used, 1, 0)
        return (expert * HALVES + upper) * cap + position - upper * used

    row0, row1 = row_of(hit0, first), row_of(hit1, second)
    rows_ref[0:1, :] = row0
    rows_ref[1:2, :] = row1
    slot = iota((experts * HALVES * cap, tok_rows), 0)
    at_x = (slot == row0) | (slot == row1)
    at0, at1 = slot == row0 + used, slot == row1 + used
    copies[1].wait()
    gates = gates_ref[...]
    gate = jnp.sum(
        jnp.where(at0, gates[0:1, :], 0.0) + jnp.where(at1, gates[1:2, :], 0.0),
        axis=1,
        keepdims=True,
    )
    copies[2].wait()
    copies[3].wait()
    held_x = dot(mask(at_x), tok_ref[...])
    held_g = dot(mask(at0 | at1), cot_ref[...]) * gate
    held_ref[...] = (held_x + held_g).astype(BF16)
    copies = [
        pltpu.make_async_copy(held_ref, sent.at[index], sent_sems.at[index])
        for index in range(sent.shape[0])
    ]
    for copy in copies:
        copy.start()
    for copy in copies:
        copy.wait()


def sorted_row(at, used, sources):
    group = 4 * used
    scale = -(-(1 << 16) // group)
    source = lax.shift_right_logical(at * scale, 16)
    inner = at - source * group
    block = lax.shift_right_logical(inner * -(-(1 << 16) // used), 16)
    return block * (sources * used) + source * used + inner - block * used


def expert_kernel(used, odd_ref, own, low, high, in_own, in_other, out_own, out_head, out_tail, *rest):
    ret_own, ret_low, ret_high, x_out, g_out, act_ref, dpre_ref = rest[:7]
    recv_ref, pick_ref, spread_ref, x_ref, g_ref, in0, in1, out0, out1, held_ref, ret_ref = rest[7:18]
    recv_sems, weight_sems, ret_sems, kept_sems = rest[18:]
    classes, all_rows, width = own.shape
    peers = 2 * classes
    rows = all_rows // 4
    sources = rows // used
    side = classes // 2
    cut = out_head.shape[0]
    odd = odd_ref[0]

    def columns(index, other):
        place = 2 * index + (1 - odd if other else odd)
        return pl.ds(pl.multiple_of(place * width, width), width)

    moves = [(own, q, columns(q, False)) for q in range(classes)]
    moves += [(low, q, columns(q, True)) for q in range(side)]
    moves += [(high, q, columns(q + side, True)) for q in range(side)]
    arrive = [
        pltpu.make_async_copy(ref.at[q], recv_ref.at[:, cols], recv_sems.at[index])
        for index, (ref, q, cols) in enumerate(moves)
    ]
    load_in = [
        pltpu.make_async_copy(in_own, in0, weight_sems.at[0]),
        pltpu.make_async_copy(in_other, in1, weight_sems.at[1]),
    ]
    load_out = [
        [pltpu.make_async_copy(out_own, out0, weight_sems.at[2])],
        [
            pltpu.make_async_copy(out_head, out1.at[pl.ds(0, cut), :], weight_sems.at[3]),
            pltpu.make_async_copy(
                out_tail, out1.at[pl.ds(cut, out1.shape[0] - cut), :], weight_sems.at[4]
            ),
        ],
    ]
    for copy in arrive + load_in + load_out[0] + load_out[1]:
        copy.start()
    shape = (all_rows, all_rows)
    pick_ref[...] = mask(iota(shape, 0) == sorted_row(iota((1, all_rows), 1), used, sources))
    spread_ref[...] = mask(iota(shape, 1) == sorted_row(iota((all_rows, 1), 0), used, sources))
    for copy in arrive:
        copy.wait()
    for pair in range(classes):
        cols = slice(pair * 2 * width, (pair + 1) * 2 * width)
        block = dot(pick_ref[...], recv_ref[:, cols]).astype(BF16)
        for part in range(HALVES):
            at = (part * peers + 2 * pair) * width
            start = part * 2 * rows
            x_ref[:, at : at + 2 * width] = block[start : start + rows, :]
            g_ref[:, at : at + 2 * width] = block[start + rows : start + 2 * rows, :]
    kept = [
        pltpu.make_async_copy(x_ref, x_out, kept_sems.at[0]),
        pltpu.make_async_copy(g_ref, g_out, kept_sems.at[1]),
    ]
    for copy in kept:
        copy.start()

    by_last = ((1,), (1,))
    acts, slopes, dpres = [], [], []
    for group, ref in enumerate((in0, in1)):
        load_in[group].wait()
        value, slope = gelu_parts(dot(x_ref[...], ref[...]))
        acts.append(value.astype(BF16))
        slopes.append(slope)
        act_ref[group] = acts[group]
    for group, ref in enumerate((out0, out1)):
        for copy in load_out[group]:
            copy.wait()
        dpres.append((dot(g_ref[...], ref[...], by_last) * slopes[group]).astype(BF16))
        dpre_ref[group] = dpres[group]
    for pair in range(classes):
        for part in range(HALVES):
            at = (part * peers + 2 * pair) * width
            cols = slice(at, at + 2 * width)
            given = dot(acts[0], out0[:, cols]) + dot(acts[1], out1[:, cols])
            back = dot(dpres[0], in0[cols, :], by_last) + dot(dpres[1], in1[cols, :], by_last)
            start = part * 2 * rows
            held_ref[start : start + rows, :] = given.astype(BF16)
            held_ref[start + rows : start + 2 * rows, :] = back.astype(BF16)
        ret_ref[:, pair * 2 * width : (pair + 1) * 2 * width] = dot(
            spread_ref[...], held_ref[...]
        ).astype(BF16)
    moves = [(ret_own, q, columns(q, False)) for q in range(classes)]
    moves += [(ret_low, q, columns(q, True)) for q in range(side)]
    moves += [(ret_high, q, columns(q + side, True)) for q in range(side)]
    leave = [
        pltpu.make_async_copy(ret_ref.at[:, cols], ref.at[q], ret_sems.at[index])
        for index, (ref, q, cols) in enumerate(moves)
    ]
    for copy in leave:
        copy.start()
    for copy in leave + kept:
        copy.wait()


def add_kernel(own_ref, low_ref, high_ref, out_ref):
    side = low_ref.shape[0]
    for index in range(own_ref.shape[0]):
        ref = low_ref.at[index] if index < side else high_ref.at[index - side]
        out_ref[index] = (own_ref[index].astype(F32) + ref[...].astype(F32)).astype(BF16)


def combine_kernel(used, rows_ref, gates_ref, home_ref, mixed_ref, grad_ref):
    groups, all_rows, _ = home_ref.shape
    tok_rows = mixed_ref.shape[0]
    slot = iota((all_rows, tok_rows), 0)
    row0, row1 = rows_ref[0:1, :], rows_ref[1:2, :]
    diagonal = iota((tok_rows, tok_rows), 0) == iota((tok_rows, tok_rows), 1)

    def column(row):
        return jnp.sum(jnp.where(diagonal, row, 0.0), axis=1, keepdims=True)

    def picked(hit):
        chosen = mask(hit)
        return sum(dot(chosen, home_ref[group], ((0,), (0,))) for group in range(groups))

    mixed = column(gates_ref[0:1, :]) * picked(slot == row0) + column(
        gates_ref[1:2, :]
    ) * picked(slot == row1)
    mixed_ref[...] = mixed.astype(BF16)
    grad_ref[...] = picked((slot == row0 + used) | (slot == row1 + used)).astype(BF16)


def call(kernel, shapes, cost, places, limit, scratch, *args):
    ins, outs = places
    flops, moved = cost
    return pl.pallas_call(
        kernel,
        out_shape=shapes,
        in_specs=[pl.BlockSpec(memory_space=place) for place in ins],
        out_specs=tuple(pl.BlockSpec(memory_space=place) for place in outs),
        scratch_shapes=scratch,
        cost_estimate=pl.CostEstimate(flops=flops, bytes_accessed=moved, transcendentals=0),
        compiler_params=pltpu.CompilerParams(vmem_limit_bytes=limit * 1024 * 1024),
    )(*args)


def struct(*shape, dtype=BF16):
    return jax.ShapeDtypeStruct(shape, dtype)


def body(tokens, cotangent, gates, routes, w_in, w_out):
    experts = lax.axis_size("dp")
    cuts = lax.axis_size("cuts")
    peers = cuts // HALVES
    classes = peers // 2
    side = classes // 2
    tok_rows, width = tokens.shape
    chosen = routes.shape[1]
    cap = 3 * chosen * tok_rows // (2 * experts)
    used = cap // HALVES
    rows = experts * used
    all_rows = 4 * rows
    model = width * cuts
    near, far = pltpu.VMEM, pltpu.HBM
    dma = pltpu.SemaphoreType.DMA
    swap = [(c, (c + peers) % cuts) for c in range(cuts)]
    up = [(c, c // peers * peers + (c + 1) % peers) for c in range(cuts)]
    down = [(d, c) for c, d in up]
    spread = [
        [d * cuts + h * peers + y for y in range(odd, peers, 2) for d in range(experts) for h in range(HALVES)]
        for odd in range(2)
    ]

    def to_partner(value):
        return lax.ppermute(value, "cuts", swap)

    def over_spread(value):
        pieces = value.reshape(classes * all_rows // FOUR, FOUR, width)
        pieces = lax.all_to_all(pieces, ("dp", "cuts"), 0, 0, tiled=True, axis_index_groups=spread)
        return pieces.reshape(classes, all_rows, width)

    in_own, out_own = w_in[0], w_out[0]
    hidden = in_own.shape[1]
    cut = hidden // 4
    in_other, out_head = to_partner(in_own), to_partner(out_own[:cut])
    routes_t, gates_t = routes.T, gates.T
    odd = (lax.axis_index("cuts") % 2).astype(jnp.int32).reshape(1)

    sent, places = call(
        functools.partial(place_kernel, experts, cap),
        (struct(classes, all_rows, width), struct(chosen, tok_rows, dtype=jnp.int32)),
        (4 * all_rows * tok_rows * width, 4 * classes * all_rows * width),
        ([far] * 4, [far, near]),
        56,
        [
            pltpu.VMEM((chosen, tok_rows), jnp.int32),
            pltpu.VMEM((chosen, tok_rows), F32),
            pltpu.VMEM((tok_rows, width), BF16),
            pltpu.VMEM((tok_rows, width), BF16),
            pltpu.VMEM((all_rows, width), BF16),
            dma((4,)),
            dma((classes,)),
        ],
        routes_t,
        gates_t,
        tokens,
        cotangent,
    )
    recv = over_spread(sent)
    recv, in_other, out_head, out_own_late = lax.optimization_barrier(
        (recv, in_other, out_head, out_own)
    )
    low = lax.ppermute(recv[:side], "cuts", up)
    high = lax.ppermute(recv[side:], "cuts", down)
    out_tail = to_partner(out_own_late[cut:])
    ret_own, ret_low, ret_high, held_x, held_g, active, dpre = call(
        functools.partial(expert_kernel, used),
        (
            struct(classes, all_rows, width),
            struct(side, all_rows, width),
            struct(classes - side, all_rows, width),
            struct(rows, model),
            struct(rows, model),
            struct(2, rows, hidden),
            struct(2, rows, hidden),
        ),
        (16 * rows * model * hidden, 12 * rows * model + 8 * model * hidden),
        ([pltpu.SMEM] + [far] * 8, [far] * 5 + [near] * 2),
        60,
        [
            pltpu.VMEM((all_rows, peers * width), BF16),
            pltpu.VMEM((all_rows, all_rows), BF16),
            pltpu.VMEM((all_rows, all_rows), BF16),
            pltpu.VMEM((rows, model), BF16),
            pltpu.VMEM((rows, model), BF16),
            pltpu.VMEM((model, hidden), BF16),
            pltpu.VMEM((model, hidden), BF16),
            pltpu.VMEM((hidden, model), BF16),
            pltpu.VMEM((hidden, model), BF16),
            pltpu.VMEM((all_rows, 2 * width), BF16),
            pltpu.VMEM((all_rows, peers * width), BF16),
            dma((peers,)),
            dma((5,)),
            dma((peers,)),
            dma((2,)),
        ],
        odd,
        recv,
        low,
        high,
        in_own,
        in_other,
        out_own,
        out_head,
        out_tail,
    )
    from_low = lax.ppermute(ret_low, "cuts", up)
    from_high = lax.ppermute(ret_high, "cuts", down)
    over_rows = ((0,), (0,))
    sent_in = to_partner(dot(held_x, dpre[1], over_rows).astype(BF16))
    sent_out = to_partner(dot(active[1], held_g, over_rows).astype(BF16))
    summed = call(
        add_kernel,
        (struct(classes, all_rows, width),),
        (classes * all_rows * width, 6 * classes * all_rows * width),
        ([near] * 3, [near]),
        16,
        [],
        ret_own,
        from_low,
        from_high,
    )[0]
    home = over_spread(summed)
    grad_in = (dot(held_x, dpre[0], over_rows) + sent_in.astype(F32)).astype(BF16)[None]
    grad_out = (dot(active[0], held_g, over_rows) + sent_out.astype(F32)).astype(BF16)[None]
    mixed, token_grad = call(
        functools.partial(combine_kernel, used),
        (struct(tok_rows, width), struct(tok_rows, width)),
        (6 * classes * all_rows * tok_rows * width, 2 * classes * all_rows * width),
        ([near] * 3, [near] * 2),
        16,
        [],
        places,
        gates_t,
        home,
    )
    return (mixed, token_grad, grad_in, grad_out)


def solution(mesh):
    in_specs = (
        P("dp", "cuts"),
        P("dp", "cuts"),
        P("dp", None),
        P("dp", None),
        P("dp", None, "cuts"),
        P("dp", "cuts", None),
    )
    out_specs = (P("dp", "cuts"), P("dp", "cuts"), P("dp", None, "cuts"), P("dp", "cuts", None))
    return jax.shard_map(body, mesh=mesh, in_specs=in_specs, out_specs=out_specs, check_vma=False)
```

time: 159 us -> 195 us (1.23)
  starting transfers between devices: 31.8 us -> 69.1 us
  blocking collectives: 27.8 us -> 0 us
  waiting for transfers between devices: 72.8 us -> 99.5 us
  matrix products: 8.25 us -> 3.84 us
  Pallas kernels: 12.8 us -> 17.2 us
    ppermute x5, waiting for transfers between devices: 27.6 us -> 82.3 us  [to_partner(): return lax.ppermute(value, 'cuts', swap)]
    all_to_all x3 -> x2, waiting for transfers between devices: 45.2 us -> 0.01 us  [over_spread(): lax.all_to_all(pieces, ('dp', 'cuts'), 0, 0, tiled=True, axis_index_group...]
    all_to_all x1 -> x0, blocking collectives: 27.8 us -> none  [over_plane(): lax.all_to_all(value, ('dp', 'cuts'), 0, 0, tiled=True, axis_index_groups...]
    all_to_all x3 -> x2, starting transfers between devices: 17.3 us -> 40.9 us  [over_spread(): lax.all_to_all(pieces, ('dp', 'cuts'), 0, 0, tiled=True, axis_index_group...]
    ppermute x0 -> x4, waiting for transfers between devices: none -> 17.2 us  [the longest x1 5.48 us: body(): high = lax.ppermute(recv[side:], 'cuts', down)]
    ppermute x0 -> x4, starting transfers between devices: none -> 14.1 us  [the longest x1 5.54 us: body(): high = lax.ppermute(recv[side:], 'cuts', down)]
    dot_general x4, matrix products: 8.25 us -> 3.84 us  [dot(): lax.dot_general(left, right, (dims, ((), ())), preferred_element_type=F32)]
    pallas_call x5 -> x4, Pallas kernels: 12.8 us -> 17.2 us  [call(): pl.pallas_call(kernel, out_shape=shapes, in_specs=[pl.BlockSpec(memory_sp...]
  transfers between devices with their start and end apart: 8 -> 11, of which waited for: 5 -> 7; matrix products, arithmetic and copies ran while one was open for 6% -> 2% of each run, Pallas kernels for 3% -> 0%
where the time goes in v4:
time: 195 us; the launch traced here: 194 us
  waiting for transfers between devices  99.5 us (51%)
  starting transfers between devices  69.1 us (35%)
  Pallas kernels  17.2 us (9%)
  matrix products  3.84 us (2%)
  local copies, waits for them, and re-layouts  3.02 us (2%)
    ppermute x5, waiting for transfers between devices, to_partner(): return lax.ppermute(value, 'cuts', swap)  82.3 us
    all_to_all x2, starting transfers between devices, over_spread(): lax.all_to_all(pieces, ('dp', 'cuts'), 0, 0, tiled=True, axis_index_group...  40.9 us
    pallas_call x4, Pallas kernels, call(): pl.pallas_call(kernel, out_shape=shapes, in_specs=[pl.BlockSpec(memory_sp...  17.2 us
    ppermute x5, starting transfers between devices, to_partner(): return lax.ppermute(value, 'cuts', swap)  14 us
    ppermute x1, starting transfers between devices, body(): high = lax.ppermute(recv[side:], 'cuts', down)  5.54 us
    ppermute x1, waiting for transfers between devices, body(): high = lax.ppermute(recv[side:], 'cuts', down)  5.48 us
    ppermute x1, waiting for transfers between devices, body(): from_low = lax.ppermute(ret_low, 'cuts', up)  5.42 us
    ppermute x1, waiting for transfers between devices, body(): low = lax.ppermute(recv[:side], 'cuts', up)  5.04 us
  transfers between devices with their start and end apart: 11, of which 7 were waited for; matrix products, arithmetic and copies ran while one was open for 2% of the time, Pallas kernels for 0%

profile of v4, /device:TPU:1, one launch (start us, length us, event | category | flops | bytes accessed | tf_op | source)
XLA Modules:
  0.0 193.6 jit_solution(9135245540866473352)
XLA Ops:
  0.6 3.1 %shard_map.93 = (bf16[4,768,128]{2,1,0:T(8,128)(2,1)}, s32[2,128]{1,0:T(2,128)}) custom-call(s32[2,128]{1,0:T(2,128)} %bitcast.41, f32[2,128]{1,0:T(2,128)} %bitcast.32, bf16[128,128]{1,0:T(8,128)(2,1)} %tok_in.1, bf16[128,128]{1,0:T(8,128)(2,1)} %cot_in.1), custom_call_target="tpu_custom_call" | custom-call | flops 50331648 | bytes 1572864 | tf_op jit(solution)/shard_map/pallas_call | solution.py:230
  3.7 22.4 %all-to-all-start = ((bf16[768,4,128]{2,1,0:T(4,128)(2,1)}), bf16[768,4,128]{2,1,0:T(4,128)(2,1)S(1)}, u32[]{:S(2)}, u32[]{:S(2)}) async-start(bf16[768,4,128]{2,1,0:T(4,128)(2,1)} %bitcast.38), calls=%async_computation | async-start | bytes 1572864 | tf_op jit(solution)/shard_map/all_to_all | solution.py:273
  26.1 3.3 %collective-permute-start = (bf16[2048,256]{1,0:T(8,128)(2,1)}, bf16[2048,256]{1,0:T(8,128)(2,1)}, u32[]{:S(2)}, u32[]{:S(2)}) collective-permute-start(bf16[2048,256]{1,0:T(8,128)(2,1)} %bitcast.39), channel_id=1, source_target_pairs={{0,8},{1,9},{2,10},{3,11},{4,12},{5,13},{6,14},{7,15},{8,0},{9,1},... | collective-permute-start | bytes 3145736 | tf_op jit(solution)/shard_map/ppermute | solution.py:269
  29.5 2.0 %collective-permute-start.1 = (bf16[64,2048]{1,0:T(8,128)(2,1)S(1)}, bf16[64,2048]{1,0:T(8,128)(2,1)S(1)}, u32[]{:S(2)}, u32[]{:S(2)}) collective-permute-start(bf16[64,2048]{1,0:T(8,128)(2,1)S(1)} %slice_bitcast_fusion), channel_id=1, source_target_pairs={{0,8},{1,9},{2,10},{3,11},{4,12},{5,13},{6,14},{7,15},{8,0},{9,1},... | collective-permute-start | bytes 786440 | tf_op jit(solution)/shard_map/ppermute | solution.py:269
  31.5 33.9 %collective-permute-done.1.out_head = bf16[64,2048]{1,0:T(8,128)(2,1)S(1)} collective-permute-done((bf16[64,2048]{1,0:T(8,128)(2,1)S(1)}, bf16[64,2048]{1,0:T(8,128)(2,1)S(1)}, u32[]{:S(2)}, u32[]{:S(2)}) %collective-permute-start.1) | collective-permute-done | bytes 262176 | tf_op jit(solution)/shard_map/ppermute | solution.py:269
  65.3 0.7 copy-done.12
  66.1 0.1 slice.31
  66.1 3.5 %collective-permute-start.4 = (bf16[192,2048]{1,0:T(8,128)(2,1)S(1)}, bf16[192,2048]{1,0:T(8,128)(2,1)S(1)}, u32[]{:S(2)}, u32[]{:S(2)}) collective-permute-start(bf16[192,2048]{1,0:T(8,128)(2,1)S(1)} %slice.31), channel_id=1, source_target_pairs={{0,8},{1,9},{2,10},{3,11},{4,12},{5,13},{6,14},{7,15},{8,0},{9,1},... | collective-permute-start | bytes 2359304 | tf_op jit(solution)/shard_map/ppermute | solution.py:269
  69.6 0.1 fusion.12
  69.7 5.5 %collective-permute-start.3 = (bf16[2,768,128]{2,1,0:T(8,128)(2,1)S(1)}, bf16[2,768,128]{2,1,0:T(8,128)(2,1)S(1)}, u32[]{:S(2)}, u32[]{:S(2)}) collective-permute-start(bf16[2,768,128]{2,1,0:T(8,128)(2,1)S(1)} %get-tuple-element.34), channel_id=1, source_target_pairs={{1,0},{2,1},{3,2},{4,3},{5,4},{6,5},{7,6},{0,7},{9,8},{10,9},{11,1... | collective-permute-start | bytes 1179656 | tf_op jit(solution)/shard_map/ppermute | solution.py:308
  75.2 1.9 collective-permute-start.2
  77.2 5.5 %collective-permute-done.3.high = bf16[2,768,128]{2,1,0:T(8,128)(2,1)S(1)} collective-permute-done((bf16[2,768,128]{2,1,0:T(8,128)(2,1)S(1)}, bf16[2,768,128]{2,1,0:T(8,128)(2,1)S(1)}, u32[]{:S(2)}, u32[]{:S(2)}) %collective-permute-start.3) | collective-permute-done | bytes 393248 | tf_op jit(solution)/shard_map/ppermute | solution.py:308
  82.7 5.0 %collective-permute-done.2.low = bf16[2,768,128]{2,1,0:T(8,128)(2,1)S(1)} collective-permute-done((bf16[2,768,128]{2,1,0:T(8,128)(2,1)S(1)}, bf16[2,768,128]{2,1,0:T(8,128)(2,1)S(1)}, u32[]{:S(2)}, u32[]{:S(2)}) %collective-permute-start.2) | collective-permute-done | bytes 393248 | tf_op jit(solution)/shard_map/ppermute | solution.py:307
  87.7 0.7 copy-done.11
  88.4 0.3 copy-done.9
  88.7 11.6 %shard_map.94 = (bf16[4,768,128]{2,1,0:T(8,128)(2,1)}, bf16[2,768,128]{2,1,0:T(8,128)(2,1)}, bf16[2,768,128]{2,1,0:T(8,128)(2,1)}, bf16[192,2048]{1,0:T(8,128)(2...) custom-call(s32[1]{0:T(128)} %bitcast.2.odd_ref, ...), custom_call_target="tpu_custom_call" | custom-call | flops 1610612736 | bytes 8912896 | tf_op jit(solution)/shard_map/pallas_call | solution.py:230
  100.3 1.9 collective-permute-start.5
  102.2 4.8 %collective-permute-start.6 = (bf16[2,768,128]{2,1,0:T(8,128)(2,1)}, bf16[2,768,128]{2,1,0:T(8,128)(2,1)S(1)}, u32[]{:S(2)}, u32[]{:S(2)}) collective-permute-start(bf16[2,768,128]{2,1,0:T(8,128)(2,1)} %get-tuple-element.27), channel_id=1, source_target_pairs={{1,0},{2,1},{3,2},{4,3},{5,4},{6,5},{7,6},{0,7},{9,8},{10,9},{11,1... | collective-permute-start | bytes 1179656 | tf_op jit(solution)/shard_map/ppermute | solution.py:352
  107.0 5.4 %collective-permute-done.5.low_ref = bf16[2,768,128]{2,1,0:T(8,128)(2,1)S(1)} collective-permute-done((bf16[2,768,128]{2,1,0:T(8,128)(2,1)}, bf16[2,768,128]{2,1,0:T(8,128)(2,1)S(1)}, u32[]{:S(2)}, u32[]{:S(2)}) %collective-permute-start.5) | collective-permute-done | bytes 393248 | tf_op jit(solution)/shard_map/ppermute | solution.py:351
  112.4 1.3 collective-permute-done.6.high_ref
  113.7 1.1 copy-done
  114.8 1.1 shard_map.95
  115.9 18.5 %all-to-all-start.1 = ((bf16[768,4,128]{2,1,0:T(4,128)(2,1)}), bf16[768,4,128]{2,1,0:T(4,128)(2,1)S(1)}, u32[]{:S(2)}, u32[]{:S(2)}) async-start(bf16[768,4,128]{2,1,0:T(4,128)(2,1)} %bitcast.8), calls=%async_computation.1 | async-start | bytes 1572864 | tf_op jit(solution)/shard_map/all_to_all | solution.py:273
  134.5 0.5 convolution_convert_fusion
  134.9 3.3 %collective-permute-start.8 = (bf16[256,2048]{1,0:T(8,128)(2,1)S(1)}, bf16[256,2048]{1,0:T(8,128)(2,1)S(1)}, u32[]{:S(2)}, u32[]{:S(2)}) collective-permute-start(bf16[256,2048]{1,0:T(8,128)(2,1)S(1)} %convolution_convert_fusion), channel_id=1, source_target_pairs={{0,8},{1,9},{2,10},{3,11},{4,12},{5,13},{6,14},{7,15},{8,0},{9,1},... | collective-permute-start | bytes 3145736 | tf_op jit(solution)/shard_map/ppermute | solution.py:269
  138.2 0.5 convolution_convert_fusion.1
  138.7 2.0 %collective-permute-start.7 = (bf16[2048,256]{1,0:T(8,128)(2,1)S(1)}, bf16[2048,256]{1,0:T(8,128)(2,1)S(1)}, u32[]{:S(2)}, u32[]{:S(2)}) collective-permute-start(bf16[2048,256]{1,0:T(8,128)(2,1)S(1)} %convolution_convert_fusion.1), channel_id=1, source_target_pairs={{0,8},{1,9},{2,10},{3,11},{4,12},{5,13},{6,14},{7,15},{8,0},{9,1},... | collective-permute-start | bytes 3145736 | tf_op jit(solution)/shard_map/ppermute | solution.py:269
  140.7 27.4 %collective-permute-done.8 = bf16[256,2048]{1,0:T(8,128)(2,1)S(1)} collective-permute-done((bf16[256,2048]{1,0:T(8,128)(2,1)S(1)}, bf16[256,2048]{1,0:T(8,128)(2,1)S(1)}, u32[]{:S(2)}, u32[]{:S(2)}) %collective-permute-start.8) | collective-permute-done | bytes 1048608 | tf_op jit(solution)/shard_map/ppermute | solution.py:269
  168.2 1.4 fusion.2
  169.6 21.0 %collective-permute-done.7 = bf16[2048,256]{1,0:T(8,128)(2,1)S(1)} collective-permute-done((bf16[2048,256]{1,0:T(8,128)(2,1)S(1)}, bf16[2048,256]{1,0:T(8,128)(2,1)S(1)}, u32[]{:S(2)}, u32[]{:S(2)}) %collective-permute-start.7) | collective-permute-done | bytes 1048608 | tf_op jit(solution)/shard_map/ppermute | solution.py:269
  190.6 1.5 fusion.3
  192.1 1.5 shard_map.96
  (27 shorter events, 0.1 us)
Async XLA Ops:
  0.6 28.8 %copy-start.6 = (bf16[1,256,2048]{2,1,0:T(8,128)(2,1)S(1)}, bf16[1,256,2048]{2,1,0:T(8,128)(2,1)}, u32[]{:S(2)}) copy-start(bf16[1,256,2048]{2,1,0:T(8,128)(2,1)} %param.11) | copy-start | bytes 3145732
  3.7 62.3 %all-to-all-start = ((bf16[768,4,128]{2,1,0:T(4,128)(2,1)}), bf16[768,4,128]{2,1,0:T(4,128)(2,1)S(1)}, u32[]{:S(2)}, u32[]{:S(2)}) async-start(bf16[768,4,128]{2,1,0:T(4,128)(2,1)} %bitcast.38), calls=%async_computation | async-start | bytes 1572864 | tf_op jit(solution)/shard_map/all_to_all | solution.py:273
  26.1 39.9 %collective-permute-start = (bf16[2048,256]{1,0:T(8,128)(2,1)}, bf16[2048,256]{1,0:T(8,128)(2,1)}, u32[]{:S(2)}, u32[]{:S(2)}) collective-permute-start(bf16[2048,256]{1,0:T(8,128)(2,1)} %bitcast.39), channel_id=1, source_target_pairs={{0,8},{1,9},{2,10},{3,11},{4,12},{5,13},{6,14},{7,15},{8,0},{9,1},... | collective-permute-start | bytes 3145736 | tf_op jit(solution)/shard_map/ppermute | solution.py:269
  29.5 35.9 %collective-permute-start.1 = (bf16[64,2048]{1,0:T(8,128)(2,1)S(1)}, bf16[64,2048]{1,0:T(8,128)(2,1)S(1)}, u32[]{:S(2)}, u32[]{:S(2)}) collective-permute-start(bf16[64,2048]{1,0:T(8,128)(2,1)S(1)} %slice_bitcast_fusion), channel_id=1, source_target_pairs={{0,8},{1,9},{2,10},{3,11},{4,12},{5,13},{6,14},{7,15},{8,0},{9,1},... | collective-permute-start | bytes 786440 | tf_op jit(solution)/shard_map/ppermute | solution.py:269
  65.3 0.7 copy-start.12
  66.1 3.6 %copy-start.3 = (bf16[768,4,128]{2,1,0:T(4,128)(2,1)}, bf16[768,4,128]{2,1,0:T(4,128)(2,1)S(1)}, u32[]{:S(2)}) copy-start(bf16[768,4,128]{2,1,0:T(4,128)(2,1)S(1)} %all-to-all-done) | copy-start | bytes 2359300
  66.1 21.6 %collective-permute-start.4 = (bf16[192,2048]{1,0:T(8,128)(2,1)S(1)}, bf16[192,2048]{1,0:T(8,128)(2,1)S(1)}, u32[]{:S(2)}, u32[]{:S(2)}) collective-permute-start(bf16[192,2048]{1,0:T(8,128)(2,1)S(1)} %slice.31), channel_id=1, source_target_pairs={{0,8},{1,9},{2,10},{3,11},{4,12},{5,13},{6,14},{7,15},{8,0},{9,1},... | collective-permute-start | bytes 2359304 | tf_op jit(solution)/shard_map/ppermute | solution.py:269
  69.7 13.0 %collective-permute-start.3 = (bf16[2,768,128]{2,1,0:T(8,128)(2,1)S(1)}, bf16[2,768,128]{2,1,0:T(8,128)(2,1)S(1)}, u32[]{:S(2)}, u32[]{:S(2)}) collective-permute-start(bf16[2,768,128]{2,1,0:T(8,128)(2,1)S(1)} %get-tuple-element.34), channel_id=1, source_target_pairs={{1,0},{2,1},{3,2},{4,3},{5,4},{6,5},{7,6},{0,7},{9,8},{10,9},{11,1... | collective-permute-start | bytes 1179656 | tf_op jit(solution)/shard_map/ppermute | solution.py:308
  75.2 12.5 %collective-permute-start.2 = (bf16[2,768,128]{2,1,0:T(8,128)(2,1)S(1)}, bf16[2,768,128]{2,1,0:T(8,128)(2,1)S(1)}, u32[]{:S(2)}, u32[]{:S(2)}) collective-permute-start(bf16[2,768,128]{2,1,0:T(8,128)(2,1)S(1)} %get-tuple-element.35), channel_id=1, source_target_pairs={{0,1},{1,2},{2,3},{3,4},{4,5},{5,6},{6,7},{7,0},{8,9},{9,10},{10,1... | collective-permute-start | bytes 1179656 | tf_op jit(solution)/shard_map/ppermute | solution.py:307
  82.6 5.1 %copy-start.10 = (bf16[2,768,128]{2,1,0:T(8,128)(2,1)}, bf16[2,768,128]{2,1,0:T(8,128)(2,1)S(1)}, u32[]{:S(2)}) copy-start(bf16[2,768,128]{2,1,0:T(8,128)(2,1)S(1)} %collective-permute-done.3.high) | copy-start | bytes 1179652
  87.7 0.8 copy-start.11
  87.7 1.0 copy-start.9
  100.3 12.1 %collective-permute-start.5 = (bf16[2,768,128]{2,1,0:T(8,128)(2,1)}, bf16[2,768,128]{2,1,0:T(8,128)(2,1)S(1)}, u32[]{:S(2)}, u32[]{:S(2)}) collective-permute-start(bf16[2,768,128]{2,1,0:T(8,128)(2,1)} %get-tuple-element.26), channel_id=1, source_target_pairs={{0,1},{1,2},{2,3},{3,4},{4,5},{5,6},{6,7},{7,0},{8,9},{9,10},{10,1... | collective-permute-start | bytes 1179656 | tf_op jit(solution)/shard_map/ppermute | solution.py:351
  102.2 11.5 %collective-permute-start.6 = (bf16[2,768,128]{2,1,0:T(8,128)(2,1)}, bf16[2,768,128]{2,1,0:T(8,128)(2,1)S(1)}, u32[]{:S(2)}, u32[]{:S(2)}) collective-permute-start(bf16[2,768,128]{2,1,0:T(8,128)(2,1)} %get-tuple-element.27), channel_id=1, source_target_pairs={{1,0},{2,1},{3,2},{4,3},{5,4},{6,5},{7,6},{0,7},{9,8},{10,9},{11,1... | collective-permute-start | bytes 1179656 | tf_op jit(solution)/shard_map/ppermute | solution.py:352
  113.7 1.1 copy-start
  115.9 18.6 %copy-start.5 = (bf16[192,2048]{1,0:T(8,128)(2,1)S(1)}, bf16[192,2048]{1,0:T(8,128)(2,1)}, u32[]{:S(2)}) copy-start(bf16[192,2048]{1,0:T(8,128)(2,1)} %get-tuple-element.33) | copy-start | bytes 2359300
  115.9 18.6 %copy-start.8 = (bf16[2,192,256]{2,1,0:T(8,128)(2,1)S(1)}, bf16[2,192,256]{2,1,0:T(8,128)(2,1)}, u32[]{:S(2)}) copy-start(bf16[2,192,256]{2,1,0:T(8,128)(2,1)} %get-tuple-element.32) | copy-start | bytes 589828
  115.9 76.2 %all-to-all-start.1 = ((bf16[768,4,128]{2,1,0:T(4,128)(2,1)}), bf16[768,4,128]{2,1,0:T(4,128)(2,1)S(1)}, u32[]{:S(2)}, u32[]{:S(2)}) async-start(bf16[768,4,128]{2,1,0:T(4,128)(2,1)} %bitcast.8), calls=%async_computation.1 | async-start | bytes 1572864 | tf_op jit(solution)/shard_map/all_to_all | solution.py:273
  134.4 3.8 %copy-start.4 = (bf16[192,2048]{1,0:T(8,128)(2,1)S(1)}, bf16[192,2048]{1,0:T(8,128)(2,1)}, u32[]{:S(2)}) copy-start(bf16[192,2048]{1,0:T(8,128)(2,1)} %get-tuple-element.30) | copy-start | bytes 2359300
  134.4 3.8 %copy-start.7 = (bf16[2,192,256]{2,1,0:T(8,128)(2,1)S(1)}, bf16[2,192,256]{2,1,0:T(8,128)(2,1)}, u32[]{:S(2)}) copy-start(bf16[2,192,256]{2,1,0:T(8,128)(2,1)} %get-tuple-element.31) | copy-start | bytes 589828
  134.9 33.3 %collective-permute-start.8 = (bf16[256,2048]{1,0:T(8,128)(2,1)S(1)}, bf16[256,2048]{1,0:T(8,128)(2,1)S(1)}, u32[]{:S(2)}, u32[]{:S(2)}) collective-permute-start(bf16[256,2048]{1,0:T(8,128)(2,1)S(1)} %convolution_convert_fusion), channel_id=1, source_target_pairs={{0,8},{1,9},{2,10},{3,11},{4,12},{5,13},{6,14},{7,15},{8,0},{9,1},... | collective-permute-start | bytes 3145736 | tf_op jit(solution)/shard_map/ppermute | solution.py:269
  138.7 51.9 %collective-permute-start.7 = (bf16[2048,256]{1,0:T(8,128)(2,1)S(1)}, bf16[2048,256]{1,0:T(8,128)(2,1)S(1)}, u32[]{:S(2)}, u32[]{:S(2)}) collective-permute-start(bf16[2048,256]{1,0:T(8,128)(2,1)S(1)} %convolution_convert_fusion.1), channel_id=1, source_target_pairs={{0,8},{1,9},{2,10},{3,11},{4,12},{5,13},{6,14},{7,15},{8,0},{9,1},... | collective-permute-start | bytes 3145736 | tf_op jit(solution)/shard_map/ppermute | solution.py:269
  169.6 22.5 %copy-start.1 = (f32[128,2]{0,1:T(2,128)S(1)}, f32[128,2]{0,1:T(2,128)}, u32[]{:S(2)}) copy-start(f32[128,2]{0,1:T(2,128)} %param.8) | copy-start | bytes 3076
  169.6 22.5 %copy-start.2 = (s32[2,128]{1,0:T(2,128)S(1)}, s32[2,128]{1,0:T(2,128)}, u32[]{:S(2)}) copy-start(s32[2,128]{1,0:T(2,128)} %get-tuple-element.19.rows_ref) | copy-start | bytes 3076

commit v5 on v4

--- a/solution.py
+++ b/solution.py
@@ -11,6 +11,7 @@
 BF16 = jnp.bfloat16
 F32 = jnp.float32
 HALVES = 2
+EARLY = (1, 2)
 FOUR = 4
 
 
@@ -37,9 +38,29 @@
     return jnp.where(hit, 1.0, 0.0).astype(BF16)
 
 
-def place_kernel(experts, cap, routes_in, gates_in, tok_in, cot_in, sent, rows_ref, *scratch):
-    routes_ref, gates_ref, tok_ref, cot_ref, held_ref, sems, sent_sems = scratch
-    tok_rows = tok_in.shape[0]
+def weight_blocks(hidden, model, width):
+    blocks = [(0, at, model) for at in range(0, hidden, width)]
+    return blocks + [(1, at, hidden) for at in range(0, model, width)]
+
+
+def split_blocks(hidden, model, width):
+    blocks = weight_blocks(hidden, model, width)
+    count = hidden // width + model // width * EARLY[0] // EARLY[1]
+    parts = []
+    for part in (blocks[:count], blocks[count:]):
+        at, placed = 0, []
+        for which, first, rows in part:
+            placed.append((which, first, at, rows))
+            at += rows
+        parts.append((placed, at))
+    return parts
+
+
+def place_kernel(experts, cap, routes_in, gates_in, tok_in, cot_in, in_own, out_own, *refs):
+    sent, rows_ref, early, late = refs[:4]
+    scratch = refs[4:]
+    routes_ref, gates_ref, tok_ref, cot_ref, held_ref, sems, sent_sems, weight_sems = scratch
+    tok_rows, width = tok_in.shape
     copies = [
         pltpu.make_async_copy(routes_in, routes_ref, sems.at[0]),
         pltpu.make_async_copy(gates_in, gates_ref, sems.at[1]),
@@ -48,6 +69,16 @@
     ]
     for copy in copies:
         copy.start()
+    weights = []
+    for (placed, _), out in zip(split_blocks(*reversed(in_own.shape), width), (early, late)):
+        for which, first, at, rows in placed:
+            source = (in_own, out_own)[which].at[:, pl.ds(first, width)]
+            weights.append(
+                pltpu.make_async_copy(
+                    source, out.at[pl.ds(at, rows), :], weight_sems.at[len(weights)]
+                )
+            )
+            weights[-1].start()
     copies[0].wait()
     routes = routes_ref[...]
     first, second = routes[0:1, :], routes[1:2, :]
@@ -87,7 +118,7 @@
     ]
     for copy in copies:
         copy.start()
-    for copy in copies:
+    for copy in copies + weights:
         copy.wait()
 
 
@@ -100,7 +131,7 @@
     return block * (sources * used) + source * used + inner - block * used
 
 
-def expert_kernel(used, odd_ref, own, low, high, in_own, in_other, out_own, out_head, out_tail, *rest):
+def expert_kernel(used, odd_ref, own, low, high, in_own, out_own, early, late, *rest):
     ret_own, ret_low, ret_high, x_out, g_out, act_ref, dpre_ref = rest[:7]
     recv_ref, pick_ref, spread_ref, x_ref, g_ref, in0, in1, out0, out1, held_ref, ret_ref = rest[7:18]
     recv_sems, weight_sems, ret_sems, kept_sems = rest[18:]
@@ -109,7 +140,6 @@
     rows = all_rows // 4
     sources = rows // used
     side = classes // 2
-    cut = out_head.shape[0]
     odd = odd_ref[0]
 
     def columns(index, other):
@@ -123,20 +153,18 @@
         pltpu.make_async_copy(ref.at[q], recv_ref.at[:, cols], recv_sems.at[index])
         for index, (ref, q, cols) in enumerate(moves)
     ]
-    load_in = [
-        pltpu.make_async_copy(in_own, in0, weight_sems.at[0]),
-        pltpu.make_async_copy(in_other, in1, weight_sems.at[1]),
-    ]
-    load_out = [
-        [pltpu.make_async_copy(out_own, out0, weight_sems.at[2])],
-        [
-            pltpu.make_async_copy(out_head, out1.at[pl.ds(0, cut), :], weight_sems.at[3]),
-            pltpu.make_async_copy(
-                out_tail, out1.at[pl.ds(cut, out1.shape[0] - cut), :], weight_sems.at[4]
-            ),
-        ],
-    ]
-    for copy in arrive + load_in + load_out[0] + load_out[1]:
+    load_in = [[pltpu.make_async_copy(in_own, in0, weight_sems.at[0])], []]
+    load_out = [[pltpu.make_async_copy(out_own, out0, weight_sems.at[1])], []]
+    for (placed, _), source in zip(split_blocks(*reversed(in0.shape), width), (early, late)):
+        for which, first, at, size in placed:
+            target = (in1, out1)[which].at[:, pl.ds(first, width)]
+            index = 2 + len(load_in[1]) + len(load_out[1])
+            (load_in, load_out)[which][1].append(
+                pltpu.make_async_copy(
+                    source.at[pl.ds(at, size), :], target, weight_sems.at[index]
+                )
+            )
+    for copy in arrive + load_in[0] + load_in[1] + load_out[0] + load_out[1]:
         copy.start()
     shape = (all_rows, all_rows)
     pick_ref[...] = mask(iota(shape, 0) == sorted_row(iota((1, all_rows), 1), used, sources))
@@ -161,7 +189,8 @@
     by_last = ((1,), (1,))
     acts, slopes, dpres = [], [], []
     for group, ref in enumerate((in0, in1)):
-        load_in[group].wait()
+        for copy in load_in[group]:
+            copy.wait()
         value, slope = gelu_parts(dot(x_ref[...], ref[...]))
         acts.append(value.astype(BF16))
         slopes.append(slope)
@@ -171,6 +200,7 @@
             copy.wait()
         dpres.append((dot(g_ref[...], ref[...], by_last) * slopes[group]).astype(BF16))
         dpre_ref[group] = dpres[group]
+    leave = []
     for pair in range(classes):
         for part in range(HALVES):
             at = (part * peers + 2 * pair) * width
@@ -183,17 +213,57 @@
         ret_ref[:, pair * 2 * width : (pair + 1) * 2 * width] = dot(
             spread_ref[...], held_ref[...]
         ).astype(BF16)
-    moves = [(ret_own, q, columns(q, False)) for q in range(classes)]
-    moves += [(ret_low, q, columns(q, True)) for q in range(side)]
-    moves += [(ret_high, q, columns(q + side, True)) for q in range(side)]
-    leave = [
-        pltpu.make_async_copy(ret_ref.at[:, cols], ref.at[q], ret_sems.at[index])
-        for index, (ref, q, cols) in enumerate(moves)
-    ]
-    for copy in leave:
-        copy.start()
+        other = ret_low.at[pair] if pair < side else ret_high.at[pair - side]
+        leave.append(
+            pltpu.make_async_copy(
+                ret_ref.at[:, columns(pair, False)], ret_own.at[pair], ret_sems.at[2 * pair]
+            )
+        )
+        leave.append(
+            pltpu.make_async_copy(
+                ret_ref.at[:, columns(pair, True)], other, ret_sems.at[2 * pair + 1]
+            )
+        )
+        leave[-2].start()
+        leave[-1].start()
     for copy in leave + kept:
         copy.wait()
+
+
+def partner_kernel(x_ref, g_ref, act_ref, dpre_ref, out_ref):
+    over_rows = ((0,), (0,))
+    model = x_ref.shape[1]
+    hidden, width = dpre_ref.shape[2], out_ref.shape[1]
+    for at in range(0, model, hidden):
+        part = dot(x_ref[:, at : at + hidden], dpre_ref[1], over_rows).astype(BF16)
+        for index in range(hidden // width):
+            start = index * model + at
+            out_ref[start : start + hidden, :] = part[:, index * width : (index + 1) * width]
+        part = dot(act_ref[1], g_ref[:, at : at + hidden], over_rows).astype(BF16)
+        for index in range(hidden // width):
+            start = hidden // width * model + (at // width + index) * hidden
+            out_ref[start : start + hidden, :] = part[:, index * width : (index + 1) * width]
+
+
+def gradient_kernel(x_ref, g_ref, act_ref, dpre_ref, sent_ref, grad_in_ref, grad_out_ref):
+    over_rows = ((0,), (0,))
+    model = x_ref.shape[1]
+    hidden, width = dpre_ref.shape[2], sent_ref.shape[1]
+    for at in range(0, model, hidden):
+        part = dot(x_ref[:, at : at + hidden], dpre_ref[0], over_rows)
+        for index in range(hidden // width):
+            start = index * model + at
+            cols = slice(index * width, (index + 1) * width)
+            grad_in_ref[0, at : at + hidden, cols] = (
+                part[:, cols] + sent_ref[start : start + hidden, :].astype(F32)
+            ).astype(BF16)
+        part = dot(act_ref[0], g_ref[:, at : at + hidden], over_rows)
+        for index in range(hidden // width):
+            start = hidden // width * model + (at // width + index) * hidden
+            cols = slice(index * width, (index + 1) * width)
+            grad_out_ref[0, :, at + index * width : at + (index + 1) * width] = (
+                part[:, cols] + sent_ref[start : start + hidden, :].astype(F32)
+            ).astype(BF16)
 
 
 def add_kernel(own_ref, low_ref, high_ref, out_ref):
@@ -275,16 +345,21 @@
 
     in_own, out_own = w_in[0], w_out[0]
     hidden = in_own.shape[1]
-    cut = hidden // 4
-    in_other, out_head = to_partner(in_own), to_partner(out_own[:cut])
+    blocks = hidden // width + cuts
+    early_rows, late_rows = (part[1] for part in split_blocks(hidden, model, width))
     routes_t, gates_t = routes.T, gates.T
     odd = (lax.axis_index("cuts") % 2).astype(jnp.int32).reshape(1)
 
-    sent, places = call(
+    sent, places, early, late = call(
         functools.partial(place_kernel, experts, cap),
-        (struct(classes, all_rows, width), struct(chosen, tok_rows, dtype=jnp.int32)),
+        (
+            struct(classes, all_rows, width),
+            struct(chosen, tok_rows, dtype=jnp.int32),
+            struct(early_rows, width),
+            struct(late_rows, width),
+        ),
         (4 * all_rows * tok_rows * width, 4 * classes * all_rows * width),
-        ([far] * 4, [far, near]),
+        ([far] * 6, [far, near, far, far]),
         56,
         [
             pltpu.VMEM((chosen, tok_rows), jnp.int32),
@@ -294,19 +369,21 @@
             pltpu.VMEM((all_rows, width), BF16),
             dma((4,)),
             dma((classes,)),
+            dma((blocks,)),
         ],
         routes_t,
         gates_t,
         tokens,
         cotangent,
-    )
+        in_own,
+        out_own,
+    )
+    early = to_partner(early)
     recv = over_spread(sent)
-    recv, in_other, out_head, out_own_late = lax.optimization_barrier(
-        (recv, in_other, out_head, out_own)
-    )
+    recv, early, late = lax.optimization_barrier((recv, early, late))
     low = lax.ppermute(recv[:side], "cuts", up)
     high = lax.ppermute(recv[side:], "cuts", down)
-    out_tail = to_partner(out_own_late[cut:])
+    late = to_partner(late)
     ret_own, ret_low, ret_high, held_x, held_g, active, dpre = call(
         functools.partial(expert_kernel, used),
         (
@@ -319,7 +396,7 @@
             struct(2, rows, hidden),
         ),
         (16 * rows * model * hidden, 12 * rows * model + 8 * model * hidden),
-        ([pltpu.SMEM] + [far] * 8, [far] * 5 + [near] * 2),
+        ([pltpu.SMEM] + [far] * 7, [far] * 5 + [near] * 2),
         60,
         [
             pltpu.VMEM((all_rows, peers * width), BF16),
@@ -334,7 +411,7 @@
             pltpu.VMEM((all_rows, 2 * width), BF16),
             pltpu.VMEM((all_rows, peers * width), BF16),
             dma((peers,)),
-            dma((5,)),
+            dma((2 + blocks,)),
             dma((peers,)),
             dma((2,)),
         ],
@@ -343,16 +420,25 @@
         low,
         high,
         in_own,
-        in_other,
         out_own,
-        out_head,
-        out_tail,
+        early,
+        late,
     )
     from_low = lax.ppermute(ret_low, "cuts", up)
     from_high = lax.ppermute(ret_high, "cuts", down)
-    over_rows = ((0,), (0,))
-    sent_in = to_partner(dot(held_x, dpre[1], over_rows).astype(BF16))
-    sent_out = to_partner(dot(active[1], held_g, over_rows).astype(BF16))
+    sent_grads = call(
+        partner_kernel,
+        (struct(early_rows + late_rows, width),),
+        (8 * rows * model * hidden, 8 * model * hidden),
+        ([near] * 4, [near]),
+        24,
+        [],
+        held_x,
+        held_g,
+        active,
+        dpre,
+    )[0]
+    sent_grads = to_partner(sent_grads)
     summed = call(
         add_kernel,
         (struct(classes, all_rows, width),),
@@ -365,8 +451,19 @@
         from_high,
     )[0]
     home = over_spread(summed)
-    grad_in = (dot(held_x, dpre[0], over_rows) + sent_in.astype(F32)).astype(BF16)[None]
-    grad_out = (dot(active[0], held_g, over_rows) + sent_out.astype(F32)).astype(BF16)[None]
+    grad_in, grad_out = call(
+        gradient_kernel,
+        (struct(1, model, hidden), struct(1, hidden, model)),
+        (8 * rows * model * hidden, 16 * model * hidden),
+        ([near] * 5, [near] * 2),
+        32,
+        [],
+        held_x,
+        held_g,
+        active,
+        dpre,
+        sent_grads,
+    )
     mixed, token_grad = call(
         functools.partial(combine_kernel, used),
         (struct(tok_rows, width), struct(tok_rows, width)),

time: 195 us -> 221 us (1.13)
  blocking collectives: 0 us -> 96.6 us
  waiting for transfers between devices: 99.5 us -> 16.4 us
  Pallas kernels: 17.2 us -> 81.4 us
  starting transfers between devices: 69.1 us -> 20.8 us
  matrix products: 3.84 us -> 0 us
    all_to_all x0 -> x2, blocking collectives: none -> 96.6 us  [over_spread(): lax.all_to_all(pieces, ('dp', 'cuts'), 0, 0, tiled=True, axis_index_group...]
    ppermute x5 -> x3, waiting for transfers between devices: 82.3 us -> 0.01 us  [to_partner(): return lax.ppermute(value, 'cuts', swap)]
    pallas_call x4 -> x6, Pallas kernels: 17.2 us -> 81.4 us  [call(): pl.pallas_call(kernel, out_shape=shapes, in_specs=[pl.BlockSpec(memory_sp...]
    all_to_all x2 -> x0, starting transfers between devices: 40.9 us -> none  [over_spread(): lax.all_to_all(pieces, ('dp', 'cuts'), 0, 0, tiled=True, axis_index_group...]
    ppermute x5 -> x3, starting transfers between devices: 14 us -> 8.79 us  [to_partner(): return lax.ppermute(value, 'cuts', swap)]
    dot_general x4 -> x0, matrix products: 3.84 us -> none  [dot(): lax.dot_general(left, right, (dims, ((), ())), preferred_element_type=F32)]
    ppermute x1, starting transfers between devices: 5.54 us -> 1.92 us  [body(): high = lax.ppermute(recv[side:], 'cuts', down)]
  transfers between devices with their start and end apart: 11 -> 7, of which waited for: 7 -> 4; matrix products, arithmetic and copies ran while one was open for 2% -> 0% of each run, Pallas kernels for 0% -> 1%
where the time goes in v5:
time: 221 us; the launch traced here: 220 us
  blocking collectives  96.6 us (44%)
  Pallas kernels  81.4 us (37%)
  starting transfers between devices  20.8 us (9%)
  waiting for transfers between devices  16.4 us (7%)
  local copies, waits for them, and re-layouts  4.21 us (2%)
    all_to_all x2, blocking collectives, over_spread(): lax.all_to_all(pieces, ('dp', 'cuts'), 0, 0, tiled=True, axis_index_group...  96.6 us
    pallas_call x6, Pallas kernels, call(): pl.pallas_call(kernel, out_shape=shapes, in_specs=[pl.BlockSpec(memory_sp...  81.4 us
    ppermute x3, starting transfers between devices, to_partner(): return lax.ppermute(value, 'cuts', swap)  8.79 us
    ppermute x1, waiting for transfers between devices, body(): high = lax.ppermute(recv[side:], 'cuts', down)  6.97 us
    ppermute x1, waiting for transfers between devices, body(): from_low = lax.ppermute(ret_low, 'cuts', up)  5.42 us
    ppermute x1, starting transfers between devices, body(): from_high = lax.ppermute(ret_high, 'cuts', down)  4.57 us
  transfers between devices with their start and end apart: 7, of which 4 were waited for; matrix products, arithmetic and copies ran while one was open for 0% of the time, Pallas kernels for 1%

profile of v5, /device:TPU:1, one launch (start us, length us, event | category | flops | bytes accessed | tf_op | source)
XLA Modules:
  0.0 220.3 jit_solution(10388162268006366035)
XLA Ops:
  0.6 65.4 %shard_map.93 = (bf16[4,768,128]{2,1,0:T(8,128)(2,1)}, s32[2,128]{1,0:T(2,128)}, bf16[6144,128]{1,0:T(8,128)(2,1)}, bf16[2048,128]{1,0:T(8,128)(2,1)}) custom-call(s32[2,128]{1,0:T(2,128)} %bitcast.20, f32[2,128]{1,0:T(2,128)} %bitcast.11, bf16[128,128]{1,0:T(8,128)(2,1)} %tok_in.1, bf16[128,128]{1,0:T(8,128)(2,1)} %cot_in.1, bf16[2048,256]{1,0:T(8,128)(2,1)} %bitcast.15, ...), custom_call_target="tpu_custom_call" | custom-call | flops 50331648 | bytes 1572864 | tf_op jit(solution)/shard_map/pallas_call | solution.py:300
  66.1 3.9 %collective-permute-start = (bf16[6144,128]{1,0:T(8,128)(2,1)}, bf16[6144,128]{1,0:T(8,128)(2,1)S(1)}, u32[]{:S(2)}, u32[]{:S(2)}) collective-permute-start(bf16[6144,128]{1,0:T(8,128)(2,1)} %get-tuple-element.24), channel_id=1, source_target_pairs={{0,8},{1,9},{2,10},{3,11},{4,12},{5,13},{6,14},{7,15},{8,0},{9,1},... | collective-permute-start | bytes 4718600 | tf_op jit(solution)/shard_map/ppermute | solution.py:339
  70.0 50.4 %all_to_all.10 = bf16[768,4,128]{2,1,0:T(4,128)(2,1)S(1)} all-to-all(bf16[768,4,128]{2,1,0:T(4,128)(2,1)} %bitcast.19), channel_id=1, replica_groups={{0,8,16,24,32,40,48,56,64,72,80,88,96,104,112,120,128,136,144,152,160,1..., dimensions={0} | all-to-all | bytes 1572864 | tf_op jit(solution)/shard_map/all_to_all | solution.py:343
  120.4 0.0 collective-permute-done.early
  120.4 2.1 collective-permute-start.3
  122.6 0.1 fusion
  122.6 1.9 collective-permute-start.2
  124.6 3.5 %collective-permute-start.1 = (bf16[2,768,128]{2,1,0:T(8,128)(2,1)S(1)}, bf16[2,768,128]{2,1,0:T(8,128)(2,1)}, u32[]{:S(2)}, u32[]{:S(2)}) collective-permute-start(bf16[2,768,128]{2,1,0:T(8,128)(2,1)S(1)} %get-tuple-element.41), channel_id=1, source_target_pairs={{0,1},{1,2},{2,3},{3,4},{4,5},{5,6},{6,7},{7,0},{8,9},{9,10},{10,1... | collective-permute-start | bytes 1179656 | tf_op jit(solution)/shard_map/ppermute | solution.py:384
  128.1 7.0 %collective-permute-done.2.high = bf16[2,768,128]{2,1,0:T(8,128)(2,1)S(1)} collective-permute-done((bf16[2,768,128]{2,1,0:T(8,128)(2,1)S(1)}, bf16[2,768,128]{2,1,0:T(8,128)(2,1)S(1)}, u32[]{:S(2)}, u32[]{:S(2)}) %collective-permute-start.2) | collective-permute-done | bytes 393248 | tf_op jit(solution)/shard_map/ppermute | solution.py:385
  135.1 3.1 %collective-permute-done.1.low = bf16[2,768,128]{2,1,0:T(8,128)(2,1)} collective-permute-done((bf16[2,768,128]{2,1,0:T(8,128)(2,1)S(1)}, bf16[2,768,128]{2,1,0:T(8,128)(2,1)}, u32[]{:S(2)}, u32[]{:S(2)}) %collective-permute-start.1) | collective-permute-done | bytes 393248 | tf_op jit(solution)/shard_map/ppermute | solution.py:384
  138.2 0.0 collective-permute-done.3.late
  138.2 0.0 copy-done.11
  138.2 11.4 %shard_map.94 = (bf16[4,768,128]{2,1,0:T(8,128)(2,1)}, bf16[2,768,128]{2,1,0:T(8,128)(2,1)}, bf16[2,768,128]{2,1,0:T(8,128)(2,1)}, bf16[192,2048]{1,0:T(8,128)(2...) custom-call(s32[1]{0:T(128)} %bitcast.4.odd_ref, ...), custom_call_target="tpu_custom_call" | custom-call | flops 1610612736 | bytes 8912896 | tf_op jit(solution)/shard_map/pallas_call | solution.py:300
  149.7 1.1 copy-done
  150.8 1.1 copy-done.2
  152.0 0.9 copy-done.4
  152.9 0.9 copy-done.6
  153.8 0.8 shard_map.97
  154.6 0.0 copy-start.9
  154.6 0.0 copy-start.10
  154.6 2.7 %collective-permute-start.6 = (bf16[8192,128]{1,0:T(8,128)(2,1)S(1)}, bf16[8192,128]{1,0:T(8,128)(2,1)S(1)}, u32[]{:S(2)}, u32[]{:S(2)}) collective-permute-start(bf16[8192,128]{1,0:T(8,128)(2,1)S(1)} %shard_map.97), channel_id=1, source_target_pairs={{0,8},{1,9},{2,10},{3,11},{4,12},{5,13},{6,14},{7,15},{8,0},{9,1},... | collective-permute-start | bytes 6291464 | tf_op jit(solution)/shard_map/ppermute | solution.py:339
  157.4 1.9 collective-permute-start.4
  159.3 4.6 %collective-permute-start.5 = (bf16[2,768,128]{2,1,0:T(8,128)(2,1)S(1)}, bf16[2,768,128]{2,1,0:T(8,128)(2,1)S(1)}, u32[]{:S(2)}, u32[]{:S(2)}) collective-permute-start(bf16[2,768,128]{2,1,0:T(8,128)(2,1)S(1)} %copy-done.14), channel_id=1, source_target_pairs={{1,0},{2,1},{3,2},{4,3},{5,4},{6,5},{7,6},{0,7},{9,8},{10,9},{11,1... | collective-permute-start | bytes 1179656 | tf_op jit(solution)/shard_map/ppermute | solution.py:428
  163.9 5.4 %collective-permute-done.4.low_ref = bf16[2,768,128]{2,1,0:T(8,128)(2,1)S(1)} collective-permute-done((bf16[2,768,128]{2,1,0:T(8,128)(2,1)S(1)}, bf16[2,768,128]{2,1,0:T(8,128)(2,1)S(1)}, u32[]{:S(2)}, u32[]{:S(2)}) %collective-permute-start.4) | collective-permute-done | bytes 393248 | tf_op jit(solution)/shard_map/ppermute | solution.py:427
  169.3 0.9 collective-permute-done.5.high_ref
  170.2 0.0 copy-done.8
  170.3 0.0 copy-start.7
  170.3 0.2 shard_map.95
  170.5 46.2 %all_to_all.11 = bf16[768,4,128]{2,1,0:T(4,128)(2,1)S(1)} all-to-all(bf16[768,4,128]{2,1,0:T(4,128)(2,1)S(1)} %bitcast.9), channel_id=1, replica_groups={{0,8,16,24,32,40,48,56,64,72,80,88,96,104,112,120,128,136,144,152,160,1..., dimensions={0} | all-to-all | bytes 1572864 | tf_op jit(solution)/shard_map/all_to_all | solution.py:343
  216.7 1.5 shard_map.96
  218.2 0.0 collective-permute-done.6.sent_ref
  218.2 2.1 shard_map.98
  (23 shorter events, 0.0 us)
Async XLA Ops:
  66.1 54.4 %collective-permute-start = (bf16[6144,128]{1,0:T(8,128)(2,1)}, bf16[6144,128]{1,0:T(8,128)(2,1)S(1)}, u32[]{:S(2)}, u32[]{:S(2)}) collective-permute-start(bf16[6144,128]{1,0:T(8,128)(2,1)} %get-tuple-element.24), channel_id=1, source_target_pairs={{0,8},{1,9},{2,10},{3,11},{4,12},{5,13},{6,14},{7,15},{8,0},{9,1},... | collective-permute-start | bytes 4718600 | tf_op jit(solution)/shard_map/ppermute | solution.py:339
  120.4 17.8 %copy-start.11 = (bf16[768,4,128]{2,1,0:T(4,128)(2,1)}, bf16[768,4,128]{2,1,0:T(4,128)(2,1)S(1)}, u32[]{:S(2)}) copy-start(bf16[768,4,128]{2,1,0:T(4,128)(2,1)S(1)} %all_to_all.10) | copy-start | bytes 2359300
  120.4 17.8 %copy-start.12 = (bf16[6144,128]{1,0:T(8,128)(2,1)}, bf16[6144,128]{1,0:T(8,128)(2,1)S(1)}, u32[]{:S(2)}) copy-start(bf16[6144,128]{1,0:T(8,128)(2,1)S(1)} %collective-permute-done.early) | copy-start | bytes 4718596
  120.4 17.8 %collective-permute-start.3 = (bf16[2048,128]{1,0:T(8,128)(2,1)}, bf16[2048,128]{1,0:T(8,128)(2,1)}, u32[]{:S(2)}, u32[]{:S(2)}) collective-permute-start(bf16[2048,128]{1,0:T(8,128)(2,1)} %get-tuple-element.28), channel_id=1, source_target_pairs={{0,8},{1,9},{2,10},{3,11},{4,12},{5,13},{6,14},{7,15},{8,0},{9,1},... | collective-permute-start | bytes 1572872 | tf_op jit(solution)/shard_map/ppermute | solution.py:339
  122.6 12.5 %collective-permute-start.2 = (bf16[2,768,128]{2,1,0:T(8,128)(2,1)S(1)}, bf16[2,768,128]{2,1,0:T(8,128)(2,1)S(1)}, u32[]{:S(2)}, u32[]{:S(2)}) collective-permute-start(bf16[2,768,128]{2,1,0:T(8,128)(2,1)S(1)} %get-tuple-element.40), channel_id=1, source_target_pairs={{1,0},{2,1},{3,2},{4,3},{5,4},{6,5},{7,6},{0,7},{9,8},{10,9},{11,1... | collective-permute-start | bytes 1179656 | tf_op jit(solution)/shard_map/ppermute | solution.py:385
  124.6 13.7 %collective-permute-start.1 = (bf16[2,768,128]{2,1,0:T(8,128)(2,1)S(1)}, bf16[2,768,128]{2,1,0:T(8,128)(2,1)}, u32[]{:S(2)}, u32[]{:S(2)}) collective-permute-start(bf16[2,768,128]{2,1,0:T(8,128)(2,1)S(1)} %get-tuple-element.41), channel_id=1, source_target_pairs={{0,1},{1,2},{2,3},{3,4},{4,5},{5,6},{6,7},{7,0},{8,9},{9,10},{10,1... | collective-permute-start | bytes 1179656 | tf_op jit(solution)/shard_map/ppermute | solution.py:384
  135.1 3.2 %copy-start.13 = (bf16[2,768,128]{2,1,0:T(8,128)(2,1)}, bf16[2,768,128]{2,1,0:T(8,128)(2,1)S(1)}, u32[]{:S(2)}) copy-start(bf16[2,768,128]{2,1,0:T(8,128)(2,1)S(1)} %collective-permute-done.2.high) | copy-start | bytes 1179652
  149.7 1.1 copy-start
  150.8 1.1 copy-start.2
  152.0 0.9 copy-start.4
  152.9 0.9 copy-start.6
  153.8 3.6 %copy-start.15 = (bf16[2,768,128]{2,1,0:T(8,128)(2,1)S(1)}, bf16[2,768,128]{2,1,0:T(8,128)(2,1)}, u32[]{:S(2)}) copy-start(bf16[2,768,128]{2,1,0:T(8,128)(2,1)} %get-tuple-element.30) | copy-start | bytes 1179652
  153.8 5.5 %copy-start.14 = (bf16[2,768,128]{2,1,0:T(8,128)(2,1)S(1)}, bf16[2,768,128]{2,1,0:T(8,128)(2,1)}, u32[]{:S(2)}) copy-start(bf16[2,768,128]{2,1,0:T(8,128)(2,1)} %get-tuple-element.31) | copy-start | bytes 1179652
  153.8 16.4 %copy-start.8 = (bf16[4,768,128]{2,1,0:T(8,128)(2,1)S(1)}, bf16[4,768,128]{2,1,0:T(8,128)(2,1)}, u32[]{:S(2)}) copy-start(bf16[4,768,128]{2,1,0:T(8,128)(2,1)} %get-tuple-element.29.own_ref) | copy-start | bytes 2359300
  154.6 62.1 %copy-start.9 = (f32[128,2]{0,1:T(2,128)S(1)}, f32[128,2]{0,1:T(2,128)}, u32[]{:S(2)}) copy-start(f32[128,2]{0,1:T(2,128)} %param.8) | copy-start | bytes 3076
  154.6 62.1 %copy-start.10 = (s32[2,128]{1,0:T(2,128)S(1)}, s32[2,128]{1,0:T(2,128)}, u32[]{:S(2)}) copy-start(s32[2,128]{1,0:T(2,128)} %get-tuple-element.22.rows_ref) | copy-start | bytes 3076
  154.6 63.5 %collective-permute-start.6 = (bf16[8192,128]{1,0:T(8,128)(2,1)S(1)}, bf16[8192,128]{1,0:T(8,128)(2,1)S(1)}, u32[]{:S(2)}, u32[]{:S(2)}) collective-permute-start(bf16[8192,128]{1,0:T(8,128)(2,1)S(1)} %shard_map.97), channel_id=1, source_target_pairs={{0,8},{1,9},{2,10},{3,11},{4,12},{5,13},{6,14},{7,15},{8,0},{9,1},... | collective-permute-start | bytes 6291464 | tf_op jit(solution)/shard_map/ppermute | solution.py:339
  157.4 11.9 %collective-permute-start.4 = (bf16[2,768,128]{2,1,0:T(8,128)(2,1)S(1)}, bf16[2,768,128]{2,1,0:T(8,128)(2,1)S(1)}, u32[]{:S(2)}, u32[]{:S(2)}) collective-permute-start(bf16[2,768,128]{2,1,0:T(8,128)(2,1)S(1)} %copy-done.15), channel_id=1, source_target_pairs={{0,1},{1,2},{2,3},{3,4},{4,5},{5,6},{6,7},{7,0},{8,9},{9,10},{10,1... | collective-permute-start | bytes 1179656 | tf_op jit(solution)/shard_map/ppermute | solution.py:427
  159.3 10.9 %collective-permute-start.5 = (bf16[2,768,128]{2,1,0:T(8,128)(2,1)S(1)}, bf16[2,768,128]{2,1,0:T(8,128)(2,1)S(1)}, u32[]{:S(2)}, u32[]{:S(2)}) collective-permute-start(bf16[2,768,128]{2,1,0:T(8,128)(2,1)S(1)} %copy-done.14), channel_id=1, source_target_pairs={{1,0},{2,1},{3,2},{4,3},{5,4},{6,5},{7,6},{0,7},{9,8},{10,9},{11,1... | collective-permute-start | bytes 1179656 | tf_op jit(solution)/shard_map/ppermute | solution.py:428
  170.2 47.9 %copy-start.1 = (bf16[192,2048]{1,0:T(8,128)(2,1)S(1)}, bf16[192,2048]{1,0:T(8,128)(2,1)}, u32[]{:S(2)}) copy-start(bf16[192,2048]{1,0:T(8,128)(2,1)} %get-tuple-element.34.x_ref) | copy-start | bytes 2359300
  170.2 47.9 %copy-start.3 = (bf16[192,2048]{1,0:T(8,128)(2,1)S(1)}, bf16[192,2048]{1,0:T(8,128)(2,1)}, u32[]{:S(2)}) copy-start(bf16[192,2048]{1,0:T(8,128)(2,1)} %get-tuple-element.35.g_ref) | copy-start | bytes 2359300
  170.2 47.9 %copy-start.5 = (bf16[2,192,256]{2,1,0:T(8,128)(2,1)S(1)}, bf16[2,192,256]{2,1,0:T(8,128)(2,1)}, u32[]{:S(2)}) copy-start(bf16[2,192,256]{2,1,0:T(8,128)(2,1)} %get-tuple-element.36.act_ref) | copy-start | bytes 589828
  170.3 47.9 %copy-start.7 = (bf16[2,192,256]{2,1,0:T(8,128)(2,1)S(1)}, bf16[2,192,256]{2,1,0:T(8,128)(2,1)}, u32[]{:S(2)}) copy-start(bf16[2,192,256]{2,1,0:T(8,128)(2,1)} %get-tuple-element.37.dpre_ref) | copy-start | bytes 589828

commit v6 on v5

--- a/solution.py
+++ b/solution.py
@@ -12,6 +12,7 @@
 F32 = jnp.float32
 HALVES = 2
 EARLY = (1, 2)
+GROUP = 8
 FOUR = 4
 
 
@@ -59,7 +60,7 @@
 def place_kernel(experts, cap, routes_in, gates_in, tok_in, cot_in, in_own, out_own, *refs):
     sent, rows_ref, early, late = refs[:4]
     scratch = refs[4:]
-    routes_ref, gates_ref, tok_ref, cot_ref, held_ref, sems, sent_sems, weight_sems = scratch
+    routes_ref, gates_ref, tok_ref, cot_ref, held_ref, in_ref, out_ref, sems, sent_sems, load_sems, weight_sems = scratch
     tok_rows, width = tok_in.shape
     copies = [
         pltpu.make_async_copy(routes_in, routes_ref, sems.at[0]),
@@ -69,16 +70,12 @@
     ]
     for copy in copies:
         copy.start()
-    weights = []
-    for (placed, _), out in zip(split_blocks(*reversed(in_own.shape), width), (early, late)):
-        for which, first, at, rows in placed:
-            source = (in_own, out_own)[which].at[:, pl.ds(first, width)]
-            weights.append(
-                pltpu.make_async_copy(
-                    source, out.at[pl.ds(at, rows), :], weight_sems.at[len(weights)]
-                )
-            )
-            weights[-1].start()
+    loads = [
+        pltpu.make_async_copy(in_own, in_ref, load_sems.at[0]),
+        pltpu.make_async_copy(out_own, out_ref, load_sems.at[1]),
+    ]
+    for copy in loads:
+        copy.start()
     copies[0].wait()
     routes = routes_ref[...]
     first, second = routes[0:1, :], routes[1:2, :]
@@ -109,6 +106,18 @@
     )
     copies[2].wait()
     copies[3].wait()
+    for copy in loads:
+        copy.wait()
+    weights = []
+    for (placed, _), out in zip(split_blocks(*reversed(in_own.shape), width), (early, late)):
+        for which, first, at, rows in placed:
+            source = (in_ref, out_ref)[which].at[:, pl.ds(first, width)]
+            weights.append(
+                pltpu.make_async_copy(
+                    source, out.at[pl.ds(at, rows), :], weight_sems.at[len(weights)]
+                )
+            )
+            weights[-1].start()
     held_x = dot(mask(at_x), tok_ref[...])
     held_g = dot(mask(at0 | at1), cot_ref[...]) * gate
     held_ref[...] = (held_x + held_g).astype(BF16)
@@ -132,9 +141,9 @@
 
 
 def expert_kernel(used, odd_ref, own, low, high, in_own, out_own, early, late, *rest):
-    ret_own, ret_low, ret_high, x_out, g_out, act_ref, dpre_ref = rest[:7]
-    recv_ref, pick_ref, spread_ref, x_ref, g_ref, in0, in1, out0, out1, held_ref, ret_ref = rest[7:18]
-    recv_sems, weight_sems, ret_sems, kept_sems = rest[18:]
+    ret_own, ret_low, ret_high, x_out, g_out, act_ref, dpre_ref, share_out = rest[:8]
+    recv_ref, x_ref, g_ref, in0, in1, out0, out1, held_ref, ret_ref, share_ref = rest[8:18]
+    recv_sems, weight_sems, ret_sems, kept_sems, share_sems = rest[18:]
     classes, all_rows, width = own.shape
     peers = 2 * classes
     rows = all_rows // 4
@@ -166,19 +175,24 @@
             )
     for copy in arrive + load_in[0] + load_in[1] + load_out[0] + load_out[1]:
         copy.start()
-    shape = (all_rows, all_rows)
-    pick_ref[...] = mask(iota(shape, 0) == sorted_row(iota((1, all_rows), 1), used, sources))
-    spread_ref[...] = mask(iota(shape, 1) == sorted_row(iota((all_rows, 1), 0), used, sources))
+    batch = GROUP if sources % GROUP == 0 else sources
+    size = 4 * used * batch
+    part_rows = used * batch
+    pick = mask(iota((size, size), 0) == sorted_row(iota((1, size), 1), used, batch))
+    spread = mask(iota((size, size), 1) == sorted_row(iota((size, 1), 0), used, batch))
     for copy in arrive:
         copy.wait()
     for pair in range(classes):
         cols = slice(pair * 2 * width, (pair + 1) * 2 * width)
-        block = dot(pick_ref[...], recv_ref[:, cols]).astype(BF16)
-        for part in range(HALVES):
-            at = (part * peers + 2 * pair) * width
-            start = part * 2 * rows
-            x_ref[:, at : at + 2 * width] = block[start : start + rows, :]
-            g_ref[:, at : at + 2 * width] = block[start + rows : start + 2 * rows, :]
+        for at_group in range(sources // batch):
+            block = dot(pick, recv_ref[at_group * size : (at_group + 1) * size, cols]).astype(BF16)
+            here = slice(at_group * part_rows, (at_group + 1) * part_rows)
+            for part in range(HALVES):
+                at = (part * peers + 2 * pair) * width
+                start = part * 2 * part_rows
+                x_ref[here, at : at + 2 * width] = block[start : start + part_rows, :]
+                start = start + part_rows
+                g_ref[here, at : at + 2 * width] = block[start : start + part_rows, :]
     kept = [
         pltpu.make_async_copy(x_ref, x_out, kept_sems.at[0]),
         pltpu.make_async_copy(g_ref, g_out, kept_sems.at[1]),
@@ -207,12 +221,17 @@
             cols = slice(at, at + 2 * width)
             given = dot(acts[0], out0[:, cols]) + dot(acts[1], out1[:, cols])
             back = dot(dpres[0], in0[cols, :], by_last) + dot(dpres[1], in1[cols, :], by_last)
-            start = part * 2 * rows
-            held_ref[start : start + rows, :] = given.astype(BF16)
-            held_ref[start + rows : start + 2 * rows, :] = back.astype(BF16)
-        ret_ref[:, pair * 2 * width : (pair + 1) * 2 * width] = dot(
-            spread_ref[...], held_ref[...]
-        ).astype(BF16)
+            for kind, block in ((0, given), (1, back)):
+                block = block.astype(BF16)
+                for at_group in range(sources // batch):
+                    start = at_group * size + (2 * part + kind) * part_rows
+                    here = slice(at_group * part_rows, (at_group + 1) * part_rows)
+                    held_ref[start : start + part_rows, :] = block[here, :]
+        for at_group in range(sources // batch):
+            here = slice(at_group * size, (at_group + 1) * size)
+            ret_ref[here, pair * 2 * width : (pair + 1) * 2 * width] = dot(
+                spread, held_ref[here, :]
+            ).astype(BF16)
         other = ret_low.at[pair] if pair < side else ret_high.at[pair - side]
         leave.append(
             pltpu.make_async_copy(
@@ -226,23 +245,28 @@
         )
         leave[-2].start()
         leave[-1].start()
-    for copy in leave + kept:
+    over_rows = ((0,), (0,))
+    model, hidden = in0.shape
+    shares = []
+
+    def share(block, start):
+        for index in range(hidden // width):
+            at = pl.ds(start(index), hidden)
+            share_ref[at, :] = block[:, index * width : (index + 1) * width]
+            shares.append(
+                pltpu.make_async_copy(
+                    share_ref.at[at, :], share_out.at[at, :], share_sems.at[len(shares)]
+                )
+            )
+            shares[-1].start()
+
+    for at in range(0, model, hidden):
+        block = dot(x_ref[:, at : at + hidden], dpres[1], over_rows).astype(BF16)
+        share(block, lambda index, at=at: index * model + at)
+        block = dot(acts[1], g_ref[:, at : at + hidden], over_rows).astype(BF16)
+        share(block, lambda index, at=at: hidden // width * model + (at // width + index) * hidden)
+    for copy in leave + kept + shares:
         copy.wait()
-
-
-def partner_kernel(x_ref, g_ref, act_ref, dpre_ref, out_ref):
-    over_rows = ((0,), (0,))
-    model = x_ref.shape[1]
-    hidden, width = dpre_ref.shape[2], out_ref.shape[1]
-    for at in range(0, model, hidden):
-        part = dot(x_ref[:, at : at + hidden], dpre_ref[1], over_rows).astype(BF16)
-        for index in range(hidden // width):
-            start = index * model + at
-            out_ref[start : start + hidden, :] = part[:, index * width : (index + 1) * width]
-        part = dot(act_ref[1], g_ref[:, at : at + hidden], over_rows).astype(BF16)
-        for index in range(hidden // width):
-            start = hidden // width * model + (at // width + index) * hidden
-            out_ref[start : start + hidden, :] = part[:, index * width : (index + 1) * width]
 
 
 def gradient_kernel(x_ref, g_ref, act_ref, dpre_ref, sent_ref, grad_in_ref, grad_out_ref):
@@ -367,8 +391,11 @@
             pltpu.VMEM((tok_rows, width), BF16),
             pltpu.VMEM((tok_rows, width), BF16),
             pltpu.VMEM((all_rows, width), BF16),
+            pltpu.VMEM((model, hidden), BF16),
+            pltpu.VMEM((hidden, model), BF16),
             dma((4,)),
             dma((classes,)),
+            dma((2,)),
             dma((blocks,)),
         ],
         routes_t,
@@ -384,7 +411,7 @@
     low = lax.ppermute(recv[:side], "cuts", up)
     high = lax.ppermute(recv[side:], "cuts", down)
     late = to_partner(late)
-    ret_own, ret_low, ret_high, held_x, held_g, active, dpre = call(
+    ret_own, ret_low, ret_high, held_x, held_g, active, dpre, sent_grads = call(
         functools.partial(expert_kernel, used),
         (
             struct(classes, all_rows, width),
@@ -394,14 +421,13 @@
             struct(rows, model),
             struct(2, rows, hidden),
             struct(2, rows, hidden),
+            struct(early_rows + late_rows, width),
         ),
         (16 * rows * model * hidden, 12 * rows * model + 8 * model * hidden),
-        ([pltpu.SMEM] + [far] * 7, [far] * 5 + [near] * 2),
+        ([pltpu.SMEM] + [far] * 7, [far] * 5 + [near] * 2 + [far]),
         60,
         [
             pltpu.VMEM((all_rows, peers * width), BF16),
-            pltpu.VMEM((all_rows, all_rows), BF16),
-            pltpu.VMEM((all_rows, all_rows), BF16),
             pltpu.VMEM((rows, model), BF16),
             pltpu.VMEM((rows, model), BF16),
             pltpu.VMEM((model, hidden), BF16),
@@ -410,10 +436,12 @@
             pltpu.VMEM((hidden, model), BF16),
             pltpu.VMEM((all_rows, 2 * width), BF16),
             pltpu.VMEM((all_rows, peers * width), BF16),
+            pltpu.VMEM((early_rows + late_rows, width), BF16),
             dma((peers,)),
             dma((2 + blocks,)),
             dma((peers,)),
             dma((2,)),
+            dma((2 * model // hidden * (hidden // width),)),
         ],
         odd,
         recv,
@@ -426,18 +454,6 @@
     )
     from_low = lax.ppermute(ret_low, "cuts", up)
     from_high = lax.ppermute(ret_high, "cuts", down)
-    sent_grads = call(
-        partner_kernel,
-        (struct(early_rows + late_rows, width),),
-        (8 * rows * model * hidden, 8 * model * hidden),
-        ([near] * 4, [near]),
-        24,
-        [],
-        held_x,
-        held_g,
-        active,
-        dpre,
-    )[0]
     sent_grads = to_partner(sent_grads)
     summed = call(
         add_kernel,

time: 221 us -> 155 us (0.70)
  Pallas kernels: 81.4 us -> 18.6 us
  local copies, waits for them, and re-layouts: 4.21 us -> 1.22 us
    pallas_call x6 -> x5, Pallas kernels: 81.4 us -> 18.6 us  [call(): pl.pallas_call(kernel, out_shape=shapes, in_specs=[pl.BlockSpec(memory_sp...]
    unnamed x32 -> x20, local copies, waits for them, and re-layouts: 4.16 us -> 1.17 us
where the time goes in v6:
time: 155 us
  blocking collectives  96.6 us (62%)
  starting transfers between devices  20.6 us (13%)
  Pallas kernels  18.6 us (12%)
  waiting for transfers between devices  16.9 us (11%)
    all_to_all x2, blocking collectives, over_spread(): lax.all_to_all(pieces, ('dp', 'cuts'), 0, 0, tiled=True, axis_index_group...  96.6 us
    pallas_call x5, Pallas kernels, call(): pl.pallas_call(kernel, out_shape=shapes, in_specs=[pl.BlockSpec(memory_sp...  18.6 us
    ppermute x3, starting transfers between devices, to_partner(): return lax.ppermute(value, 'cuts', swap)  8.79 us
    ppermute x1, waiting for transfers between devices, body(): high = lax.ppermute(recv[side:], 'cuts', down)  7.15 us
    ppermute x1, waiting for transfers between devices, body(): from_low = lax.ppermute(ret_low, 'cuts', up)  5.64 us
    ppermute x1, starting transfers between devices, body(): from_high = lax.ppermute(ret_high, 'cuts', down)  4.57 us
    ppermute x1, starting transfers between devices, body(): low = lax.ppermute(recv[:side], 'cuts', up)  3.36 us
    ppermute x1, waiting for transfers between devices, body(): low = lax.ppermute(recv[:side], 'cuts', up)  3.14 us
  transfers between devices with their start and end apart: 7, of which 4 were waited for; matrix products, arithmetic and copies ran while one was open for 0% of the time, Pallas kernels for 1%

profile of v6, /device:TPU:1, one launch (start us, length us, event | category | flops | bytes accessed | tf_op | source)
XLA Modules:
  0.0 154.8 jit_solution(1808358536667975956)
XLA Ops:
  0.6 4.0 %shard_map.93 = (bf16[4,768,128]{2,1,0:T(8,128)(2,1)}, s32[2,128]{1,0:T(2,128)}, bf16[6144,128]{1,0:T(8,128)(2,1)}, bf16[2048,128]{1,0:T(8,128)(2,1)}) custom-call(s32[2,128]{1,0:T(2,128)} %bitcast.20, f32[2,128]{1,0:T(2,128)} %bitcast.11, bf16[128,128]{1,0:T(8,128)(2,1)} %tok_in.1, bf16[128,128]{1,0:T(8,128)(2,1)} %cot_in.1, bf16[2048,256]{1,0:T(8,128)(2,1)} %bitcast.15, ...), custom_call_target="tpu_custom_call" | custom-call | flops 50331648 | bytes 1572864 | tf_op jit(solution)/shard_map/pallas_call | solution.py:324
  4.6 3.9 %collective-permute-start = (bf16[6144,128]{1,0:T(8,128)(2,1)}, bf16[6144,128]{1,0:T(8,128)(2,1)S(1)}, u32[]{:S(2)}, u32[]{:S(2)}) collective-permute-start(bf16[6144,128]{1,0:T(8,128)(2,1)} %get-tuple-element.25), channel_id=1, source_target_pairs={{0,8},{1,9},{2,10},{3,11},{4,12},{5,13},{6,14},{7,15},{8,0},{9,1},... | collective-permute-start | bytes 4718600 | tf_op jit(solution)/shard_map/ppermute | solution.py:363
  8.6 50.4 %all_to_all.10 = bf16[768,4,128]{2,1,0:T(4,128)(2,1)S(1)} all-to-all(bf16[768,4,128]{2,1,0:T(4,128)(2,1)} %bitcast.19), channel_id=1, replica_groups={{0,8,16,24,32,40,48,56,64,72,80,88,96,104,112,120,128,136,144,152,160,1..., dimensions={0} | all-to-all | bytes 1572864 | tf_op jit(solution)/shard_map/all_to_all | solution.py:367
  59.0 0.0 collective-permute-done.early
  59.0 2.1 %collective-permute-start.3 = (bf16[2048,128]{1,0:T(8,128)(2,1)}, bf16[2048,128]{1,0:T(8,128)(2,1)}, u32[]{:S(2)}, u32[]{:S(2)}) collective-permute-start(bf16[2048,128]{1,0:T(8,128)(2,1)} %get-tuple-element.29), channel_id=1, source_target_pairs={{0,8},{1,9},{2,10},{3,11},{4,12},{5,13},{6,14},{7,15},{8,0},{9,1},... | collective-permute-start | bytes 1572872 | tf_op jit(solution)/shard_map/ppermute | solution.py:363
  61.1 0.1 fusion
  61.2 1.9 %collective-permute-start.2 = (bf16[2,768,128]{2,1,0:T(8,128)(2,1)S(1)}, bf16[2,768,128]{2,1,0:T(8,128)(2,1)S(1)}, u32[]{:S(2)}, u32[]{:S(2)}) collective-permute-start(bf16[2,768,128]{2,1,0:T(8,128)(2,1)S(1)} %get-tuple-element.42), channel_id=1, source_target_pairs={{1,0},{2,1},{3,2},{4,3},{5,4},{6,5},{7,6},{0,7},{9,8},{10,9},{11,1... | collective-permute-start | bytes 1179656 | tf_op jit(solution)/shard_map/ppermute | solution.py:412
  63.1 3.4 %collective-permute-start.1 = (bf16[2,768,128]{2,1,0:T(8,128)(2,1)S(1)}, bf16[2,768,128]{2,1,0:T(8,128)(2,1)}, u32[]{:S(2)}, u32[]{:S(2)}) collective-permute-start(bf16[2,768,128]{2,1,0:T(8,128)(2,1)S(1)} %get-tuple-element.43), channel_id=1, source_target_pairs={{0,1},{1,2},{2,3},{3,4},{4,5},{5,6},{6,7},{7,0},{8,9},{9,10},{10,1... | collective-permute-start | bytes 1179656 | tf_op jit(solution)/shard_map/ppermute | solution.py:411
  66.5 7.2 %collective-permute-done.2.high = bf16[2,768,128]{2,1,0:T(8,128)(2,1)S(1)} collective-permute-done((bf16[2,768,128]{2,1,0:T(8,128)(2,1)S(1)}, bf16[2,768,128]{2,1,0:T(8,128)(2,1)S(1)}, u32[]{:S(2)}, u32[]{:S(2)}) %collective-permute-start.2) | collective-permute-done | bytes 393248 | tf_op jit(solution)/shard_map/ppermute | solution.py:412
  73.7 3.1 %collective-permute-done.1.low = bf16[2,768,128]{2,1,0:T(8,128)(2,1)} collective-permute-done((bf16[2,768,128]{2,1,0:T(8,128)(2,1)S(1)}, bf16[2,768,128]{2,1,0:T(8,128)(2,1)}, u32[]{:S(2)}, u32[]{:S(2)}) %collective-permute-start.1) | collective-permute-done | bytes 393248 | tf_op jit(solution)/shard_map/ppermute | solution.py:411
  76.8 0.0 collective-permute-done.3.late
  76.8 0.0 copy-done.7
  76.8 0.0 copy-done.8
  76.8 0.0 copy-done.9
  76.8 10.9 %shard_map.94 = (bf16[4,768,128]{2,1,0:T(8,128)(2,1)}, bf16[2,768,128]{2,1,0:T(8,128)(2,1)}, bf16[2,768,128]{2,1,0:T(8,128)(2,1)}, bf16[192,2048]{1,0:T(8,128)(2...) custom-call(s32[1]{0:T(128)} %bitcast.4.odd_ref, ...), custom_call_target="tpu_custom_call" | custom-call | flops 1610612736 | bytes 8912896 | tf_op jit(solution)/shard_map/pallas_call | solution.py:324
  87.7 0.0 copy-start.5
  87.7 0.0 copy-start.6
  87.7 2.7 %collective-permute-start.6 = (bf16[8192,128]{1,0:T(8,128)(2,1)}, bf16[8192,128]{1,0:T(8,128)(2,1)S(1)}, u32[]{:S(2)}, u32[]{:S(2)}) collective-permute-start(bf16[8192,128]{1,0:T(8,128)(2,1)} %get-tuple-element.39), channel_id=1, source_target_pairs={{0,8},{1,9},{2,10},{3,11},{4,12},{5,13},{6,14},{7,15},{8,0},{9,1},... | collective-permute-start | bytes 6291464 | tf_op jit(solution)/shard_map/ppermute | solution.py:363
  90.5 1.9 %collective-permute-start.4 = (bf16[2,768,128]{2,1,0:T(8,128)(2,1)}, bf16[2,768,128]{2,1,0:T(8,128)(2,1)S(1)}, u32[]{:S(2)}, u32[]{:S(2)}) collective-permute-start(bf16[2,768,128]{2,1,0:T(8,128)(2,1)} %get-tuple-element.31), channel_id=1, source_target_pairs={{0,1},{1,2},{2,3},{3,4},{4,5},{5,6},{6,7},{7,0},{8,9},{9,10},{10,1... | collective-permute-start | bytes 1179656 | tf_op jit(solution)/shard_map/ppermute | solution.py:455
  92.4 4.6 %collective-permute-start.5 = (bf16[2,768,128]{2,1,0:T(8,128)(2,1)}, bf16[2,768,128]{2,1,0:T(8,128)(2,1)S(1)}, u32[]{:S(2)}, u32[]{:S(2)}) collective-permute-start(bf16[2,768,128]{2,1,0:T(8,128)(2,1)} %get-tuple-element.32), channel_id=1, source_target_pairs={{1,0},{2,1},{3,2},{4,3},{5,4},{6,5},{7,6},{0,7},{9,8},{10,9},{11,1... | collective-permute-start | bytes 1179656 | tf_op jit(solution)/shard_map/ppermute | solution.py:456
  97.0 5.6 %collective-permute-done.4.low_ref = bf16[2,768,128]{2,1,0:T(8,128)(2,1)S(1)} collective-permute-done((bf16[2,768,128]{2,1,0:T(8,128)(2,1)}, bf16[2,768,128]{2,1,0:T(8,128)(2,1)S(1)}, u32[]{:S(2)}, u32[]{:S(2)}) %collective-permute-start.4) | collective-permute-done | bytes 393248 | tf_op jit(solution)/shard_map/ppermute | solution.py:455
  102.6 1.0 collective-permute-done.5.high_ref
  103.6 1.1 copy-done
  104.8 0.2 shard_map.95
  104.9 46.2 %all_to_all.11 = bf16[768,4,128]{2,1,0:T(4,128)(2,1)S(1)} all-to-all(bf16[768,4,128]{2,1,0:T(4,128)(2,1)S(1)} %bitcast.9), channel_id=1, replica_groups={{0,8,16,24,32,40,48,56,64,72,80,88,96,104,112,120,128,136,144,152,160,1..., dimensions={0} | all-to-all | bytes 1572864 | tf_op jit(solution)/shard_map/all_to_all | solution.py:367
  151.2 0.0 copy-done.5
  151.2 0.0 copy-done.6
  151.2 1.5 shard_map.96
  152.6 0.0 collective-permute-done.6.sent_ref
  152.6 0.0 copy-done.1
  152.6 0.0 copy-done.2
  152.7 2.1 %shard_map.97 = (bf16[1,2048,256]{2,1,0:T(8,128)(2,1)}, bf16[1,256,2048]{2,1,0:T(8,128)(2,1)}) custom-call(bf16[192,2048]{1,0:T(8,128)(2,1)S(1)} %copy-done.1, bf16[192,2048]{1,0:T(8,128)(2,1)S(1)} %copy-done.2, bf16[2,192,256]{2,1,0:T(8,128)(2,1)S(1)} %copy-done.3, bf16[2,192,256]{2,1,0:T(8,128)(2,1)S(1)} %copy-done.4, ...), custom_call_target="tpu_custom_call" | custom-call | flops 805306368 | bytes 8388608 | tf_op jit(solution)/shard_map/pallas_call | solution.py:324
  (10 shorter events, 0.0 us)
Async XLA Ops:
  4.6 54.4 %collective-permute-start = (bf16[6144,128]{1,0:T(8,128)(2,1)}, bf16[6144,128]{1,0:T(8,128)(2,1)S(1)}, u32[]{:S(2)}, u32[]{:S(2)}) collective-permute-start(bf16[6144,128]{1,0:T(8,128)(2,1)} %get-tuple-element.25), channel_id=1, source_target_pairs={{0,8},{1,9},{2,10},{3,11},{4,12},{5,13},{6,14},{7,15},{8,0},{9,1},... | collective-permute-start | bytes 4718600 | tf_op jit(solution)/shard_map/ppermute | solution.py:363
  59.0 17.8 %copy-start.7 = (bf16[768,4,128]{2,1,0:T(4,128)(2,1)}, bf16[768,4,128]{2,1,0:T(4,128)(2,1)S(1)}, u32[]{:S(2)}) copy-start(bf16[768,4,128]{2,1,0:T(4,128)(2,1)S(1)} %all_to_all.10) | copy-start | bytes 2359300
  59.0 17.8 %copy-start.8 = (bf16[6144,128]{1,0:T(8,128)(2,1)}, bf16[6144,128]{1,0:T(8,128)(2,1)S(1)}, u32[]{:S(2)}) copy-start(bf16[6144,128]{1,0:T(8,128)(2,1)S(1)} %collective-permute-done.early) | copy-start | bytes 4718596
  59.0 17.8 %collective-permute-start.3 = (bf16[2048,128]{1,0:T(8,128)(2,1)}, bf16[2048,128]{1,0:T(8,128)(2,1)}, u32[]{:S(2)}, u32[]{:S(2)}) collective-permute-start(bf16[2048,128]{1,0:T(8,128)(2,1)} %get-tuple-element.29), channel_id=1, source_target_pairs={{0,8},{1,9},{2,10},{3,11},{4,12},{5,13},{6,14},{7,15},{8,0},{9,1},... | collective-permute-start | bytes 1572872 | tf_op jit(solution)/shard_map/ppermute | solution.py:363
  61.2 12.5 %collective-permute-start.2 = (bf16[2,768,128]{2,1,0:T(8,128)(2,1)S(1)}, bf16[2,768,128]{2,1,0:T(8,128)(2,1)S(1)}, u32[]{:S(2)}, u32[]{:S(2)}) collective-permute-start(bf16[2,768,128]{2,1,0:T(8,128)(2,1)S(1)} %get-tuple-element.42), channel_id=1, source_target_pairs={{1,0},{2,1},{3,2},{4,3},{5,4},{6,5},{7,6},{0,7},{9,8},{10,9},{11,1... | collective-permute-start | bytes 1179656 | tf_op jit(solution)/shard_map/ppermute | solution.py:412
  63.1 13.7 %collective-permute-start.1 = (bf16[2,768,128]{2,1,0:T(8,128)(2,1)S(1)}, bf16[2,768,128]{2,1,0:T(8,128)(2,1)}, u32[]{:S(2)}, u32[]{:S(2)}) collective-permute-start(bf16[2,768,128]{2,1,0:T(8,128)(2,1)S(1)} %get-tuple-element.43), channel_id=1, source_target_pairs={{0,1},{1,2},{2,3},{3,4},{4,5},{5,6},{6,7},{7,0},{8,9},{9,10},{10,1... | collective-permute-start | bytes 1179656 | tf_op jit(solution)/shard_map/ppermute | solution.py:411
  73.7 3.2 %copy-start.9 = (bf16[2,768,128]{2,1,0:T(8,128)(2,1)}, bf16[2,768,128]{2,1,0:T(8,128)(2,1)S(1)}, u32[]{:S(2)}) copy-start(bf16[2,768,128]{2,1,0:T(8,128)(2,1)S(1)} %collective-permute-done.2.high) | copy-start | bytes 1179652
  87.7 63.5 %copy-start.5 = (f32[128,2]{0,1:T(2,128)S(1)}, f32[128,2]{0,1:T(2,128)}, u32[]{:S(2)}) copy-start(f32[128,2]{0,1:T(2,128)} %param.8) | copy-start | bytes 3076
  87.7 63.5 %copy-start.6 = (s32[2,128]{1,0:T(2,128)S(1)}, s32[2,128]{1,0:T(2,128)}, u32[]{:S(2)}) copy-start(s32[2,128]{1,0:T(2,128)} %get-tuple-element.23.rows_ref) | copy-start | bytes 3076
  87.7 64.9 %collective-permute-start.6 = (bf16[8192,128]{1,0:T(8,128)(2,1)}, bf16[8192,128]{1,0:T(8,128)(2,1)S(1)}, u32[]{:S(2)}, u32[]{:S(2)}) collective-permute-start(bf16[8192,128]{1,0:T(8,128)(2,1)} %get-tuple-element.39), channel_id=1, source_target_pairs={{0,8},{1,9},{2,10},{3,11},{4,12},{5,13},{6,14},{7,15},{8,0},{9,1},... | collective-permute-start | bytes 6291464 | tf_op jit(solution)/shard_map/ppermute | solution.py:363
  90.5 12.1 %collective-permute-start.4 = (bf16[2,768,128]{2,1,0:T(8,128)(2,1)}, bf16[2,768,128]{2,1,0:T(8,128)(2,1)S(1)}, u32[]{:S(2)}, u32[]{:S(2)}) collective-permute-start(bf16[2,768,128]{2,1,0:T(8,128)(2,1)} %get-tuple-element.31), channel_id=1, source_target_pairs={{0,1},{1,2},{2,3},{3,4},{4,5},{5,6},{6,7},{7,0},{8,9},{9,10},{10,1... | collective-permute-start | bytes 1179656 | tf_op jit(solution)/shard_map/ppermute | solution.py:455
  92.4 11.2 %collective-permute-start.5 = (bf16[2,768,128]{2,1,0:T(8,128)(2,1)}, bf16[2,768,128]{2,1,0:T(8,128)(2,1)S(1)}, u32[]{:S(2)}, u32[]{:S(2)}) collective-permute-start(bf16[2,768,128]{2,1,0:T(8,128)(2,1)} %get-tuple-element.32), channel_id=1, source_target_pairs={{1,0},{2,1},{3,2},{4,3},{5,4},{6,5},{7,6},{0,7},{9,8},{10,9},{11,1... | collective-permute-start | bytes 1179656 | tf_op jit(solution)/shard_map/ppermute | solution.py:456
  103.6 1.1 copy-start
  104.7 47.9 %copy-start.1 = (bf16[192,2048]{1,0:T(8,128)(2,1)S(1)}, bf16[192,2048]{1,0:T(8,128)(2,1)}, u32[]{:S(2)}) copy-start(bf16[192,2048]{1,0:T(8,128)(2,1)} %get-tuple-element.35.x_ref) | copy-start | bytes 2359300
  104.8 47.9 %copy-start.2 = (bf16[192,2048]{1,0:T(8,128)(2,1)S(1)}, bf16[192,2048]{1,0:T(8,128)(2,1)}, u32[]{:S(2)}) copy-start(bf16[192,2048]{1,0:T(8,128)(2,1)} %get-tuple-element.36.g_ref) | copy-start | bytes 2359300
  104.8 47.9 %copy-start.3 = (bf16[2,192,256]{2,1,0:T(8,128)(2,1)S(1)}, bf16[2,192,256]{2,1,0:T(8,128)(2,1)}, u32[]{:S(2)}) copy-start(bf16[2,192,256]{2,1,0:T(8,128)(2,1)} %get-tuple-element.37.act_ref) | copy-start | bytes 589828
  104.8 47.9 %copy-start.4 = (bf16[2,192,256]{2,1,0:T(8,128)(2,1)S(1)}, bf16[2,192,256]{2,1,0:T(8,128)(2,1)}, u32[]{:S(2)}) copy-start(bf16[2,192,256]{2,1,0:T(8,128)(2,1)} %get-tuple-element.38.dpre_ref) | copy-start | bytes 589828

commit v7 on v6

--- a/solution.py
+++ b/solution.py
@@ -55,6 +55,13 @@
             at += rows
         parts.append((placed, at))
     return parts
+
+
+def travelling(refs, start, rows):
+    early, late = refs
+    if start < early.shape[0]:
+        return early.at[pl.ds(start, rows), :]
+    return late.at[pl.ds(start - early.shape[0], rows), :]
 
 
 def place_kernel(experts, cap, routes_in, gates_in, tok_in, cot_in, in_own, out_own, *refs):
@@ -141,9 +148,9 @@
 
 
 def expert_kernel(used, odd_ref, own, low, high, in_own, out_own, early, late, *rest):
-    ret_own, ret_low, ret_high, x_out, g_out, act_ref, dpre_ref, share_out = rest[:8]
-    recv_ref, x_ref, g_ref, in0, in1, out0, out1, held_ref, ret_ref, share_ref = rest[8:18]
-    recv_sems, weight_sems, ret_sems, kept_sems, share_sems = rest[18:]
+    ret_own, ret_low, ret_high, x_out, g_out, act_ref, dpre_ref, *share_outs = rest[:9]
+    recv_ref, x_ref, g_ref, in0, in1, out0, out1, held_ref, ret_ref, share_ref = rest[9:19]
+    recv_sems, weight_sems, ret_sems, kept_sems, share_sems = rest[19:]
     classes, all_rows, width = own.shape
     peers = 2 * classes
     rows = all_rows // 4
@@ -173,7 +180,7 @@
                     source.at[pl.ds(at, size), :], target, weight_sems.at[index]
                 )
             )
-    for copy in arrive + load_in[0] + load_in[1] + load_out[0] + load_out[1]:
+    for copy in arrive + load_in[0] + load_in[1]:
         copy.start()
     batch = GROUP if sources % GROUP == 0 else sources
     size = 4 * used * batch
@@ -182,6 +189,8 @@
     spread = mask(iota((size, size), 1) == sorted_row(iota((size, 1), 0), used, batch))
     for copy in arrive:
         copy.wait()
+    for copy in load_out[0] + load_out[1]:
+        copy.start()
     for pair in range(classes):
         cols = slice(pair * 2 * width, (pair + 1) * 2 * width)
         for at_group in range(sources // batch):
@@ -197,8 +206,6 @@
         pltpu.make_async_copy(x_ref, x_out, kept_sems.at[0]),
         pltpu.make_async_copy(g_ref, g_out, kept_sems.at[1]),
     ]
-    for copy in kept:
-        copy.start()
 
     by_last = ((1,), (1,))
     acts, slopes, dpres = [], [], []
@@ -214,6 +221,8 @@
             copy.wait()
         dpres.append((dot(g_ref[...], ref[...], by_last) * slopes[group]).astype(BF16))
         dpre_ref[group] = dpres[group]
+    for copy in kept:
+        copy.start()
     leave = []
     for pair in range(classes):
         for part in range(HALVES):
@@ -253,10 +262,9 @@
         for index in range(hidden // width):
             at = pl.ds(start(index), hidden)
             share_ref[at, :] = block[:, index * width : (index + 1) * width]
+            target = travelling(share_outs, start(index), hidden)
             shares.append(
-                pltpu.make_async_copy(
-                    share_ref.at[at, :], share_out.at[at, :], share_sems.at[len(shares)]
-                )
+                pltpu.make_async_copy(share_ref.at[at, :], target, share_sems.at[len(shares)])
             )
             shares[-1].start()
 
@@ -269,24 +277,25 @@
         copy.wait()
 
 
-def gradient_kernel(x_ref, g_ref, act_ref, dpre_ref, sent_ref, grad_in_ref, grad_out_ref):
+def gradient_kernel(x_ref, g_ref, act_ref, dpre_ref, *refs):
+    sent_refs, grad_in_ref, grad_out_ref = refs[:2], refs[2], refs[3]
     over_rows = ((0,), (0,))
     model = x_ref.shape[1]
-    hidden, width = dpre_ref.shape[2], sent_ref.shape[1]
+    hidden, width = dpre_ref.shape[2], sent_refs[0].shape[1]
     for at in range(0, model, hidden):
         part = dot(x_ref[:, at : at + hidden], dpre_ref[0], over_rows)
         for index in range(hidden // width):
             start = index * model + at
             cols = slice(index * width, (index + 1) * width)
             grad_in_ref[0, at : at + hidden, cols] = (
-                part[:, cols] + sent_ref[start : start + hidden, :].astype(F32)
+                part[:, cols] + travelling(sent_refs, start, hidden)[...].astype(F32)
             ).astype(BF16)
         part = dot(act_ref[0], g_ref[:, at : at + hidden], over_rows)
         for index in range(hidden // width):
             start = hidden // width * model + (at // width + index) * hidden
             cols = slice(index * width, (index + 1) * width)
             grad_out_ref[0, :, at + index * width : at + (index + 1) * width] = (
-                part[:, cols] + sent_ref[start : start + hidden, :].astype(F32)
+                part[:, cols] + travelling(sent_refs, start, hidden)[...].astype(F32)
             ).astype(BF16)
 
 
@@ -405,13 +414,12 @@
         in_own,
         out_own,
     )
-    early = to_partner(early)
+    early, late = to_partner(early), to_partner(late)
     recv = over_spread(sent)
-    recv, early, late = lax.optimization_barrier((recv, early, late))
+    recv, early = lax.optimization_barrier((recv, early))
     low = lax.ppermute(recv[:side], "cuts", up)
     high = lax.ppermute(recv[side:], "cuts", down)
-    late = to_partner(late)
-    ret_own, ret_low, ret_high, held_x, held_g, active, dpre, sent_grads = call(
+    ret_own, ret_low, ret_high, held_x, held_g, active, dpre, grads, late_grads = call(
         functools.partial(expert_kernel, used),
         (
             struct(classes, all_rows, width),
@@ -421,10 +429,11 @@
             struct(rows, model),
             struct(2, rows, hidden),
             struct(2, rows, hidden),
-            struct(early_rows + late_rows, width),
+            struct(early_rows, width),
+            struct(late_rows, width),
         ),
         (16 * rows * model * hidden, 12 * rows * model + 8 * model * hidden),
-        ([pltpu.SMEM] + [far] * 7, [far] * 5 + [near] * 2 + [far]),
+        ([pltpu.SMEM] + [far] * 7, [far] * 5 + [near] * 2 + [far] * 2),
         60,
         [
             pltpu.VMEM((all_rows, peers * width), BF16),
@@ -454,7 +463,7 @@
     )
     from_low = lax.ppermute(ret_low, "cuts", up)
     from_high = lax.ppermute(ret_high, "cuts", down)
-    sent_grads = to_partner(sent_grads)
+    grads, late_grads = to_partner(grads), to_partner(late_grads)
     summed = call(
         add_kernel,
         (struct(classes, all_rows, width),),
@@ -471,14 +480,15 @@
         gradient_kernel,
         (struct(1, model, hidden), struct(1, hidden, model)),
         (8 * rows * model * hidden, 16 * model * hidden),
-        ([near] * 5, [near] * 2),
+        ([near] * 6, [near] * 2),
         32,
         [],
         held_x,
         held_g,
         active,
         dpre,
-        sent_grads,
+        grads,
+        late_grads,
     )
     mixed, token_grad = call(
         functools.partial(combine_kernel, used),

time: 155 us -> 154 us (level)
  blocking collectives: 96.6 us -> 0 us
  waiting for transfers between devices: 16.9 us -> 66.8 us
  starting transfers between devices: 20.6 us -> 63.5 us
    all_to_all x2 -> x0, blocking collectives: 96.6 us -> none  [over_spread(): lax.all_to_all(pieces, ('dp', 'cuts'), 0, 0, tiled=True, axis_index_group...]
    all_to_all x0 -> x2, starting transfers between devices: none -> 38.8 us  [over_spread(): lax.all_to_all(pieces, ('dp', 'cuts'), 0, 0, tiled=True, axis_index_group...]
    ppermute x3 -> x4, waiting for transfers between devices: 0.01 us -> 25.9 us  [to_partner(): return lax.ppermute(value, 'cuts', swap)]
    all_to_all x0 -> x2, waiting for transfers between devices: none -> 25.7 us  [over_spread(): lax.all_to_all(pieces, ('dp', 'cuts'), 0, 0, tiled=True, axis_index_group...]
    ppermute x3 -> x4, starting transfers between devices: 8.79 us -> 12.9 us  [to_partner(): return lax.ppermute(value, 'cuts', swap)]
    ppermute x1, waiting for transfers between devices: 5.64 us -> 3.91 us  [body(): from_low = lax.ppermute(ret_low, 'cuts', up)]
  transfers between devices with their start and end apart: 7 -> 10, of which waited for: 4 -> 6; matrix products, arithmetic and copies ran while one was open for 0% -> 0% of each run, Pallas kernels for 1% -> 2%
where the time goes in v7:
time: 154 us; the launch traced here: 153 us
  waiting for transfers between devices  66.8 us (43%)
  starting transfers between devices  63.5 us (41%)
  Pallas kernels  19.4 us (13%)
  local copies, waits for them, and re-layouts  2.34 us (2%)
    all_to_all x2, starting transfers between devices, over_spread(): lax.all_to_all(pieces, ('dp', 'cuts'), 0, 0, tiled=True, axis_index_group...  38.8 us
    ppermute x4, waiting for transfers between devices, to_partner(): return lax.ppermute(value, 'cuts', swap)  25.9 us
    all_to_all x2, waiting for transfers between devices, over_spread(): lax.all_to_all(pieces, ('dp', 'cuts'), 0, 0, tiled=True, axis_index_group...  25.7 us
    pallas_call x5, Pallas kernels, call(): pl.pallas_call(kernel, out_shape=shapes, in_specs=[pl.BlockSpec(memory_sp...  19.4 us
    ppermute x4, starting transfers between devices, to_partner(): return lax.ppermute(value, 'cuts', swap)  12.9 us
    ppermute x1, waiting for transfers between devices, body(): high = lax.ppermute(recv[side:], 'cuts', down)  7.15 us
    ppermute x1, starting transfers between devices, body(): from_high = lax.ppermute(ret_high, 'cuts', down)  4.57 us
    ppermute x1, waiting for transfers between devices, body(): from_low = lax.ppermute(ret_low, 'cuts', up)  3.91 us
  transfers between devices with their start and end apart: 10, of which 6 were waited for; matrix products, arithmetic and copies ran while one was open for 0% of the time, Pallas kernels for 2%

profile of v7, /device:TPU:1, one launch (start us, length us, event | category | flops | bytes accessed | tf_op | source)
XLA Modules:
  0.0 152.8 jit_solution(15378366591864880155)
XLA Ops:
  0.6 4.0 %shard_map.93 = (bf16[4,768,128]{2,1,0:T(8,128)(2,1)}, s32[2,128]{1,0:T(2,128)}, bf16[6144,128]{1,0:T(8,128)(2,1)}, bf16[2048,128]{1,0:T(8,128)(2,1)}) custom-call(s32[2,128]{1,0:T(2,128)} %bitcast.19, f32[2,128]{1,0:T(2,128)} %bitcast.10, bf16[128,128]{1,0:T(8,128)(2,1)} %tok_in.1, bf16[128,128]{1,0:T(8,128)(2,1)} %cot_in.1, bf16[2048,256]{1,0:T(8,128)(2,1)} %bitcast.14, ...), custom_call_target="tpu_custom_call" | custom-call | flops 50331648 | bytes 1572864 | tf_op jit(solution)/shard_map/pallas_call | solution.py:333
  4.6 3.9 %collective-permute-start = (bf16[6144,128]{1,0:T(8,128)(2,1)}, bf16[6144,128]{1,0:T(8,128)(2,1)S(1)}, u32[]{:S(2)}, u32[]{:S(2)}) collective-permute-start(bf16[6144,128]{1,0:T(8,128)(2,1)} %get-tuple-element.25), channel_id=1, source_target_pairs={{0,8},{1,9},{2,10},{3,11},{4,12},{5,13},{6,14},{7,15},{8,0},{9,1},... | collective-permute-start | bytes 4718600 | tf_op jit(solution)/shard_map/ppermute | solution.py:372
  8.6 21.6 %all-to-all-start = ((bf16[768,4,128]{2,1,0:T(4,128)(2,1)}), bf16[768,4,128]{2,1,0:T(4,128)(2,1)S(1)}, u32[]{:S(2)}, u32[]{:S(2)}) async-start(bf16[768,4,128]{2,1,0:T(4,128)(2,1)} %bitcast.18), calls=%async_computation | async-start | bytes 1572864 | tf_op jit(solution)/shard_map/all_to_all | solution.py:376
  30.2 3.3 %collective-permute-start.3 = (bf16[2048,128]{1,0:T(8,128)(2,1)}, bf16[2048,128]{1,0:T(8,128)(2,1)}, u32[]{:S(2)}, u32[]{:S(2)}) collective-permute-start(bf16[2048,128]{1,0:T(8,128)(2,1)} %get-tuple-element.28), channel_id=1, source_target_pairs={{0,8},{1,9},{2,10},{3,11},{4,12},{5,13},{6,14},{7,15},{8,0},{9,1},... | collective-permute-start | bytes 1572872 | tf_op jit(solution)/shard_map/ppermute | solution.py:372
  33.5 25.7 %all-to-all-done = bf16[768,4,128]{2,1,0:T(4,128)(2,1)S(1)} async-done(((bf16[768,4,128]{2,1,0:T(4,128)(2,1)}), bf16[768,4,128]{2,1,0:T(4,128)(2,1)S(1)}, u32[]{:S(2)}, u32[]{:S(2)}) %all-to-all-start) | async-done | bytes 786464 | tf_op jit(solution)/shard_map/all_to_all | solution.py:376
  59.1 0.0 collective-permute-done.early
  59.1 0.1 fusion
  59.2 1.9 %collective-permute-start.2 = (bf16[2,768,128]{2,1,0:T(8,128)(2,1)S(1)}, bf16[2,768,128]{2,1,0:T(8,128)(2,1)S(1)}, u32[]{:S(2)}, u32[]{:S(2)}) collective-permute-start(bf16[2,768,128]{2,1,0:T(8,128)(2,1)S(1)} %get-tuple-element.42), channel_id=1, source_target_pairs={{1,0},{2,1},{3,2},{4,3},{5,4},{6,5},{7,6},{0,7},{9,8},{10,9},{11,1... | collective-permute-start | bytes 1179656 | tf_op jit(solution)/shard_map/ppermute | solution.py:421
  61.1 3.4 %collective-permute-start.1 = (bf16[2,768,128]{2,1,0:T(8,128)(2,1)S(1)}, bf16[2,768,128]{2,1,0:T(8,128)(2,1)}, u32[]{:S(2)}, u32[]{:S(2)}) collective-permute-start(bf16[2,768,128]{2,1,0:T(8,128)(2,1)S(1)} %get-tuple-element.43), channel_id=1, source_target_pairs={{0,1},{1,2},{2,3},{3,4},{4,5},{5,6},{6,7},{7,0},{8,9},{9,10},{10,1... | collective-permute-start | bytes 1179656 | tf_op jit(solution)/shard_map/ppermute | solution.py:420
  64.5 0.0 collective-permute-done.3.late
  64.5 7.2 %collective-permute-done.2.high = bf16[2,768,128]{2,1,0:T(8,128)(2,1)S(1)} collective-permute-done((bf16[2,768,128]{2,1,0:T(8,128)(2,1)S(1)}, bf16[2,768,128]{2,1,0:T(8,128)(2,1)S(1)}, u32[]{:S(2)}, u32[]{:S(2)}) %collective-permute-start.2) | collective-permute-done | bytes 393248 | tf_op jit(solution)/shard_map/ppermute | solution.py:421
  71.7 3.1 %collective-permute-done.1.low = bf16[2,768,128]{2,1,0:T(8,128)(2,1)} collective-permute-done((bf16[2,768,128]{2,1,0:T(8,128)(2,1)S(1)}, bf16[2,768,128]{2,1,0:T(8,128)(2,1)}, u32[]{:S(2)}, u32[]{:S(2)}) %collective-permute-start.1) | collective-permute-done | bytes 393248 | tf_op jit(solution)/shard_map/ppermute | solution.py:420
  74.7 0.0 copy-done.7
  74.7 0.0 copy-done.8
  74.7 0.0 copy-done.9
  74.8 10.8 %shard_map.94 = (bf16[4,768,128]{2,1,0:T(8,128)(2,1)}, bf16[2,768,128]{2,1,0:T(8,128)(2,1)}, bf16[2,768,128]{2,1,0:T(8,128)(2,1)}, bf16[192,2048]{1,0:T(8,128)(2...) custom-call(s32[1]{0:T(128)} %bitcast.4.odd_ref, ...), custom_call_target="tpu_custom_call" | custom-call | flops 1610612736 | bytes 8912896 | tf_op jit(solution)/shard_map/pallas_call | solution.py:333
  85.5 1.9 %collective-permute-start.4 = (bf16[2,768,128]{2,1,0:T(8,128)(2,1)}, bf16[2,768,128]{2,1,0:T(8,128)(2,1)S(1)}, u32[]{:S(2)}, u32[]{:S(2)}) collective-permute-start(bf16[2,768,128]{2,1,0:T(8,128)(2,1)} %get-tuple-element.30), channel_id=1, source_target_pairs={{0,1},{1,2},{2,3},{3,4},{4,5},{5,6},{6,7},{7,0},{8,9},{9,10},{10,1... | collective-permute-start | bytes 1179656 | tf_op jit(solution)/shard_map/ppermute | solution.py:464
  87.5 4.6 %collective-permute-start.5 = (bf16[2,768,128]{2,1,0:T(8,128)(2,1)}, bf16[2,768,128]{2,1,0:T(8,128)(2,1)S(1)}, u32[]{:S(2)}, u32[]{:S(2)}) collective-permute-start(bf16[2,768,128]{2,1,0:T(8,128)(2,1)} %get-tuple-element.31), channel_id=1, source_target_pairs={{1,0},{2,1},{3,2},{4,3},{5,4},{6,5},{7,6},{0,7},{9,8},{10,9},{11,1... | collective-permute-start | bytes 1179656 | tf_op jit(solution)/shard_map/ppermute | solution.py:465
  92.0 2.4 %collective-permute-start.6 = (bf16[6144,128]{1,0:T(8,128)(2,1)}, bf16[6144,128]{1,0:T(8,128)(2,1)S(1)}, u32[]{:S(2)}, u32[]{:S(2)}) collective-permute-start(bf16[6144,128]{1,0:T(8,128)(2,1)} %get-tuple-element.38), channel_id=1, source_target_pairs={{0,8},{1,9},{2,10},{3,11},{4,12},{5,13},{6,14},{7,15},{8,0},{9,1},... | collective-permute-start | bytes 4718600 | tf_op jit(solution)/shard_map/ppermute | solution.py:372
  94.4 3.9 %collective-permute-done.4.low_ref = bf16[2,768,128]{2,1,0:T(8,128)(2,1)S(1)} collective-permute-done((bf16[2,768,128]{2,1,0:T(8,128)(2,1)}, bf16[2,768,128]{2,1,0:T(8,128)(2,1)S(1)}, u32[]{:S(2)}, u32[]{:S(2)}) %collective-permute-start.4) | collective-permute-done | bytes 393248 | tf_op jit(solution)/shard_map/ppermute | solution.py:464
  98.4 1.0 collective-permute-done.5.high_ref
  99.4 1.1 copy-done
  100.5 1.1 shard_map.95
  101.6 17.2 %all-to-all-start.1 = ((bf16[768,4,128]{2,1,0:T(4,128)(2,1)}), bf16[768,4,128]{2,1,0:T(4,128)(2,1)S(1)}, u32[]{:S(2)}, u32[]{:S(2)}) async-start(bf16[768,4,128]{2,1,0:T(4,128)(2,1)} %bitcast.7), calls=%async_computation.1 | async-start | bytes 1572864 | tf_op jit(solution)/shard_map/all_to_all | solution.py:376
  118.8 3.3 %collective-permute-start.7 = (bf16[2048,128]{1,0:T(8,128)(2,1)}, bf16[2048,128]{1,0:T(8,128)(2,1)S(1)}, u32[]{:S(2)}, u32[]{:S(2)}) collective-permute-start(bf16[2048,128]{1,0:T(8,128)(2,1)} %get-tuple-element.39), channel_id=1, source_target_pairs={{0,8},{1,9},{2,10},{3,11},{4,12},{5,13},{6,14},{7,15},{8,0},{9,1},... | collective-permute-start | bytes 1572872 | tf_op jit(solution)/shard_map/ppermute | solution.py:372
  122.1 25.9 %collective-permute-done.7.refs_1_ = bf16[2048,128]{1,0:T(8,128)(2,1)S(1)} collective-permute-done((bf16[2048,128]{1,0:T(8,128)(2,1)}, bf16[2048,128]{1,0:T(8,128)(2,1)S(1)}, u32[]{:S(2)}, u32[]{:S(2)}) %collective-permute-start.7) | collective-permute-done | bytes 524320 | tf_op jit(solution)/shard_map/ppermute | solution.py:372
  148.0 0.0 collective-permute-done.6.refs_0_
  148.0 0.0 copy-done.1
  148.1 1.1 copy-done.2
  149.2 2.1 %shard_map.97 = (bf16[1,2048,256]{2,1,0:T(8,128)(2,1)}, bf16[1,256,2048]{2,1,0:T(8,128)(2,1)}) custom-call(bf16[192,2048]{1,0:T(8,128)(2,1)S(1)} %copy-done.1, bf16[192,2048]{1,0:T(8,128)(2,1)S(1)} %copy-done.2, bf16[2,192,256]{2,1,0:T(8,128)(2,1)S(1)} %copy-done.3, bf16[2,192,256]{2,1,0:T(8,128)(2,1)S(1)} %copy-done.4, ...), custom_call_target="tpu_custom_call" | custom-call | flops 805306368 | bytes 8388608 | tf_op jit(solution)/shard_map/pallas_call | solution.py:333
  151.3 0.0 all-to-all-done.1
  151.3 1.5 shard_map.96
  (14 shorter events, 0.0 us)
Async XLA Ops:
  4.6 54.5 %collective-permute-start = (bf16[6144,128]{1,0:T(8,128)(2,1)}, bf16[6144,128]{1,0:T(8,128)(2,1)S(1)}, u32[]{:S(2)}, u32[]{:S(2)}) collective-permute-start(bf16[6144,128]{1,0:T(8,128)(2,1)} %get-tuple-element.25), channel_id=1, source_target_pairs={{0,8},{1,9},{2,10},{3,11},{4,12},{5,13},{6,14},{7,15},{8,0},{9,1},... | collective-permute-start | bytes 4718600 | tf_op jit(solution)/shard_map/ppermute | solution.py:372
  8.6 50.5 %all-to-all-start = ((bf16[768,4,128]{2,1,0:T(4,128)(2,1)}), bf16[768,4,128]{2,1,0:T(4,128)(2,1)S(1)}, u32[]{:S(2)}, u32[]{:S(2)}) async-start(bf16[768,4,128]{2,1,0:T(4,128)(2,1)} %bitcast.18), calls=%async_computation | async-start | bytes 1572864 | tf_op jit(solution)/shard_map/all_to_all | solution.py:376
  30.2 34.3 %collective-permute-start.3 = (bf16[2048,128]{1,0:T(8,128)(2,1)}, bf16[2048,128]{1,0:T(8,128)(2,1)}, u32[]{:S(2)}, u32[]{:S(2)}) collective-permute-start(bf16[2048,128]{1,0:T(8,128)(2,1)} %get-tuple-element.28), channel_id=1, source_target_pairs={{0,8},{1,9},{2,10},{3,11},{4,12},{5,13},{6,14},{7,15},{8,0},{9,1},... | collective-permute-start | bytes 1572872 | tf_op jit(solution)/shard_map/ppermute | solution.py:372
  59.1 15.6 %copy-start.7 = (bf16[768,4,128]{2,1,0:T(4,128)(2,1)}, bf16[768,4,128]{2,1,0:T(4,128)(2,1)S(1)}, u32[]{:S(2)}) copy-start(bf16[768,4,128]{2,1,0:T(4,128)(2,1)S(1)} %all-to-all-done) | copy-start | bytes 2359300
  59.1 15.6 %copy-start.8 = (bf16[6144,128]{1,0:T(8,128)(2,1)}, bf16[6144,128]{1,0:T(8,128)(2,1)S(1)}, u32[]{:S(2)}) copy-start(bf16[6144,128]{1,0:T(8,128)(2,1)S(1)} %collective-permute-done.early) | copy-start | bytes 4718596
  59.2 12.5 %collective-permute-start.2 = (bf16[2,768,128]{2,1,0:T(8,128)(2,1)S(1)}, bf16[2,768,128]{2,1,0:T(8,128)(2,1)S(1)}, u32[]{:S(2)}, u32[]{:S(2)}) collective-permute-start(bf16[2,768,128]{2,1,0:T(8,128)(2,1)S(1)} %get-tuple-element.42), channel_id=1, source_target_pairs={{1,0},{2,1},{3,2},{4,3},{5,4},{6,5},{7,6},{0,7},{9,8},{10,9},{11,1... | collective-permute-start | bytes 1179656 | tf_op jit(solution)/shard_map/ppermute | solution.py:421
  61.1 13.6 %collective-permute-start.1 = (bf16[2,768,128]{2,1,0:T(8,128)(2,1)S(1)}, bf16[2,768,128]{2,1,0:T(8,128)(2,1)}, u32[]{:S(2)}, u32[]{:S(2)}) collective-permute-start(bf16[2,768,128]{2,1,0:T(8,128)(2,1)S(1)} %get-tuple-element.43), channel_id=1, source_target_pairs={{0,1},{1,2},{2,3},{3,4},{4,5},{5,6},{6,7},{7,0},{8,9},{9,10},{10,1... | collective-permute-start | bytes 1179656 | tf_op jit(solution)/shard_map/ppermute | solution.py:420
  71.7 3.1 %copy-start.9 = (bf16[2,768,128]{2,1,0:T(8,128)(2,1)}, bf16[2,768,128]{2,1,0:T(8,128)(2,1)S(1)}, u32[]{:S(2)}) copy-start(bf16[2,768,128]{2,1,0:T(8,128)(2,1)S(1)} %collective-permute-done.2.high) | copy-start | bytes 1179652
  85.5 12.8 %collective-permute-start.4 = (bf16[2,768,128]{2,1,0:T(8,128)(2,1)}, bf16[2,768,128]{2,1,0:T(8,128)(2,1)S(1)}, u32[]{:S(2)}, u32[]{:S(2)}) collective-permute-start(bf16[2,768,128]{2,1,0:T(8,128)(2,1)} %get-tuple-element.30), channel_id=1, source_target_pairs={{0,1},{1,2},{2,3},{3,4},{4,5},{5,6},{6,7},{7,0},{8,9},{9,10},{10,1... | collective-permute-start | bytes 1179656 | tf_op jit(solution)/shard_map/ppermute | solution.py:464
  87.5 11.9 %collective-permute-start.5 = (bf16[2,768,128]{2,1,0:T(8,128)(2,1)}, bf16[2,768,128]{2,1,0:T(8,128)(2,1)S(1)}, u32[]{:S(2)}, u32[]{:S(2)}) collective-permute-start(bf16[2,768,128]{2,1,0:T(8,128)(2,1)} %get-tuple-element.31), channel_id=1, source_target_pairs={{1,0},{2,1},{3,2},{4,3},{5,4},{6,5},{7,6},{0,7},{9,8},{10,9},{11,1... | collective-permute-start | bytes 1179656 | tf_op jit(solution)/shard_map/ppermute | solution.py:465
  92.0 56.0 %collective-permute-start.6 = (bf16[6144,128]{1,0:T(8,128)(2,1)}, bf16[6144,128]{1,0:T(8,128)(2,1)S(1)}, u32[]{:S(2)}, u32[]{:S(2)}) collective-permute-start(bf16[6144,128]{1,0:T(8,128)(2,1)} %get-tuple-element.38), channel_id=1, source_target_pairs={{0,8},{1,9},{2,10},{3,11},{4,12},{5,13},{6,14},{7,15},{8,0},{9,1},... | collective-permute-start | bytes 4718600 | tf_op jit(solution)/shard_map/ppermute | solution.py:372
  99.4 1.1 copy-start
  100.5 47.5 %copy-start.1 = (bf16[192,2048]{1,0:T(8,128)(2,1)S(1)}, bf16[192,2048]{1,0:T(8,128)(2,1)}, u32[]{:S(2)}) copy-start(bf16[192,2048]{1,0:T(8,128)(2,1)} %get-tuple-element.34.x_ref) | copy-start | bytes 2359300
  100.5 47.5 %copy-start.3 = (bf16[2,192,256]{2,1,0:T(8,128)(2,1)S(1)}, bf16[2,192,256]{2,1,0:T(8,128)(2,1)}, u32[]{:S(2)}) copy-start(bf16[2,192,256]{2,1,0:T(8,128)(2,1)} %get-tuple-element.36.act_ref) | copy-start | bytes 589828
  100.5 47.5 %copy-start.4 = (bf16[2,192,256]{2,1,0:T(8,128)(2,1)S(1)}, bf16[2,192,256]{2,1,0:T(8,128)(2,1)}, u32[]{:S(2)}) copy-start(bf16[2,192,256]{2,1,0:T(8,128)(2,1)} %get-tuple-element.37.dpre_ref) | copy-start | bytes 589828
  101.6 49.7 %all-to-all-start.1 = ((bf16[768,4,128]{2,1,0:T(4,128)(2,1)}), bf16[768,4,128]{2,1,0:T(4,128)(2,1)S(1)}, u32[]{:S(2)}, u32[]{:S(2)}) async-start(bf16[768,4,128]{2,1,0:T(4,128)(2,1)} %bitcast.7), calls=%async_computation.1 | async-start | bytes 1572864 | tf_op jit(solution)/shard_map/all_to_all | solution.py:376
  118.8 29.2 %collective-permute-start.7 = (bf16[2048,128]{1,0:T(8,128)(2,1)}, bf16[2048,128]{1,0:T(8,128)(2,1)S(1)}, u32[]{:S(2)}, u32[]{:S(2)}) collective-permute-start(bf16[2048,128]{1,0:T(8,128)(2,1)} %get-tuple-element.39), channel_id=1, source_target_pairs={{0,8},{1,9},{2,10},{3,11},{4,12},{5,13},{6,14},{7,15},{8,0},{9,1},... | collective-permute-start | bytes 1572872 | tf_op jit(solution)/shard_map/ppermute | solution.py:372
  148.1 1.1 copy-start.2
  149.2 2.1 %copy-start.5 = (f32[128,2]{0,1:T(2,128)S(1)}, f32[128,2]{0,1:T(2,128)}, u32[]{:S(2)}) copy-start(f32[128,2]{0,1:T(2,128)} %param.8) | copy-start | bytes 3076
  149.2 2.1 %copy-start.6 = (s32[2,128]{1,0:T(2,128)S(1)}, s32[2,128]{1,0:T(2,128)}, u32[]{:S(2)}) copy-start(s32[2,128]{1,0:T(2,128)} %get-tuple-element.23.rows_ref) | copy-start | bytes 3076

commit v8 on v7

--- a/solution.py
+++ b/solution.py
@@ -55,13 +55,6 @@
             at += rows
         parts.append((placed, at))
     return parts
-
-
-def travelling(refs, start, rows):
-    early, late = refs
-    if start < early.shape[0]:
-        return early.at[pl.ds(start, rows), :]
-    return late.at[pl.ds(start - early.shape[0], rows), :]
 
 
 def place_kernel(experts, cap, routes_in, gates_in, tok_in, cot_in, in_own, out_own, *refs):
@@ -148,9 +141,9 @@
 
 
 def expert_kernel(used, odd_ref, own, low, high, in_own, out_own, early, late, *rest):
-    ret_own, ret_low, ret_high, x_out, g_out, act_ref, dpre_ref, *share_outs = rest[:9]
-    recv_ref, x_ref, g_ref, in0, in1, out0, out1, held_ref, ret_ref, share_ref = rest[9:19]
-    recv_sems, weight_sems, ret_sems, kept_sems, share_sems = rest[19:]
+    ret_own, ret_low, ret_high, rows_out, own_ref, other_ref = rest[:6]
+    recv_ref, x_ref, g_ref, in0, in1, out0, out1, held_ref, ret_ref = rest[6:15]
+    recv_sems, weight_sems, ret_sems, kept_sems = rest[15:]
     classes, all_rows, width = own.shape
     peers = 2 * classes
     rows = all_rows // 4
@@ -203,8 +196,8 @@
                 start = start + part_rows
                 g_ref[here, at : at + 2 * width] = block[start : start + part_rows, :]
     kept = [
-        pltpu.make_async_copy(x_ref, x_out, kept_sems.at[0]),
-        pltpu.make_async_copy(g_ref, g_out, kept_sems.at[1]),
+        pltpu.make_async_copy(x_ref, rows_out.at[0], kept_sems.at[0]),
+        pltpu.make_async_copy(g_ref, rows_out.at[1], kept_sems.at[1]),
     ]
 
     by_last = ((1,), (1,))
@@ -215,12 +208,12 @@
         value, slope = gelu_parts(dot(x_ref[...], ref[...]))
         acts.append(value.astype(BF16))
         slopes.append(slope)
-        act_ref[group] = acts[group]
+        (own_ref, other_ref)[group][0] = acts[group]
     for group, ref in enumerate((out0, out1)):
         for copy in load_out[group]:
             copy.wait()
         dpres.append((dot(g_ref[...], ref[...], by_last) * slopes[group]).astype(BF16))
-        dpre_ref[group] = dpres[group]
+        (own_ref, other_ref)[group][1] = dpres[group]
     for copy in kept:
         copy.start()
     leave = []
@@ -254,49 +247,21 @@
         )
         leave[-2].start()
         leave[-1].start()
+    for copy in leave + kept:
+        copy.wait()
+
+
+def gradient_kernel(rows_ref, other_rows_ref, own_ref, other_ref, grad_in_ref, grad_out_ref):
     over_rows = ((0,), (0,))
-    model, hidden = in0.shape
-    shares = []
-
-    def share(block, start):
-        for index in range(hidden // width):
-            at = pl.ds(start(index), hidden)
-            share_ref[at, :] = block[:, index * width : (index + 1) * width]
-            target = travelling(share_outs, start(index), hidden)
-            shares.append(
-                pltpu.make_async_copy(share_ref.at[at, :], target, share_sems.at[len(shares)])
-            )
-            shares[-1].start()
-
+    model, hidden = rows_ref.shape[2], own_ref.shape[2]
     for at in range(0, model, hidden):
-        block = dot(x_ref[:, at : at + hidden], dpres[1], over_rows).astype(BF16)
-        share(block, lambda index, at=at: index * model + at)
-        block = dot(acts[1], g_ref[:, at : at + hidden], over_rows).astype(BF16)
-        share(block, lambda index, at=at: hidden // width * model + (at // width + index) * hidden)
-    for copy in leave + kept + shares:
-        copy.wait()
-
-
-def gradient_kernel(x_ref, g_ref, act_ref, dpre_ref, *refs):
-    sent_refs, grad_in_ref, grad_out_ref = refs[:2], refs[2], refs[3]
-    over_rows = ((0,), (0,))
-    model = x_ref.shape[1]
-    hidden, width = dpre_ref.shape[2], sent_refs[0].shape[1]
-    for at in range(0, model, hidden):
-        part = dot(x_ref[:, at : at + hidden], dpre_ref[0], over_rows)
-        for index in range(hidden // width):
-            start = index * model + at
-            cols = slice(index * width, (index + 1) * width)
-            grad_in_ref[0, at : at + hidden, cols] = (
-                part[:, cols] + travelling(sent_refs, start, hidden)[...].astype(F32)
-            ).astype(BF16)
-        part = dot(act_ref[0], g_ref[:, at : at + hidden], over_rows)
-        for index in range(hidden // width):
-            start = hidden // width * model + (at // width + index) * hidden
-            cols = slice(index * width, (index + 1) * width)
-            grad_out_ref[0, :, at + index * width : at + (index + 1) * width] = (
-                part[:, cols] + travelling(sent_refs, start, hidden)[...].astype(F32)
-            ).astype(BF16)
+        cols = slice(at, at + hidden)
+        part = dot(rows_ref[0, :, cols], own_ref[1], over_rows)
+        part = part + dot(other_rows_ref[0, :, cols], other_ref[1], over_rows)
+        grad_in_ref[0, cols, :] = part.astype(BF16)
+        part = dot(own_ref[0], rows_ref[1, :, cols], over_rows)
+        part = part + dot(other_ref[0], other_rows_ref[1, :, cols], over_rows)
+        grad_out_ref[0, :, cols] = part.astype(BF16)
 
 
 def add_kernel(own_ref, low_ref, high_ref, out_ref):
@@ -419,21 +384,18 @@
     recv, early = lax.optimization_barrier((recv, early))
     low = lax.ppermute(recv[:side], "cuts", up)
     high = lax.ppermute(recv[side:], "cuts", down)
-    ret_own, ret_low, ret_high, held_x, held_g, active, dpre, grads, late_grads = call(
+    ret_own, ret_low, ret_high, held_rows, own_units, other_units = call(
         functools.partial(expert_kernel, used),
         (
             struct(classes, all_rows, width),
             struct(side, all_rows, width),
             struct(classes - side, all_rows, width),
-            struct(rows, model),
-            struct(rows, model),
+            struct(2, rows, model),
             struct(2, rows, hidden),
             struct(2, rows, hidden),
-            struct(early_rows, width),
-            struct(late_rows, width),
         ),
         (16 * rows * model * hidden, 12 * rows * model + 8 * model * hidden),
-        ([pltpu.SMEM] + [far] * 7, [far] * 5 + [near] * 2 + [far] * 2),
+        ([pltpu.SMEM] + [far] * 7, [far] * 4 + [near] * 2),
         60,
         [
             pltpu.VMEM((all_rows, peers * width), BF16),
@@ -445,12 +407,10 @@
             pltpu.VMEM((hidden, model), BF16),
             pltpu.VMEM((all_rows, 2 * width), BF16),
             pltpu.VMEM((all_rows, peers * width), BF16),
-            pltpu.VMEM((early_rows + late_rows, width), BF16),
             dma((peers,)),
             dma((2 + blocks,)),
             dma((peers,)),
             dma((2,)),
-            dma((2 * model // hidden * (hidden // width),)),
         ],
         odd,
         recv,
@@ -463,7 +423,7 @@
     )
     from_low = lax.ppermute(ret_low, "cuts", up)
     from_high = lax.ppermute(ret_high, "cuts", down)
-    grads, late_grads = to_partner(grads), to_partner(late_grads)
+    partner_rows, partner_units = to_partner(held_rows), to_partner(other_units)
     summed = call(
         add_kernel,
         (struct(classes, all_rows, width),),
@@ -479,16 +439,14 @@
     grad_in, grad_out = call(
         gradient_kernel,
         (struct(1, model, hidden), struct(1, hidden, model)),
-        (8 * rows * model * hidden, 16 * model * hidden),
-        ([near] * 6, [near] * 2),
+        (16 * rows * model * hidden, 16 * model * hidden),
+        ([near] * 4, [near] * 2),
         32,
         [],
-        held_x,
-        held_g,
-        active,
-        dpre,
-        grads,
-        late_grads,
+        held_rows,
+        partner_rows,
+        own_units,
+        partner_units,
     )
     mixed, token_grad = call(
         functools.partial(combine_kernel, used),

time: 154 us -> 149 us (0.968)
  waiting for transfers between devices: 66.8 us -> 62.7 us
    ppermute x4, waiting for transfers between devices: 25.9 us -> 18.7 us  [to_partner(): return lax.ppermute(value, 'cuts', swap)]
    all_to_all x2, waiting for transfers between devices: 25.7 us -> 28.8 us  [over_spread(): lax.all_to_all(pieces, ('dp', 'cuts'), 0, 0, tiled=True, axis_index_group...]
  transfers between devices with their start and end apart: 10 -> 10, of which waited for: 6 -> 7; matrix products, arithmetic and copies ran while one was open for 0% -> 0% of each run, Pallas kernels for 2% -> 3%
where the time goes in v8:
time: 149 us; the launch traced here: 148 us
  starting transfers between devices  63.5 us (43%)
  waiting for transfers between devices  62.7 us (42%)
  Pallas kernels  19.9 us (13%)
    all_to_all x2, starting transfers between devices, over_spread(): lax.all_to_all(pieces, ('dp', 'cuts'), 0, 0, tiled=True, axis_index_group...  38.8 us
    all_to_all x2, waiting for transfers between devices, over_spread(): lax.all_to_all(pieces, ('dp', 'cuts'), 0, 0, tiled=True, axis_index_group...  28.8 us
    pallas_call x5, Pallas kernels, call(): pl.pallas_call(kernel, out_shape=shapes, in_specs=[pl.BlockSpec(memory_sp...  19.9 us
    ppermute x4, waiting for transfers between devices, to_partner(): return lax.ppermute(value, 'cuts', swap)  18.7 us
    ppermute x4, starting transfers between devices, to_partner(): return lax.ppermute(value, 'cuts', swap)  12.9 us
    ppermute x1, waiting for transfers between devices, body(): high = lax.ppermute(recv[side:], 'cuts', down)  7.15 us
    ppermute x1, starting transfers between devices, body(): from_high = lax.ppermute(ret_high, 'cuts', down)  4.57 us
    ppermute x1, waiting for transfers between devices, body(): from_low = lax.ppermute(ret_low, 'cuts', up)  3.92 us
  transfers between devices with their start and end apart: 10, of which 7 were waited for; matrix products, arithmetic and copies ran while one was open for 0% of the time, Pallas kernels for 3%

profile of v8, /device:TPU:1, one launch (start us, length us, event | category | flops | bytes accessed | tf_op | source)
XLA Modules:
  0.0 148.0 jit_solution(841139204534260771)
XLA Ops:
  0.6 4.0 %shard_map.93 = (bf16[4,768,128]{2,1,0:T(8,128)(2,1)}, s32[2,128]{1,0:T(2,128)}, bf16[6144,128]{1,0:T(8,128)(2,1)}, bf16[2048,128]{1,0:T(8,128)(2,1)}) custom-call(s32[2,128]{1,0:T(2,128)} %bitcast.19, f32[2,128]{1,0:T(2,128)} %bitcast.10, bf16[128,128]{1,0:T(8,128)(2,1)} %tok_in.1, bf16[128,128]{1,0:T(8,128)(2,1)} %cot_in.1, bf16[2048,256]{1,0:T(8,128)(2,1)} %bitcast.14, ...), custom_call_target="tpu_custom_call" | custom-call | flops 50331648 | bytes 1572864 | tf_op jit(solution)/shard_map/pallas_call | solution.py:298
  4.6 3.9 %collective-permute-start = (bf16[6144,128]{1,0:T(8,128)(2,1)}, bf16[6144,128]{1,0:T(8,128)(2,1)S(1)}, u32[]{:S(2)}, u32[]{:S(2)}) collective-permute-start(bf16[6144,128]{1,0:T(8,128)(2,1)} %get-tuple-element.22), channel_id=1, source_target_pairs={{0,8},{1,9},{2,10},{3,11},{4,12},{5,13},{6,14},{7,15},{8,0},{9,1},... | collective-permute-start | bytes 4718600 | tf_op jit(solution)/shard_map/ppermute | solution.py:337
  8.6 21.6 %all-to-all-start = ((bf16[768,4,128]{2,1,0:T(4,128)(2,1)}), bf16[768,4,128]{2,1,0:T(4,128)(2,1)S(1)}, u32[]{:S(2)}, u32[]{:S(2)}) async-start(bf16[768,4,128]{2,1,0:T(4,128)(2,1)} %bitcast.18), calls=%async_computation | async-start | bytes 1572864 | tf_op jit(solution)/shard_map/all_to_all | solution.py:341
  30.2 3.3 %collective-permute-start.3 = (bf16[2048,128]{1,0:T(8,128)(2,1)}, bf16[2048,128]{1,0:T(8,128)(2,1)}, u32[]{:S(2)}, u32[]{:S(2)}) collective-permute-start(bf16[2048,128]{1,0:T(8,128)(2,1)} %get-tuple-element.25), channel_id=1, source_target_pairs={{0,8},{1,9},{2,10},{3,11},{4,12},{5,13},{6,14},{7,15},{8,0},{9,1},... | collective-permute-start | bytes 1572872 | tf_op jit(solution)/shard_map/ppermute | solution.py:337
  33.5 25.7 %all-to-all-done = bf16[768,4,128]{2,1,0:T(4,128)(2,1)S(1)} async-done(((bf16[768,4,128]{2,1,0:T(4,128)(2,1)}), bf16[768,4,128]{2,1,0:T(4,128)(2,1)S(1)}, u32[]{:S(2)}, u32[]{:S(2)}) %all-to-all-start) | async-done | bytes 786464 | tf_op jit(solution)/shard_map/all_to_all | solution.py:341
  59.1 0.0 collective-permute-done.early
  59.1 0.1 fusion
  59.2 1.9 %collective-permute-start.2 = (bf16[2,768,128]{2,1,0:T(8,128)(2,1)S(1)}, bf16[2,768,128]{2,1,0:T(8,128)(2,1)S(1)}, u32[]{:S(2)}, u32[]{:S(2)}) collective-permute-start(bf16[2,768,128]{2,1,0:T(8,128)(2,1)S(1)} %get-tuple-element.36), channel_id=1, source_target_pairs={{1,0},{2,1},{3,2},{4,3},{5,4},{6,5},{7,6},{0,7},{9,8},{10,9},{11,1... | collective-permute-start | bytes 1179656 | tf_op jit(solution)/shard_map/ppermute | solution.py:386
  61.1 3.4 %collective-permute-start.1 = (bf16[2,768,128]{2,1,0:T(8,128)(2,1)S(1)}, bf16[2,768,128]{2,1,0:T(8,128)(2,1)}, u32[]{:S(2)}, u32[]{:S(2)}) collective-permute-start(bf16[2,768,128]{2,1,0:T(8,128)(2,1)S(1)} %get-tuple-element.37), channel_id=1, source_target_pairs={{0,1},{1,2},{2,3},{3,4},{4,5},{5,6},{6,7},{7,0},{8,9},{9,10},{10,1... | collective-permute-start | bytes 1179656 | tf_op jit(solution)/shard_map/ppermute | solution.py:385
  64.5 0.0 collective-permute-done.3.late
  64.5 7.2 %collective-permute-done.2.high = bf16[2,768,128]{2,1,0:T(8,128)(2,1)S(1)} collective-permute-done((bf16[2,768,128]{2,1,0:T(8,128)(2,1)S(1)}, bf16[2,768,128]{2,1,0:T(8,128)(2,1)S(1)}, u32[]{:S(2)}, u32[]{:S(2)}) %collective-permute-start.2) | collective-permute-done | bytes 393248 | tf_op jit(solution)/shard_map/ppermute | solution.py:386
  71.7 3.1 %collective-permute-done.1.low = bf16[2,768,128]{2,1,0:T(8,128)(2,1)} collective-permute-done((bf16[2,768,128]{2,1,0:T(8,128)(2,1)S(1)}, bf16[2,768,128]{2,1,0:T(8,128)(2,1)}, u32[]{:S(2)}, u32[]{:S(2)}) %collective-permute-start.1) | collective-permute-done | bytes 393248 | tf_op jit(solution)/shard_map/ppermute | solution.py:385
  74.7 0.0 copy-done.5
  74.7 0.0 copy-done.6
  74.8 9.3 %shard_map.94 = (bf16[4,768,128]{2,1,0:T(8,128)(2,1)}, bf16[2,768,128]{2,1,0:T(8,128)(2,1)}, bf16[2,768,128]{2,1,0:T(8,128)(2,1)}, bf16[2,192,2048]{2,1,0:T(8,12...) custom-call(s32[1]{0:T(128)} %bitcast.4.odd_ref, bf16[4,768,128]{2,1,0:T(8,128)(2,1)} %bitcast.13, ...), custom_call_target="tpu_custom_call" | custom-call | flops 1610612736 | bytes 8912896 | tf_op jit(solution)/shard_map/pallas_call | solution.py:298
  84.0 1.9 %collective-permute-start.4 = (bf16[2,768,128]{2,1,0:T(8,128)(2,1)}, bf16[2,768,128]{2,1,0:T(8,128)(2,1)S(1)}, u32[]{:S(2)}, u32[]{:S(2)}) collective-permute-start(bf16[2,768,128]{2,1,0:T(8,128)(2,1)} %get-tuple-element.27), channel_id=1, source_target_pairs={{0,1},{1,2},{2,3},{3,4},{4,5},{5,6},{6,7},{7,0},{8,9},{9,10},{10,1... | collective-permute-start | bytes 1179656 | tf_op jit(solution)/shard_map/ppermute | solution.py:424
  85.9 4.6 %collective-permute-start.5 = (bf16[2,768,128]{2,1,0:T(8,128)(2,1)}, bf16[2,768,128]{2,1,0:T(8,128)(2,1)S(1)}, u32[]{:S(2)}, u32[]{:S(2)}) collective-permute-start(bf16[2,768,128]{2,1,0:T(8,128)(2,1)} %get-tuple-element.28), channel_id=1, source_target_pairs={{1,0},{2,1},{3,2},{4,3},{5,4},{6,5},{7,6},{0,7},{9,8},{10,9},{11,1... | collective-permute-start | bytes 1179656 | tf_op jit(solution)/shard_map/ppermute | solution.py:425
  90.5 2.4 %collective-permute-start.6 = (bf16[2,192,2048]{2,1,0:T(8,128)(2,1)}, bf16[2,192,2048]{2,1,0:T(8,128)(2,1)}, u32[]{:S(2)}, u32[]{:S(2)}) collective-permute-start(bf16[2,192,2048]{2,1,0:T(8,128)(2,1)} %get-tuple-element.31.rows_ref), channel_id=1, source_target_pairs={{0,8},{1,9},{2,10},{3,11},{4,12},{5,13},{6,14},{7,15},{8,0},{9,1},... | collective-permute-start | bytes 4718600 | tf_op jit(solution)/shard_map/ppermute | solution.py:337
  92.9 3.9 %collective-permute-done.4.low_ref = bf16[2,768,128]{2,1,0:T(8,128)(2,1)S(1)} collective-permute-done((bf16[2,768,128]{2,1,0:T(8,128)(2,1)}, bf16[2,768,128]{2,1,0:T(8,128)(2,1)S(1)}, u32[]{:S(2)}, u32[]{:S(2)}) %collective-permute-start.4) | collective-permute-done | bytes 393248 | tf_op jit(solution)/shard_map/ppermute | solution.py:424
  96.8 1.0 collective-permute-done.5.high_ref
  97.8 1.1 copy-done
  99.0 1.1 shard_map.95
  100.1 17.2 %all-to-all-start.1 = ((bf16[768,4,128]{2,1,0:T(4,128)(2,1)}), bf16[768,4,128]{2,1,0:T(4,128)(2,1)S(1)}, u32[]{:S(2)}, u32[]{:S(2)}) async-start(bf16[768,4,128]{2,1,0:T(4,128)(2,1)} %bitcast.7), calls=%async_computation.1 | async-start | bytes 1572864 | tf_op jit(solution)/shard_map/all_to_all | solution.py:341
  117.3 3.3 %collective-permute-start.7 = (bf16[2,192,256]{2,1,0:T(8,128)(2,1)S(1)}, bf16[2,192,256]{2,1,0:T(8,128)(2,1)S(1)}, u32[]{:S(2)}, u32[]{:S(2)}) collective-permute-start(bf16[2,192,256]{2,1,0:T(8,128)(2,1)S(1)} %copy-done.8), channel_id=1, source_target_pairs={{0,8},{1,9},{2,10},{3,11},{4,12},{5,13},{6,14},{7,15},{8,0},{9,1},... | collective-permute-start | bytes 589832 | tf_op jit(solution)/shard_map/ppermute | solution.py:337
  120.6 18.7 %collective-permute-done.7.other_ref = bf16[2,192,256]{2,1,0:T(8,128)(2,1)S(1)} collective-permute-done((bf16[2,192,256]{2,1,0:T(8,128)(2,1)S(1)}, bf16[2,192,256]{2,1,0:T(8,128)(2,1)S(1)}, u32[]{:S(2)}, u32[]{:S(2)}) %collective-permute-start.7) | collective-permute-done | bytes 196640 | tf_op jit(solution)/shard_map/ppermute | solution.py:337
  139.3 0.0 collective-permute-done.6.other_rows_ref
  139.3 0.0 copy-start.1
  139.3 0.0 copy-start.3
  139.3 4.1 %shard_map.97 = (bf16[1,2048,256]{2,1,0:T(8,128)(2,1)}, bf16[1,256,2048]{2,1,0:T(8,128)(2,1)}) custom-call(bf16[2,192,2048]{2,1,0:T(8,128)(2,1)S(1)} %copy-done.2, bf16[2,192,2048]{2,1,0:T(8,128)(2,1)} %collective-permute-done.6.other_rows_ref, bf16[2,192,256]{2,1,0:T(8,128)(2,1)S(1)} %copy-done.4, bf16[2,192,256]{2,1,0:T(8,128)(2,1)S(1)} %collective-permute-done.7.other_ref), custom_call_target="tpu_custom_call" | custom-call | flops 1610612736 | bytes 8388608 | tf_op jit(solution)/shard_map/pallas_call | solution.py:298
  143.4 3.1 %all-to-all-done.1 = bf16[768,4,128]{2,1,0:T(4,128)(2,1)S(1)} async-done(((bf16[768,4,128]{2,1,0:T(4,128)(2,1)}), bf16[768,4,128]{2,1,0:T(4,128)(2,1)S(1)}, u32[]{:S(2)}, u32[]{:S(2)}) %all-to-all-start.1) | async-done | bytes 786464 | tf_op jit(solution)/shard_map/all_to_all | solution.py:341
  146.6 0.0 copy-done.1
  146.6 1.5 shard_map.96
  (12 shorter events, 0.0 us)
Async XLA Ops:
  4.6 54.5 %collective-permute-start = (bf16[6144,128]{1,0:T(8,128)(2,1)}, bf16[6144,128]{1,0:T(8,128)(2,1)S(1)}, u32[]{:S(2)}, u32[]{:S(2)}) collective-permute-start(bf16[6144,128]{1,0:T(8,128)(2,1)} %get-tuple-element.22), channel_id=1, source_target_pairs={{0,8},{1,9},{2,10},{3,11},{4,12},{5,13},{6,14},{7,15},{8,0},{9,1},... | collective-permute-start | bytes 4718600 | tf_op jit(solution)/shard_map/ppermute | solution.py:337
  8.6 50.5 %all-to-all-start = ((bf16[768,4,128]{2,1,0:T(4,128)(2,1)}), bf16[768,4,128]{2,1,0:T(4,128)(2,1)S(1)}, u32[]{:S(2)}, u32[]{:S(2)}) async-start(bf16[768,4,128]{2,1,0:T(4,128)(2,1)} %bitcast.18), calls=%async_computation | async-start | bytes 1572864 | tf_op jit(solution)/shard_map/all_to_all | solution.py:341
  30.2 34.3 %collective-permute-start.3 = (bf16[2048,128]{1,0:T(8,128)(2,1)}, bf16[2048,128]{1,0:T(8,128)(2,1)}, u32[]{:S(2)}, u32[]{:S(2)}) collective-permute-start(bf16[2048,128]{1,0:T(8,128)(2,1)} %get-tuple-element.25), channel_id=1, source_target_pairs={{0,8},{1,9},{2,10},{3,11},{4,12},{5,13},{6,14},{7,15},{8,0},{9,1},... | collective-permute-start | bytes 1572872 | tf_op jit(solution)/shard_map/ppermute | solution.py:337
  59.1 15.6 %copy-start.5 = (bf16[768,4,128]{2,1,0:T(4,128)(2,1)}, bf16[768,4,128]{2,1,0:T(4,128)(2,1)S(1)}, u32[]{:S(2)}) copy-start(bf16[768,4,128]{2,1,0:T(4,128)(2,1)S(1)} %all-to-all-done) | copy-start | bytes 2359300
  59.1 15.6 %copy-start.6 = (bf16[6144,128]{1,0:T(8,128)(2,1)}, bf16[6144,128]{1,0:T(8,128)(2,1)S(1)}, u32[]{:S(2)}) copy-start(bf16[6144,128]{1,0:T(8,128)(2,1)S(1)} %collective-permute-done.early) | copy-start | bytes 4718596
  59.2 12.5 %collective-permute-start.2 = (bf16[2,768,128]{2,1,0:T(8,128)(2,1)S(1)}, bf16[2,768,128]{2,1,0:T(8,128)(2,1)S(1)}, u32[]{:S(2)}, u32[]{:S(2)}) collective-permute-start(bf16[2,768,128]{2,1,0:T(8,128)(2,1)S(1)} %get-tuple-element.36), channel_id=1, source_target_pairs={{1,0},{2,1},{3,2},{4,3},{5,4},{6,5},{7,6},{0,7},{9,8},{10,9},{11,1... | collective-permute-start | bytes 1179656 | tf_op jit(solution)/shard_map/ppermute | solution.py:386
  61.1 13.6 %collective-permute-start.1 = (bf16[2,768,128]{2,1,0:T(8,128)(2,1)S(1)}, bf16[2,768,128]{2,1,0:T(8,128)(2,1)}, u32[]{:S(2)}, u32[]{:S(2)}) collective-permute-start(bf16[2,768,128]{2,1,0:T(8,128)(2,1)S(1)} %get-tuple-element.37), channel_id=1, source_target_pairs={{0,1},{1,2},{2,3},{3,4},{4,5},{5,6},{6,7},{7,0},{8,9},{9,10},{10,1... | collective-permute-start | bytes 1179656 | tf_op jit(solution)/shard_map/ppermute | solution.py:385
  71.7 3.1 %copy-start.7 = (bf16[2,768,128]{2,1,0:T(8,128)(2,1)}, bf16[2,768,128]{2,1,0:T(8,128)(2,1)S(1)}, u32[]{:S(2)}) copy-start(bf16[2,768,128]{2,1,0:T(8,128)(2,1)S(1)} %collective-permute-done.2.high) | copy-start | bytes 1179652
  84.0 12.8 %collective-permute-start.4 = (bf16[2,768,128]{2,1,0:T(8,128)(2,1)}, bf16[2,768,128]{2,1,0:T(8,128)(2,1)S(1)}, u32[]{:S(2)}, u32[]{:S(2)}) collective-permute-start(bf16[2,768,128]{2,1,0:T(8,128)(2,1)} %get-tuple-element.27), channel_id=1, source_target_pairs={{0,1},{1,2},{2,3},{3,4},{4,5},{5,6},{6,7},{7,0},{8,9},{9,10},{10,1... | collective-permute-start | bytes 1179656 | tf_op jit(solution)/shard_map/ppermute | solution.py:424
  85.9 11.9 %collective-permute-start.5 = (bf16[2,768,128]{2,1,0:T(8,128)(2,1)}, bf16[2,768,128]{2,1,0:T(8,128)(2,1)S(1)}, u32[]{:S(2)}, u32[]{:S(2)}) collective-permute-start(bf16[2,768,128]{2,1,0:T(8,128)(2,1)} %get-tuple-element.28), channel_id=1, source_target_pairs={{1,0},{2,1},{3,2},{4,3},{5,4},{6,5},{7,6},{0,7},{9,8},{10,9},{11,1... | collective-permute-start | bytes 1179656 | tf_op jit(solution)/shard_map/ppermute | solution.py:425
  90.5 48.8 %collective-permute-start.6 = (bf16[2,192,2048]{2,1,0:T(8,128)(2,1)}, bf16[2,192,2048]{2,1,0:T(8,128)(2,1)}, u32[]{:S(2)}, u32[]{:S(2)}) collective-permute-start(bf16[2,192,2048]{2,1,0:T(8,128)(2,1)} %get-tuple-element.31.rows_ref), channel_id=1, source_target_pairs={{0,8},{1,9},{2,10},{3,11},{4,12},{5,13},{6,14},{7,15},{8,0},{9,1},... | collective-permute-start | bytes 4718600 | tf_op jit(solution)/shard_map/ppermute | solution.py:337
  97.8 1.1 copy-start
  99.0 18.3 %copy-start.8 = (bf16[2,192,256]{2,1,0:T(8,128)(2,1)S(1)}, bf16[2,192,256]{2,1,0:T(8,128)(2,1)}, u32[]{:S(2)}) copy-start(bf16[2,192,256]{2,1,0:T(8,128)(2,1)} %get-tuple-element.33) | copy-start | bytes 589828
  99.0 40.3 %copy-start.2 = (bf16[2,192,2048]{2,1,0:T(8,128)(2,1)S(1)}, bf16[2,192,2048]{2,1,0:T(8,128)(2,1)}, u32[]{:S(2)}) copy-start(bf16[2,192,2048]{2,1,0:T(8,128)(2,1)} %get-tuple-element.31.rows_ref) | copy-start | bytes 4718596
  99.0 40.3 %copy-start.4 = (bf16[2,192,256]{2,1,0:T(8,128)(2,1)S(1)}, bf16[2,192,256]{2,1,0:T(8,128)(2,1)}, u32[]{:S(2)}) copy-start(bf16[2,192,256]{2,1,0:T(8,128)(2,1)} %get-tuple-element.32.own_ref) | copy-start | bytes 589828
  100.1 46.5 %all-to-all-start.1 = ((bf16[768,4,128]{2,1,0:T(4,128)(2,1)}), bf16[768,4,128]{2,1,0:T(4,128)(2,1)S(1)}, u32[]{:S(2)}, u32[]{:S(2)}) async-start(bf16[768,4,128]{2,1,0:T(4,128)(2,1)} %bitcast.7), calls=%async_computation.1 | async-start | bytes 1572864 | tf_op jit(solution)/shard_map/all_to_all | solution.py:341
  117.3 22.0 %collective-permute-start.7 = (bf16[2,192,256]{2,1,0:T(8,128)(2,1)S(1)}, bf16[2,192,256]{2,1,0:T(8,128)(2,1)S(1)}, u32[]{:S(2)}, u32[]{:S(2)}) collective-permute-start(bf16[2,192,256]{2,1,0:T(8,128)(2,1)S(1)} %copy-done.8), channel_id=1, source_target_pairs={{0,8},{1,9},{2,10},{3,11},{4,12},{5,13},{6,14},{7,15},{8,0},{9,1},... | collective-permute-start | bytes 589832 | tf_op jit(solution)/shard_map/ppermute | solution.py:337
  139.3 7.2 %copy-start.1 = (f32[128,2]{0,1:T(2,128)S(1)}, f32[128,2]{0,1:T(2,128)}, u32[]{:S(2)}) copy-start(f32[128,2]{0,1:T(2,128)} %param.8) | copy-start | bytes 3076
  139.3 7.2 %copy-start.3 = (s32[2,128]{1,0:T(2,128)S(1)}, s32[2,128]{1,0:T(2,128)}, u32[]{:S(2)}) copy-start(s32[2,128]{1,0:T(2,128)} %get-tuple-element.20.rows_ref) | copy-start | bytes 3076

commit v9 on v8

--- a/solution.py
+++ b/solution.py
@@ -12,6 +12,7 @@
 F32 = jnp.float32
 HALVES = 2
 EARLY = (1, 2)
+PIECES = 4
 GROUP = 8
 FOUR = 4
 
@@ -57,6 +58,18 @@
     return parts
 
 
+def in_pieces(source, target, sems, first):
+    rows = source.shape[0] // PIECES
+    return [
+        pltpu.make_async_copy(
+            source.at[pl.ds(index * rows, rows), :],
+            target.at[pl.ds(index * rows, rows), :],
+            sems.at[first + index],
+        )
+        for index in range(PIECES)
+    ]
+
+
 def place_kernel(experts, cap, routes_in, gates_in, tok_in, cot_in, in_own, out_own, *refs):
     sent, rows_ref, early, late = refs[:4]
     scratch = refs[4:]
@@ -70,10 +83,7 @@
     ]
     for copy in copies:
         copy.start()
-    loads = [
-        pltpu.make_async_copy(in_own, in_ref, load_sems.at[0]),
-        pltpu.make_async_copy(out_own, out_ref, load_sems.at[1]),
-    ]
+    loads = in_pieces(in_own, in_ref, load_sems, 0) + in_pieces(out_own, out_ref, load_sems, PIECES)
     for copy in loads:
         copy.start()
     copies[0].wait()
@@ -141,8 +151,8 @@
 
 
 def expert_kernel(used, odd_ref, own, low, high, in_own, out_own, early, late, *rest):
-    ret_own, ret_low, ret_high, rows_out, own_ref, other_ref = rest[:6]
-    recv_ref, x_ref, g_ref, in0, in1, out0, out1, held_ref, ret_ref = rest[6:15]
+    ret_own, ret_low, ret_high, rows_out, own_ref = rest[:5]
+    recv_ref, x_ref, g_ref, in0, in1, out0, out1, held_ref, ret_ref, other_ref = rest[5:15]
     recv_sems, weight_sems, ret_sems, kept_sems = rest[15:]
     classes, all_rows, width = own.shape
     peers = 2 * classes
@@ -162,12 +172,12 @@
         pltpu.make_async_copy(ref.at[q], recv_ref.at[:, cols], recv_sems.at[index])
         for index, (ref, q, cols) in enumerate(moves)
     ]
-    load_in = [[pltpu.make_async_copy(in_own, in0, weight_sems.at[0])], []]
-    load_out = [[pltpu.make_async_copy(out_own, out0, weight_sems.at[1])], []]
+    load_in = [in_pieces(in_own, in0, weight_sems, 0), []]
+    load_out = [in_pieces(out_own, out0, weight_sems, PIECES), []]
     for (placed, _), source in zip(split_blocks(*reversed(in0.shape), width), (early, late)):
         for which, first, at, size in placed:
             target = (in1, out1)[which].at[:, pl.ds(first, width)]
-            index = 2 + len(load_in[1]) + len(load_out[1])
+            index = 2 * PIECES + len(load_in[1]) + len(load_out[1])
             (load_in, load_out)[which][1].append(
                 pltpu.make_async_copy(
                     source.at[pl.ds(at, size), :], target, weight_sems.at[index]
@@ -195,9 +205,21 @@
                 x_ref[here, at : at + 2 * width] = block[start : start + part_rows, :]
                 start = start + part_rows
                 g_ref[here, at : at + 2 * width] = block[start : start + part_rows, :]
+    model, hidden = in0.shape
     kept = [
-        pltpu.make_async_copy(x_ref, rows_out.at[0], kept_sems.at[0]),
-        pltpu.make_async_copy(g_ref, rows_out.at[1], kept_sems.at[1]),
+        pltpu.make_async_copy(
+            ref.at[:, pl.ds(at, model // PIECES)],
+            rows_out.at[kind, :, pl.ds(at, model // PIECES)],
+            kept_sems.at[kind, at * PIECES // model],
+        )
+        for kind, ref in enumerate((x_ref, g_ref))
+        for at in range(0, model, model // PIECES)
+    ]
+    kept += [
+        pltpu.make_async_copy(
+            other_ref.at[kind], rows_out.at[kind, :, pl.ds(model, hidden)], kept_sems.at[kind, PIECES]
+        )
+        for kind in range(2)
     ]
 
     by_last = ((1,), (1,))
@@ -251,16 +273,18 @@
         copy.wait()
 
 
-def gradient_kernel(rows_ref, other_rows_ref, own_ref, other_ref, grad_in_ref, grad_out_ref):
+def gradient_kernel(rows_ref, other_ref, own_ref, grad_in_ref, grad_out_ref):
     over_rows = ((0,), (0,))
-    model, hidden = rows_ref.shape[2], own_ref.shape[2]
+    hidden = own_ref.shape[2]
+    model = rows_ref.shape[2] - hidden
+    units = slice(model, model + hidden)
     for at in range(0, model, hidden):
         cols = slice(at, at + hidden)
         part = dot(rows_ref[0, :, cols], own_ref[1], over_rows)
-        part = part + dot(other_rows_ref[0, :, cols], other_ref[1], over_rows)
+        part = part + dot(other_ref[0, :, cols], other_ref[1, :, units], over_rows)
         grad_in_ref[0, cols, :] = part.astype(BF16)
         part = dot(own_ref[0], rows_ref[1, :, cols], over_rows)
-        part = part + dot(other_ref[0], other_rows_ref[1, :, cols], over_rows)
+        part = part + dot(other_ref[0, :, units], other_ref[1, :, cols], over_rows)
         grad_out_ref[0, :, cols] = part.astype(BF16)
 
 
@@ -369,7 +393,7 @@
             pltpu.VMEM((hidden, model), BF16),
             dma((4,)),
             dma((classes,)),
-            dma((2,)),
+            dma((2 * PIECES,)),
             dma((blocks,)),
         ],
         routes_t,
@@ -384,18 +408,17 @@
     recv, early = lax.optimization_barrier((recv, early))
     low = lax.ppermute(recv[:side], "cuts", up)
     high = lax.ppermute(recv[side:], "cuts", down)
-    ret_own, ret_low, ret_high, held_rows, own_units, other_units = call(
+    ret_own, ret_low, ret_high, held_rows, own_units = call(
         functools.partial(expert_kernel, used),
         (
             struct(classes, all_rows, width),
             struct(side, all_rows, width),
             struct(classes - side, all_rows, width),
-            struct(2, rows, model),
-            struct(2, rows, hidden),
+            struct(2, rows, model + hidden),
             struct(2, rows, hidden),
         ),
         (16 * rows * model * hidden, 12 * rows * model + 8 * model * hidden),
-        ([pltpu.SMEM] + [far] * 7, [far] * 4 + [near] * 2),
+        ([pltpu.SMEM] + [far] * 7, [far] * 4 + [near]),
         60,
         [
             pltpu.VMEM((all_rows, peers * width), BF16),
@@ -407,10 +430,11 @@
             pltpu.VMEM((hidden, model), BF16),
             pltpu.VMEM((all_rows, 2 * width), BF16),
             pltpu.VMEM((all_rows, peers * width), BF16),
+            pltpu.VMEM((2, rows, hidden), BF16),
             dma((peers,)),
-            dma((2 + blocks,)),
+            dma((2 * PIECES + blocks,)),
             dma((peers,)),
-            dma((2,)),
+            dma((2, PIECES + 1)),
         ],
         odd,
         recv,
@@ -423,7 +447,7 @@
     )
     from_low = lax.ppermute(ret_low, "cuts", up)
     from_high = lax.ppermute(ret_high, "cuts", down)
-    partner_rows, partner_units = to_partner(held_rows), to_partner(other_units)
+    partner_rows = to_partner(held_rows)
     summed = call(
         add_kernel,
         (struct(classes, all_rows, width),),
@@ -440,13 +464,12 @@
         gradient_kernel,
         (struct(1, model, hidden), struct(1, hidden, model)),
         (16 * rows * model * hidden, 16 * model * hidden),
-        ([near] * 4, [near] * 2),
+        ([near] * 3, [near] * 2),
         32,
         [],
         held_rows,
         partner_rows,
         own_units,
-        partner_units,
     )
     mixed, token_grad = call(
         functools.partial(combine_kernel, used),

time: 149 us -> 149 us (level)
  starting transfers between devices: 63.5 us -> 60.2 us
  waiting for transfers between devices: 62.7 us -> 65.9 us
    ppermute x4 -> x3, starting transfers between devices: 12.9 us -> 9.64 us  [to_partner(): return lax.ppermute(value, 'cuts', swap)]
    ppermute x4 -> x3, waiting for transfers between devices: 18.7 us -> 21.8 us  [to_partner(): return lax.ppermute(value, 'cuts', swap)]
  transfers between devices with their start and end apart: 10 -> 9, of which waited for: 7 -> 7; matrix products, arithmetic and copies ran while one was open for 0% -> 0% of each run, Pallas kernels for 3% -> 4%
where the time goes in v9:
time: 149 us; the launch traced here: 148 us
  waiting for transfers between devices  65.9 us (44%)
  starting transfers between devices  60.2 us (40%)
  Pallas kernels  20.1 us (13%)
    all_to_all x2, starting transfers between devices, over_spread(): lax.all_to_all(pieces, ('dp', 'cuts'), 0, 0, tiled=True, axis_index_group...  38.8 us
    all_to_all x2, waiting for transfers between devices, over_spread(): lax.all_to_all(pieces, ('dp', 'cuts'), 0, 0, tiled=True, axis_index_group...  29 us
    ppermute x3, waiting for transfers between devices, to_partner(): return lax.ppermute(value, 'cuts', swap)  21.8 us
    pallas_call x5, Pallas kernels, call(): pl.pallas_call(kernel, out_shape=shapes, in_specs=[pl.BlockSpec(memory_sp...  20.1 us
    ppermute x3, starting transfers between devices, to_partner(): return lax.ppermute(value, 'cuts', swap)  9.64 us
    ppermute x1, waiting for transfers between devices, body(): high = lax.ppermute(recv[side:], 'cuts', down)  7.15 us
    ppermute x1, starting transfers between devices, body(): from_high = lax.ppermute(ret_high, 'cuts', down)  4.57 us
    ppermute x1, waiting for transfers between devices, body(): from_low = lax.ppermute(ret_low, 'cuts', up)  3.88 us
  transfers between devices with their start and end apart: 9, of which 7 were waited for; matrix products, arithmetic and copies ran while one was open for 0% of the time, Pallas kernels for 4%

profile of v9, /device:TPU:1, one launch (start us, length us, event | category | flops | bytes accessed | tf_op | source)
XLA Modules:
  0.0 148.2 jit_solution(2609779634359672061)
XLA Ops:
  0.6 4.0 %shard_map.93 = (bf16[4,768,128]{2,1,0:T(8,128)(2,1)}, s32[2,128]{1,0:T(2,128)}, bf16[6144,128]{1,0:T(8,128)(2,1)}, bf16[2048,128]{1,0:T(8,128)(2,1)}) custom-call(s32[2,128]{1,0:T(2,128)} %bitcast.19, f32[2,128]{1,0:T(2,128)} %bitcast.10, bf16[128,128]{1,0:T(8,128)(2,1)} %tok_in.1, bf16[128,128]{1,0:T(8,128)(2,1)} %cot_in.1, bf16[2048,256]{1,0:T(8,128)(2,1)} %bitcast.14, ...), custom_call_target="tpu_custom_call" | custom-call | flops 50331648 | bytes 1572864 | tf_op jit(solution)/shard_map/pallas_call | solution.py:322
  4.6 3.9 %collective-permute-start = (bf16[6144,128]{1,0:T(8,128)(2,1)}, bf16[6144,128]{1,0:T(8,128)(2,1)S(1)}, u32[]{:S(2)}, u32[]{:S(2)}) collective-permute-start(bf16[6144,128]{1,0:T(8,128)(2,1)} %get-tuple-element.21), channel_id=1, source_target_pairs={{0,8},{1,9},{2,10},{3,11},{4,12},{5,13},{6,14},{7,15},{8,0},{9,1},... | collective-permute-start | bytes 4718600 | tf_op jit(solution)/shard_map/ppermute | solution.py:361
  8.6 21.6 %all-to-all-start = ((bf16[768,4,128]{2,1,0:T(4,128)(2,1)}), bf16[768,4,128]{2,1,0:T(4,128)(2,1)S(1)}, u32[]{:S(2)}, u32[]{:S(2)}) async-start(bf16[768,4,128]{2,1,0:T(4,128)(2,1)} %bitcast.18), calls=%async_computation | async-start | bytes 1572864 | tf_op jit(solution)/shard_map/all_to_all | solution.py:365
  30.2 3.3 %collective-permute-start.3 = (bf16[2048,128]{1,0:T(8,128)(2,1)}, bf16[2048,128]{1,0:T(8,128)(2,1)}, u32[]{:S(2)}, u32[]{:S(2)}) collective-permute-start(bf16[2048,128]{1,0:T(8,128)(2,1)} %get-tuple-element.24), channel_id=1, source_target_pairs={{0,8},{1,9},{2,10},{3,11},{4,12},{5,13},{6,14},{7,15},{8,0},{9,1},... | collective-permute-start | bytes 1572872 | tf_op jit(solution)/shard_map/ppermute | solution.py:361
  33.5 25.7 %all-to-all-done = bf16[768,4,128]{2,1,0:T(4,128)(2,1)S(1)} async-done(((bf16[768,4,128]{2,1,0:T(4,128)(2,1)}), bf16[768,4,128]{2,1,0:T(4,128)(2,1)S(1)}, u32[]{:S(2)}, u32[]{:S(2)}) %all-to-all-start) | async-done | bytes 786464 | tf_op jit(solution)/shard_map/all_to_all | solution.py:365
  59.1 0.0 collective-permute-done.early
  59.1 0.1 fusion
  59.2 1.9 %collective-permute-start.2 = (bf16[2,768,128]{2,1,0:T(8,128)(2,1)S(1)}, bf16[2,768,128]{2,1,0:T(8,128)(2,1)S(1)}, u32[]{:S(2)}, u32[]{:S(2)}) collective-permute-start(bf16[2,768,128]{2,1,0:T(8,128)(2,1)S(1)} %get-tuple-element.34), channel_id=1, source_target_pairs={{1,0},{2,1},{3,2},{4,3},{5,4},{6,5},{7,6},{0,7},{9,8},{10,9},{11,1... | collective-permute-start | bytes 1179656 | tf_op jit(solution)/shard_map/ppermute | solution.py:410
  61.1 3.4 %collective-permute-start.1 = (bf16[2,768,128]{2,1,0:T(8,128)(2,1)S(1)}, bf16[2,768,128]{2,1,0:T(8,128)(2,1)}, u32[]{:S(2)}, u32[]{:S(2)}) collective-permute-start(bf16[2,768,128]{2,1,0:T(8,128)(2,1)S(1)} %get-tuple-element.35), channel_id=1, source_target_pairs={{0,1},{1,2},{2,3},{3,4},{4,5},{5,6},{6,7},{7,0},{8,9},{9,10},{10,1... | collective-permute-start | bytes 1179656 | tf_op jit(solution)/shard_map/ppermute | solution.py:409
  64.5 0.0 collective-permute-done.3.late
  64.5 7.2 %collective-permute-done.2.high = bf16[2,768,128]{2,1,0:T(8,128)(2,1)S(1)} collective-permute-done((bf16[2,768,128]{2,1,0:T(8,128)(2,1)S(1)}, bf16[2,768,128]{2,1,0:T(8,128)(2,1)S(1)}, u32[]{:S(2)}, u32[]{:S(2)}) %collective-permute-start.2) | collective-permute-done | bytes 393248 | tf_op jit(solution)/shard_map/ppermute | solution.py:410
  71.7 3.1 %collective-permute-done.1.low = bf16[2,768,128]{2,1,0:T(8,128)(2,1)} collective-permute-done((bf16[2,768,128]{2,1,0:T(8,128)(2,1)S(1)}, bf16[2,768,128]{2,1,0:T(8,128)(2,1)}, u32[]{:S(2)}, u32[]{:S(2)}) %collective-permute-start.1) | collective-permute-done | bytes 393248 | tf_op jit(solution)/shard_map/ppermute | solution.py:409
  74.7 0.0 copy-done.5
  74.7 0.0 copy-done.6
  74.8 0.0 copy-done.7
  74.8 9.4 %shard_map.94 = (bf16[4,768,128]{2,1,0:T(8,128)(2,1)}, bf16[2,768,128]{2,1,0:T(8,128)(2,1)}, bf16[2,768,128]{2,1,0:T(8,128)(2,1)}, bf16[2,192,2304]{2,1,0:T(8,128)(2,1)}, bf16[2,192,256]{2,1,0:T(8,128)(2,1)}) custom-call(s32[1]{0:T(128)} %bitcast.4.odd_ref, bf16[4,768,128]{2,1,0:T(8,128)(2,1)} %bitcast.13, bf16[2,768,128]{2,1,0:T(8,128)(2,1)} %collective-permute-done.1.low, ...), custom_call_target="tpu_custom_call" | custom-call | flops 1610612736 | bytes 8912896 | tf_op jit(solution)/shard_map/pallas_call | solution.py:322
  84.2 1.9 %collective-permute-start.4 = (bf16[2,768,128]{2,1,0:T(8,128)(2,1)}, bf16[2,768,128]{2,1,0:T(8,128)(2,1)S(1)}, u32[]{:S(2)}, u32[]{:S(2)}) collective-permute-start(bf16[2,768,128]{2,1,0:T(8,128)(2,1)} %get-tuple-element.26), channel_id=1, source_target_pairs={{0,1},{1,2},{2,3},{3,4},{4,5},{5,6},{6,7},{7,0},{8,9},{9,10},{10,1... | collective-permute-start | bytes 1179656 | tf_op jit(solution)/shard_map/ppermute | solution.py:448
  86.1 4.6 %collective-permute-start.5 = (bf16[2,768,128]{2,1,0:T(8,128)(2,1)}, bf16[2,768,128]{2,1,0:T(8,128)(2,1)S(1)}, u32[]{:S(2)}, u32[]{:S(2)}) collective-permute-start(bf16[2,768,128]{2,1,0:T(8,128)(2,1)} %get-tuple-element.27), channel_id=1, source_target_pairs={{1,0},{2,1},{3,2},{4,3},{5,4},{6,5},{7,6},{0,7},{9,8},{10,9},{11,1... | collective-permute-start | bytes 1179656 | tf_op jit(solution)/shard_map/ppermute | solution.py:449
  90.7 2.4 %collective-permute-start.6 = (bf16[2,192,2304]{2,1,0:T(8,128)(2,1)}, bf16[2,192,2304]{2,1,0:T(8,128)(2,1)}, u32[]{:S(2)}, u32[]{:S(2)}) collective-permute-start(bf16[2,192,2304]{2,1,0:T(8,128)(2,1)} %get-tuple-element.30.rows_ref), channel_id=1, source_target_pairs={{0,8},{1,9},{2,10},{3,11},{4,12},{5,13},{6,14},{7,15},{8,0},{9,1},... | collective-permute-start | bytes 5308424 | tf_op jit(solution)/shard_map/ppermute | solution.py:361
  93.1 3.9 %collective-permute-done.4.low_ref = bf16[2,768,128]{2,1,0:T(8,128)(2,1)S(1)} collective-permute-done((bf16[2,768,128]{2,1,0:T(8,128)(2,1)}, bf16[2,768,128]{2,1,0:T(8,128)(2,1)S(1)}, u32[]{:S(2)}, u32[]{:S(2)}) %collective-permute-start.4) | collective-permute-done | bytes 393248 | tf_op jit(solution)/shard_map/ppermute | solution.py:448
  97.0 1.0 collective-permute-done.5.high_ref
  98.0 1.1 copy-done
  99.1 1.1 shard_map.95
  100.2 17.3 %all-to-all-start.1 = ((bf16[768,4,128]{2,1,0:T(4,128)(2,1)}), bf16[768,4,128]{2,1,0:T(4,128)(2,1)S(1)}, u32[]{:S(2)}, u32[]{:S(2)}) async-start(bf16[768,4,128]{2,1,0:T(4,128)(2,1)} %bitcast.7), calls=%async_computation.1 | async-start | bytes 1572864 | tf_op jit(solution)/shard_map/all_to_all | solution.py:365
  117.4 21.8 %collective-permute-done.6.other_ref = bf16[2,192,2304]{2,1,0:T(8,128)(2,1)} collective-permute-done((bf16[2,192,2304]{2,1,0:T(8,128)(2,1)}, bf16[2,192,2304]{2,1,0:T(8,128)(2,1)}, u32[]{:S(2)}, u32[]{:S(2)}) %collective-permute-start.6) | collective-permute-done | bytes 1769504 | tf_op jit(solution)/shard_map/ppermute | solution.py:361
  139.2 0.0 copy-done.2
  139.2 0.0 copy-done.4
  139.2 4.2 %shard_map.97 = (bf16[1,2048,256]{2,1,0:T(8,128)(2,1)}, bf16[1,256,2048]{2,1,0:T(8,128)(2,1)}) custom-call(bf16[2,192,2304]{2,1,0:T(8,128)(2,1)S(1)} %copy-done.2, bf16[2,192,2304]{2,1,0:T(8,128)(2,1)} %collective-permute-done.6.other_ref, bf16[2,192,256]{2,1,0:T(8,128)(2,1)S(1)} %copy-done.4), custom_call_target="tpu_custom_call" | custom-call | flops 1610612736 | bytes 8388608 | tf_op jit(solution)/shard_map/pallas_call | solution.py:322
  143.4 3.3 %all-to-all-done.1 = bf16[768,4,128]{2,1,0:T(4,128)(2,1)S(1)} async-done(((bf16[768,4,128]{2,1,0:T(4,128)(2,1)}), bf16[768,4,128]{2,1,0:T(4,128)(2,1)S(1)}, u32[]{:S(2)}, u32[]{:S(2)}) %all-to-all-start.1) | async-done | bytes 786464 | tf_op jit(solution)/shard_map/all_to_all | solution.py:365
  146.7 0.0 copy-done.1
  146.7 0.0 copy-done.3
  146.7 1.5 shard_map.96
  (8 shorter events, 0.0 us)
Async XLA Ops:
  4.6 54.5 %collective-permute-start = (bf16[6144,128]{1,0:T(8,128)(2,1)}, bf16[6144,128]{1,0:T(8,128)(2,1)S(1)}, u32[]{:S(2)}, u32[]{:S(2)}) collective-permute-start(bf16[6144,128]{1,0:T(8,128)(2,1)} %get-tuple-element.21), channel_id=1, source_target_pairs={{0,8},{1,9},{2,10},{3,11},{4,12},{5,13},{6,14},{7,15},{8,0},{9,1},... | collective-permute-start | bytes 4718600 | tf_op jit(solution)/shard_map/ppermute | solution.py:361
  8.6 50.5 %all-to-all-start = ((bf16[768,4,128]{2,1,0:T(4,128)(2,1)}), bf16[768,4,128]{2,1,0:T(4,128)(2,1)S(1)}, u32[]{:S(2)}, u32[]{:S(2)}) async-start(bf16[768,4,128]{2,1,0:T(4,128)(2,1)} %bitcast.18), calls=%async_computation | async-start | bytes 1572864 | tf_op jit(solution)/shard_map/all_to_all | solution.py:365
  30.2 34.3 %collective-permute-start.3 = (bf16[2048,128]{1,0:T(8,128)(2,1)}, bf16[2048,128]{1,0:T(8,128)(2,1)}, u32[]{:S(2)}, u32[]{:S(2)}) collective-permute-start(bf16[2048,128]{1,0:T(8,128)(2,1)} %get-tuple-element.24), channel_id=1, source_target_pairs={{0,8},{1,9},{2,10},{3,11},{4,12},{5,13},{6,14},{7,15},{8,0},{9,1},... | collective-permute-start | bytes 1572872 | tf_op jit(solution)/shard_map/ppermute | solution.py:361
  59.1 15.6 %copy-start.5 = (bf16[768,4,128]{2,1,0:T(4,128)(2,1)}, bf16[768,4,128]{2,1,0:T(4,128)(2,1)S(1)}, u32[]{:S(2)}) copy-start(bf16[768,4,128]{2,1,0:T(4,128)(2,1)S(1)} %all-to-all-done) | copy-start | bytes 2359300
  59.1 15.6 %copy-start.6 = (bf16[6144,128]{1,0:T(8,128)(2,1)}, bf16[6144,128]{1,0:T(8,128)(2,1)S(1)}, u32[]{:S(2)}) copy-start(bf16[6144,128]{1,0:T(8,128)(2,1)S(1)} %collective-permute-done.early) | copy-start | bytes 4718596
  59.2 12.5 %collective-permute-start.2 = (bf16[2,768,128]{2,1,0:T(8,128)(2,1)S(1)}, bf16[2,768,128]{2,1,0:T(8,128)(2,1)S(1)}, u32[]{:S(2)}, u32[]{:S(2)}) collective-permute-start(bf16[2,768,128]{2,1,0:T(8,128)(2,1)S(1)} %get-tuple-element.34), channel_id=1, source_target_pairs={{1,0},{2,1},{3,2},{4,3},{5,4},{6,5},{7,6},{0,7},{9,8},{10,9},{11,1... | collective-permute-start | bytes 1179656 | tf_op jit(solution)/shard_map/ppermute | solution.py:410
  61.1 13.6 %collective-permute-start.1 = (bf16[2,768,128]{2,1,0:T(8,128)(2,1)S(1)}, bf16[2,768,128]{2,1,0:T(8,128)(2,1)}, u32[]{:S(2)}, u32[]{:S(2)}) collective-permute-start(bf16[2,768,128]{2,1,0:T(8,128)(2,1)S(1)} %get-tuple-element.35), channel_id=1, source_target_pairs={{0,1},{1,2},{2,3},{3,4},{4,5},{5,6},{6,7},{7,0},{8,9},{9,10},{10,1... | collective-permute-start | bytes 1179656 | tf_op jit(solution)/shard_map/ppermute | solution.py:409
  71.7 3.1 %copy-start.7 = (bf16[2,768,128]{2,1,0:T(8,128)(2,1)}, bf16[2,768,128]{2,1,0:T(8,128)(2,1)S(1)}, u32[]{:S(2)}) copy-start(bf16[2,768,128]{2,1,0:T(8,128)(2,1)S(1)} %collective-permute-done.2.high) | copy-start | bytes 1179652
  84.2 12.8 %collective-permute-start.4 = (bf16[2,768,128]{2,1,0:T(8,128)(2,1)}, bf16[2,768,128]{2,1,0:T(8,128)(2,1)S(1)}, u32[]{:S(2)}, u32[]{:S(2)}) collective-permute-start(bf16[2,768,128]{2,1,0:T(8,128)(2,1)} %get-tuple-element.26), channel_id=1, source_target_pairs={{0,1},{1,2},{2,3},{3,4},{4,5},{5,6},{6,7},{7,0},{8,9},{9,10},{10,1... | collective-permute-start | bytes 1179656 | tf_op jit(solution)/shard_map/ppermute | solution.py:448
  86.1 11.9 %collective-permute-start.5 = (bf16[2,768,128]{2,1,0:T(8,128)(2,1)}, bf16[2,768,128]{2,1,0:T(8,128)(2,1)S(1)}, u32[]{:S(2)}, u32[]{:S(2)}) collective-permute-start(bf16[2,768,128]{2,1,0:T(8,128)(2,1)} %get-tuple-element.27), channel_id=1, source_target_pairs={{1,0},{2,1},{3,2},{4,3},{5,4},{6,5},{7,6},{0,7},{9,8},{10,9},{11,1... | collective-permute-start | bytes 1179656 | tf_op jit(solution)/shard_map/ppermute | solution.py:449
  90.7 48.5 %collective-permute-start.6 = (bf16[2,192,2304]{2,1,0:T(8,128)(2,1)}, bf16[2,192,2304]{2,1,0:T(8,128)(2,1)}, u32[]{:S(2)}, u32[]{:S(2)}) collective-permute-start(bf16[2,192,2304]{2,1,0:T(8,128)(2,1)} %get-tuple-element.30.rows_ref), channel_id=1, source_target_pairs={{0,8},{1,9},{2,10},{3,11},{4,12},{5,13},{6,14},{7,15},{8,0},{9,1},... | collective-permute-start | bytes 5308424 | tf_op jit(solution)/shard_map/ppermute | solution.py:361
  98.0 1.1 copy-start
  99.1 40.1 %copy-start.2 = (bf16[2,192,2304]{2,1,0:T(8,128)(2,1)S(1)}, bf16[2,192,2304]{2,1,0:T(8,128)(2,1)}, u32[]{:S(2)}) copy-start(bf16[2,192,2304]{2,1,0:T(8,128)(2,1)} %get-tuple-element.30.rows_ref) | copy-start | bytes 5308420
  99.1 40.1 %copy-start.4 = (bf16[2,192,256]{2,1,0:T(8,128)(2,1)S(1)}, bf16[2,192,256]{2,1,0:T(8,128)(2,1)}, u32[]{:S(2)}) copy-start(bf16[2,192,256]{2,1,0:T(8,128)(2,1)} %get-tuple-element.31.own_ref) | copy-start | bytes 589828
  100.2 46.5 %all-to-all-start.1 = ((bf16[768,4,128]{2,1,0:T(4,128)(2,1)}), bf16[768,4,128]{2,1,0:T(4,128)(2,1)S(1)}, u32[]{:S(2)}, u32[]{:S(2)}) async-start(bf16[768,4,128]{2,1,0:T(4,128)(2,1)} %bitcast.7), calls=%async_computation.1 | async-start | bytes 1572864 | tf_op jit(solution)/shard_map/all_to_all | solution.py:365
  139.2 7.5 %copy-start.1 = (f32[128,2]{0,1:T(2,128)S(1)}, f32[128,2]{0,1:T(2,128)}, u32[]{:S(2)}) copy-start(f32[128,2]{0,1:T(2,128)} %param.8) | copy-start | bytes 3076
  139.2 7.5 %copy-start.3 = (s32[2,128]{1,0:T(2,128)S(1)}, s32[2,128]{1,0:T(2,128)}, u32[]{:S(2)}) copy-start(s32[2,128]{1,0:T(2,128)} %get-tuple-element.19.rows_ref) | copy-start | bytes 3076

commit v10 on v9

--- a/solution.py
+++ b/solution.py
@@ -11,7 +11,7 @@
 BF16 = jnp.bfloat16
 F32 = jnp.float32
 HALVES = 2
-EARLY = (1, 2)
+EARLY = (1, 1)
 PIECES = 4
 GROUP = 8
 FOUR = 4
@@ -47,9 +47,9 @@
 
 def split_blocks(hidden, model, width):
     blocks = weight_blocks(hidden, model, width)
-    count = hidden // width + model // width * EARLY[0] // EARLY[1]
+    ins, outs = blocks[: hidden // width], blocks[hidden // width :]
     parts = []
-    for part in (blocks[:count], blocks[count:]):
+    for part in (ins[: EARLY[0]] + outs[: EARLY[1]], ins[EARLY[0] :] + outs[EARLY[1] :]):
         at, placed = 0, []
         for which, first, rows in part:
             placed.append((which, first, at, rows))
@@ -150,10 +150,10 @@
     return block * (sources * used) + source * used + inner - block * used
 
 
-def expert_kernel(used, odd_ref, own, low, high, in_own, out_own, early, late, *rest):
-    ret_own, ret_low, ret_high, rows_out, own_ref = rest[:5]
-    recv_ref, x_ref, g_ref, in0, in1, out0, out1, held_ref, ret_ref, other_ref = rest[5:15]
-    recv_sems, weight_sems, ret_sems, kept_sems = rest[15:]
+def expert_kernel(used, odd_ref, own, low, high, in_own, out_own, in_other, early, late, *rest):
+    ret_own, ret_low, ret_high, x_out, g_out, own_ref = rest[:6]
+    recv_ref, x_ref, g_ref, in0, in1, out0, out1, held_ref, ret_ref, other_ref = rest[6:16]
+    recv_sems, weight_sems, ret_sems, kept_sems = rest[16:]
     classes, all_rows, width = own.shape
     peers = 2 * classes
     rows = all_rows // 4
@@ -172,17 +172,18 @@
         pltpu.make_async_copy(ref.at[q], recv_ref.at[:, cols], recv_sems.at[index])
         for index, (ref, q, cols) in enumerate(moves)
     ]
-    load_in = [in_pieces(in_own, in0, weight_sems, 0), []]
-    load_out = [in_pieces(out_own, out0, weight_sems, PIECES), []]
+    load_in = [in_pieces(in_own, in0, weight_sems, 0), in_pieces(in_other, in1, weight_sems, PIECES)]
+    load_out = [in_pieces(out_own, out0, weight_sems, 2 * PIECES), []]
     for (placed, _), source in zip(split_blocks(*reversed(in0.shape), width), (early, late)):
         for which, first, at, size in placed:
-            target = (in1, out1)[which].at[:, pl.ds(first, width)]
-            index = 2 * PIECES + len(load_in[1]) + len(load_out[1])
-            (load_in, load_out)[which][1].append(
-                pltpu.make_async_copy(
-                    source.at[pl.ds(at, size), :], target, weight_sems.at[index]
+            if which == 1:
+                load_out[1].append(
+                    pltpu.make_async_copy(
+                        source.at[pl.ds(at, size), :],
+                        out1.at[:, pl.ds(first, width)],
+                        weight_sems.at[3 * PIECES + len(load_out[1])],
+                    )
                 )
-            )
     for copy in arrive + load_in[0] + load_in[1]:
         copy.start()
     batch = GROUP if sources % GROUP == 0 else sources
@@ -209,15 +210,17 @@
     kept = [
         pltpu.make_async_copy(
             ref.at[:, pl.ds(at, model // PIECES)],
-            rows_out.at[kind, :, pl.ds(at, model // PIECES)],
+            out.at[:, pl.ds(at, model // PIECES)],
             kept_sems.at[kind, at * PIECES // model],
         )
-        for kind, ref in enumerate((x_ref, g_ref))
+        for kind, (ref, out) in enumerate(((x_ref, x_out), (g_ref, g_out)))
         for at in range(0, model, model // PIECES)
     ]
     kept += [
         pltpu.make_async_copy(
-            other_ref.at[kind], rows_out.at[kind, :, pl.ds(model, hidden)], kept_sems.at[kind, PIECES]
+            other_ref.at[kind],
+            g_out.at[:, pl.ds(model + kind * hidden, hidden)],
+            kept_sems.at[kind, PIECES],
         )
         for kind in range(2)
     ]
@@ -273,18 +276,18 @@
         copy.wait()
 
 
-def gradient_kernel(rows_ref, other_ref, own_ref, grad_in_ref, grad_out_ref):
+def gradient_kernel(x_ref, g_ref, other_x_ref, other_g_ref, own_ref, grad_in_ref, grad_out_ref):
     over_rows = ((0,), (0,))
-    hidden = own_ref.shape[2]
-    model = rows_ref.shape[2] - hidden
-    units = slice(model, model + hidden)
+    model, hidden = x_ref.shape[1], own_ref.shape[2]
+    act = other_g_ref[:, model : model + hidden]
+    dpre = other_g_ref[:, model + hidden :]
     for at in range(0, model, hidden):
         cols = slice(at, at + hidden)
-        part = dot(rows_ref[0, :, cols], own_ref[1], over_rows)
-        part = part + dot(other_ref[0, :, cols], other_ref[1, :, units], over_rows)
+        part = dot(x_ref[:, cols], own_ref[1], over_rows)
+        part = part + dot(other_x_ref[:, cols], dpre, over_rows)
         grad_in_ref[0, cols, :] = part.astype(BF16)
-        part = dot(own_ref[0], rows_ref[1, :, cols], over_rows)
-        part = part + dot(other_ref[0, :, units], other_ref[1, :, cols], over_rows)
+        part = dot(own_ref[0], g_ref[:, cols], over_rows)
+        part = part + dot(act, other_g_ref[:, cols], over_rows)
         grad_out_ref[0, :, cols] = part.astype(BF16)
 
 
@@ -296,7 +299,7 @@
 
 
 def combine_kernel(used, rows_ref, gates_ref, home_ref, mixed_ref, grad_ref):
-    groups, all_rows, _ = home_ref.shape
+    groups, all_rows, width = home_ref.shape
     tok_rows = mixed_ref.shape[0]
     slot = iota((all_rows, tok_rows), 0)
     row0, row1 = rows_ref[0:1, :], rows_ref[1:2, :]
@@ -305,15 +308,21 @@
     def column(row):
         return jnp.sum(jnp.where(diagonal, row, 0.0), axis=1, keepdims=True)
 
-    def picked(hit):
-        chosen = mask(hit)
-        return sum(dot(chosen, home_ref[group], ((0,), (0,))) for group in range(groups))
-
-    mixed = column(gates_ref[0:1, :]) * picked(slot == row0) + column(
-        gates_ref[1:2, :]
-    ) * picked(slot == row1)
+    total = home_ref[0].astype(F32)
+    for group in range(1, groups):
+        total = total + home_ref[group].astype(F32)
+    high = total.astype(BF16)
+    low = (total - high.astype(F32)).astype(BF16)
+    hits = (slot == row0, slot == row1, (slot == row0 + used) | (slot == row1 + used))
+    chosen = jnp.concatenate([mask(hit) for hit in hits], axis=1)
+    picked = dot(chosen, jnp.concatenate([high, low], axis=1), ((0,), (0,)))
+    picked = picked[:, :width] + picked[:, width:]
+    mixed = (
+        column(gates_ref[0:1, :]) * picked[:tok_rows]
+        + column(gates_ref[1:2, :]) * picked[tok_rows : 2 * tok_rows]
+    )
     mixed_ref[...] = mixed.astype(BF16)
-    grad_ref[...] = picked((slot == row0 + used) | (slot == row1 + used)).astype(BF16)
+    grad_ref[...] = picked[2 * tok_rows :].astype(BF16)
 
 
 def call(kernel, shapes, cost, places, limit, scratch, *args):
@@ -403,22 +412,26 @@
         in_own,
         out_own,
     )
-    early, late = to_partner(early), to_partner(late)
+    early, late = lax.optimization_barrier((to_partner(early), late))
+    late = to_partner(late)
     recv = over_spread(sent)
-    recv, early = lax.optimization_barrier((recv, early))
     low = lax.ppermute(recv[:side], "cuts", up)
     high = lax.ppermute(recv[side:], "cuts", down)
-    ret_own, ret_low, ret_high, held_rows, own_units = call(
+    early_in = early[: EARLY[0] * model].reshape(EARLY[0], model, width)
+    late_in = late[: (hidden // width - EARLY[0]) * model].reshape(-1, model, width)
+    in_other = jnp.concatenate([*early_in, *late_in], axis=1)
+    ret_own, ret_low, ret_high, held_x, held_g, own_units = call(
         functools.partial(expert_kernel, used),
         (
             struct(classes, all_rows, width),
             struct(side, all_rows, width),
             struct(classes - side, all_rows, width),
-            struct(2, rows, model + hidden),
+            struct(rows, model),
+            struct(rows, model + 2 * hidden),
             struct(2, rows, hidden),
         ),
         (16 * rows * model * hidden, 12 * rows * model + 8 * model * hidden),
-        ([pltpu.SMEM] + [far] * 7, [far] * 4 + [near]),
+        ([pltpu.SMEM] + [far] * 8, [far] * 5 + [near]),
         60,
         [
             pltpu.VMEM((all_rows, peers * width), BF16),
@@ -432,7 +445,7 @@
             pltpu.VMEM((all_rows, peers * width), BF16),
             pltpu.VMEM((2, rows, hidden), BF16),
             dma((peers,)),
-            dma((2 * PIECES + blocks,)),
+            dma((3 * PIECES + blocks,)),
             dma((peers,)),
             dma((2, PIECES + 1)),
         ],
@@ -442,12 +455,14 @@
         high,
         in_own,
         out_own,
+        in_other,
         early,
         late,
     )
     from_low = lax.ppermute(ret_low, "cuts", up)
     from_high = lax.ppermute(ret_high, "cuts", down)
-    partner_rows = to_partner(held_rows)
+    partner_x, sent_g = lax.optimization_barrier((to_partner(held_x), held_g))
+    partner_g = to_partner(sent_g)
     summed = call(
         add_kernel,
         (struct(classes, all_rows, width),),
@@ -464,11 +479,13 @@
         gradient_kernel,
         (struct(1, model, hidden), struct(1, hidden, model)),
         (16 * rows * model * hidden, 16 * model * hidden),
-        ([near] * 3, [near] * 2),
+        ([near] * 5, [near] * 2),
         32,
         [],
-        held_rows,
-        partner_rows,
+        held_x,
+        held_g,
+        partner_x,
+        partner_g,
         own_units,
     )
     mixed, token_grad = call(

time: 149 us -> 158 us (1.060)
  starting transfers between devices: 60.2 us -> 66.4 us
  Pallas kernels: 20.1 us -> 18.3 us
    ppermute x3 -> x4, waiting for transfers between devices: 21.8 us -> 35.6 us  [to_partner(): return lax.ppermute(value, 'cuts', swap)]
    ppermute x1, waiting for transfers between devices: 7.15 us -> 0.01 us  [body(): high = lax.ppermute(recv[side:], 'cuts', down)]
    ppermute x3 -> x4, starting transfers between devices: 9.64 us -> 13.3 us  [to_partner(): return lax.ppermute(value, 'cuts', swap)]
    all_to_all x2, waiting for transfers between devices: 29 us -> 25.6 us  [over_spread(): lax.all_to_all(pieces, ('dp', 'cuts'), 0, 0, tiled=True, axis_index_group...]
    ppermute x1, waiting for transfers between devices: 3.09 us -> 0.01 us  [body(): low = lax.ppermute(recv[:side], 'cuts', up)]
    ppermute x1, starting transfers between devices: 1.92 us -> 3.73 us  [body(): high = lax.ppermute(recv[side:], 'cuts', down)]
    pallas_call x5, Pallas kernels: 20.1 us -> 18.3 us  [call(): pl.pallas_call(kernel, out_shape=shapes, in_specs=[pl.BlockSpec(memory_sp...]
  transfers between devices with their start and end apart: 9 -> 10, of which waited for: 7 -> 5; matrix products, arithmetic and copies ran while one was open for 0% -> 1% of each run, Pallas kernels for 4% -> 2%
where the time goes in v10:
time: 158 us; the launch traced here: 156 us
  waiting for transfers between devices  66.6 us (42%)
  starting transfers between devices  66.4 us (42%)
  Pallas kernels  18.3 us (12%)
  local copies, waits for them, and re-layouts  2.52 us (2%)
    all_to_all x2, starting transfers between devices, over_spread(): lax.all_to_all(pieces, ('dp', 'cuts'), 0, 0, tiled=True, axis_index_group...  38.4 us
    ppermute x4, waiting for transfers between devices, to_partner(): return lax.ppermute(value, 'cuts', swap)  35.6 us
    all_to_all x2, waiting for transfers between devices, over_spread(): lax.all_to_all(pieces, ('dp', 'cuts'), 0, 0, tiled=True, axis_index_group...  25.6 us
    pallas_call x5, Pallas kernels, call(): pl.pallas_call(kernel, out_shape=shapes, in_specs=[pl.BlockSpec(memory_sp...  18.3 us
    ppermute x4, starting transfers between devices, to_partner(): return lax.ppermute(value, 'cuts', swap)  13.3 us
    ppermute x1, starting transfers between devices, body(): from_high = lax.ppermute(ret_high, 'cuts', down)  5.77 us
    ppermute x1, waiting for transfers between devices, body(): from_low = lax.ppermute(ret_low, 'cuts', up)  4.36 us
    ppermute x1, starting transfers between devices, body(): high = lax.ppermute(recv[side:], 'cuts', down)  3.73 us
  transfers between devices with their start and end apart: 10, of which 5 were waited for; matrix products, arithmetic and copies ran while one was open for 1% of the time, Pallas kernels for 2%

profile of v10, /device:TPU:1, one launch (start us, length us, event | category | flops | bytes accessed | tf_op | source)
XLA Modules:
  0.0 155.8 jit_solution(8280744574935940228)
XLA Ops:
  0.6 4.0 %shard_map.93 = (bf16[4,768,128]{2,1,0:T(8,128)(2,1)}, s32[2,128]{1,0:T(2,128)}, bf16[2304,128]{1,0:T(8,128)(2,1)}, bf16[5888,128]{1,0:T(8,128)(2,1)}) custom-call(s32[2,128]{1,0:T(2,128)} %bitcast.21, f32[2,128]{1,0:T(2,128)} %bitcast.12, bf16[128,128]{1,0:T(8,128)(2,1)} %tok_in.1, bf16[128,128]{1,0:T(8,128)(2,1)} %cot_in.1, bf16[2048,256]{1,0:T(8,128)(2,1)} %bitcast.15, ...), custom_call_target="tpu_custom_call" | custom-call | flops 50331648 | bytes 1572864 | tf_op jit(solution)/shard_map/pallas_call | solution.py:331
  4.6 3.9 %collective-permute-start.2 = (bf16[2304,128]{1,0:T(8,128)(2,1)}, bf16[2304,128]{1,0:T(8,128)(2,1)S(1)}, u32[]{:S(2)}, u32[]{:S(2)}) collective-permute-start(bf16[2304,128]{1,0:T(8,128)(2,1)} %get-tuple-element.24), channel_id=1, source_target_pairs={{0,8},{1,9},{2,10},{3,11},{4,12},{5,13},{6,14},{7,15},{8,0},{9,1},... | collective-permute-start | bytes 1769480 | tf_op jit(solution)/shard_map/ppermute | solution.py:370
  8.6 21.6 %all-to-all-start = ((bf16[768,4,128]{2,1,0:T(4,128)(2,1)}), bf16[768,4,128]{2,1,0:T(4,128)(2,1)S(1)}, u32[]{:S(2)}, u32[]{:S(2)}) async-start(bf16[768,4,128]{2,1,0:T(4,128)(2,1)} %bitcast.19), calls=%async_computation | async-start | bytes 1572864 | tf_op jit(solution)/shard_map/all_to_all | solution.py:374
  30.2 0.0 collective-permute-done.2.early
  30.2 3.3 %collective-permute-start.3 = (bf16[5888,128]{1,0:T(8,128)(2,1)}, bf16[5888,128]{1,0:T(8,128)(2,1)S(1)}, u32[]{:S(2)}, u32[]{:S(2)}) collective-permute-start(bf16[5888,128]{1,0:T(8,128)(2,1)} %get-tuple-element.27), channel_id=1, source_target_pairs={{0,8},{1,9},{2,10},{3,11},{4,12},{5,13},{6,14},{7,15},{8,0},{9,1},... | collective-permute-start | bytes 4521992 | tf_op jit(solution)/shard_map/ppermute | solution.py:370
  33.5 25.6 %all-to-all-done = bf16[768,4,128]{2,1,0:T(4,128)(2,1)S(1)} async-done(((bf16[768,4,128]{2,1,0:T(4,128)(2,1)}), bf16[768,4,128]{2,1,0:T(4,128)(2,1)S(1)}, u32[]{:S(2)}, u32[]{:S(2)}) %all-to-all-start) | async-done | bytes 786464 | tf_op jit(solution)/shard_map/all_to_all | solution.py:374
  59.1 1.0 fusion
  60.1 2.8 %collective-permute-start = (bf16[2,768,128]{2,1,0:T(8,128)(2,1)}, bf16[2,768,128]{2,1,0:T(8,128)(2,1)}, u32[]{:S(2)}, u32[]{:S(2)}) collective-permute-start(bf16[2,768,128]{2,1,0:T(8,128)(2,1)} %bitcast.7), channel_id=1, source_target_pairs={{0,1},{1,2},{2,3},{3,4},{4,5},{5,6},{6,7},{7,0},{8,9},{9,10},{10,1... | collective-permute-start | bytes 1179656 | tf_op jit(solution)/shard_map/ppermute | solution.py:418
  62.9 3.7 %collective-permute-start.1 = (bf16[2,768,128]{2,1,0:T(8,128)(2,1)S(1)}, bf16[2,768,128]{2,1,0:T(8,128)(2,1)}, u32[]{:S(2)}, u32[]{:S(2)}) collective-permute-start(bf16[2,768,128]{2,1,0:T(8,128)(2,1)S(1)} %bitcast.20), channel_id=1, source_target_pairs={{1,0},{2,1},{3,2},{4,3},{5,4},{6,5},{7,6},{0,7},{9,8},{10,9},{11,1... | collective-permute-start | bytes 1179656 | tf_op jit(solution)/shard_map/ppermute | solution.py:419
  66.7 7.0 %collective-permute-done.3.late = bf16[5888,128]{1,0:T(8,128)(2,1)S(1)} collective-permute-done((bf16[5888,128]{1,0:T(8,128)(2,1)}, bf16[5888,128]{1,0:T(8,128)(2,1)S(1)}, u32[]{:S(2)}, u32[]{:S(2)}) %collective-permute-start.3) | collective-permute-done | bytes 1507360 | tf_op jit(solution)/shard_map/ppermute | solution.py:370
  73.7 0.0 copy-done.8
  73.7 0.0 copy-done.6
  73.7 1.2 pad_maximum_fusion.in_other
  75.0 0.3 copy-done.7
  75.2 0.0 collective-permute-done.low
  75.2 0.0 collective-permute-done.1.high
  75.2 9.4 %shard_map.94 = (bf16[4,768,128]{2,1,0:T(8,128)(2,1)}, bf16[2,768,128]{2,1,0:T(8,128)(2,1)}, bf16[2,768,128]{2,1,0:T(8,128)(2,1)}, bf16[192,2048]{1,0:T(8,128)(2...) custom-call(s32[1]{0:T(128)} %bitcast.4.odd_ref, bf16[4,768,128]{2,1,0:T(8,128)(2,1)} %bitcast.14, ...), custom_call_target="tpu_custom_call" | custom-call | flops 1610612736 | bytes 8912896 | tf_op jit(solution)/shard_map/pallas_call | solution.py:331
  84.7 2.4 %collective-permute-start.4 = (bf16[2,768,128]{2,1,0:T(8,128)(2,1)}, bf16[2,768,128]{2,1,0:T(8,128)(2,1)S(1)}, u32[]{:S(2)}, u32[]{:S(2)}) collective-permute-start(bf16[2,768,128]{2,1,0:T(8,128)(2,1)} %get-tuple-element.29), channel_id=1, source_target_pairs={{0,1},{1,2},{2,3},{3,4},{4,5},{5,6},{6,7},{7,0},{8,9},{9,10},{10,1... | collective-permute-start | bytes 1179656 | tf_op jit(solution)/shard_map/ppermute | solution.py:462
  87.1 5.8 %collective-permute-start.5 = (bf16[2,768,128]{2,1,0:T(8,128)(2,1)}, bf16[2,768,128]{2,1,0:T(8,128)(2,1)S(1)}, u32[]{:S(2)}, u32[]{:S(2)}) collective-permute-start(bf16[2,768,128]{2,1,0:T(8,128)(2,1)} %get-tuple-element.30), channel_id=1, source_target_pairs={{1,0},{2,1},{3,2},{4,3},{5,4},{6,5},{7,6},{0,7},{9,8},{10,9},{11,1... | collective-permute-start | bytes 1179656 | tf_op jit(solution)/shard_map/ppermute | solution.py:463
  92.9 2.8 %collective-permute-start.6 = (bf16[192,2048]{1,0:T(8,128)(2,1)}, bf16[192,2048]{1,0:T(8,128)(2,1)S(1)}, u32[]{:S(2)}, u32[]{:S(2)}) collective-permute-start(bf16[192,2048]{1,0:T(8,128)(2,1)} %get-tuple-element.33.x_ref), channel_id=1, source_target_pairs={{0,8},{1,9},{2,10},{3,11},{4,12},{5,13},{6,14},{7,15},{8,0},{9,1},... | collective-permute-start | bytes 2359304 | tf_op jit(solution)/shard_map/ppermute | solution.py:370
  95.7 4.4 %collective-permute-done.4.low_ref = bf16[2,768,128]{2,1,0:T(8,128)(2,1)S(1)} collective-permute-done((bf16[2,768,128]{2,1,0:T(8,128)(2,1)}, bf16[2,768,128]{2,1,0:T(8,128)(2,1)S(1)}, u32[]{:S(2)}, u32[]{:S(2)}) %collective-permute-start.4) | collective-permute-done | bytes 393248 | tf_op jit(solution)/shard_map/ppermute | solution.py:462
  100.0 1.0 collective-permute-done.5.high_ref
  101.0 1.1 copy-done
  102.1 1.1 shard_map.95
  103.2 16.8 %all-to-all-start.1 = ((bf16[768,4,128]{2,1,0:T(4,128)(2,1)}), bf16[768,4,128]{2,1,0:T(4,128)(2,1)S(1)}, u32[]{:S(2)}, u32[]{:S(2)}) async-start(bf16[768,4,128]{2,1,0:T(4,128)(2,1)} %bitcast.9), calls=%async_computation.1 | async-start | bytes 1572864 | tf_op jit(solution)/shard_map/all_to_all | solution.py:374
  120.0 0.0 collective-permute-done.6.other_x_ref
  120.0 3.3 %collective-permute-start.7 = (bf16[192,2560]{1,0:T(8,128)(2,1)S(1)}, bf16[192,2560]{1,0:T(8,128)(2,1)S(1)}, u32[]{:S(2)}, u32[]{:S(2)}) collective-permute-start(bf16[192,2560]{1,0:T(8,128)(2,1)S(1)} %copy-done.2), channel_id=1, source_target_pairs={{0,8},{1,9},{2,10},{3,11},{4,12},{5,13},{6,14},{7,15},{8,0},{9,1},... | collective-permute-start | bytes 2949128 | tf_op jit(solution)/shard_map/ppermute | solution.py:370
  123.3 28.6 %collective-permute-done.7.other_g_ref = bf16[192,2560]{1,0:T(8,128)(2,1)S(1)} collective-permute-done((bf16[192,2560]{1,0:T(8,128)(2,1)S(1)}, bf16[192,2560]{1,0:T(8,128)(2,1)S(1)}, u32[]{:S(2)}, u32[]{:S(2)}) %collective-permute-start.7) | collective-permute-done | bytes 983072 | tf_op jit(solution)/shard_map/ppermute | solution.py:370
  152.0 2.7 %shard_map.97 = (bf16[1,2048,256]{2,1,0:T(8,128)(2,1)}, bf16[1,256,2048]{2,1,0:T(8,128)(2,1)}) custom-call(bf16[192,2048]{1,0:T(8,128)(2,1)S(1)} %copy-done.3, bf16[192,2560]{1,0:T(8,128)(2,1)S(1)} %copy-done.2, bf16[192,2048]{1,0:T(8,128)(2,1)S(1)} %collective-permute-done.6.other_x_ref, bf16[192,2560]{1,0:T(8,128)(2,1)S(1)} %collective-permute-done.7.other_g_ref, ...), custom_call_target="tpu_custom_call" | custom-call | flops 1610612736 | bytes 8388608 | tf_op jit(solution)/shard_map/pallas_call | solution.py:331
  154.6 0.0 all-to-all-done.1
  154.6 0.0 copy-done.5
  154.6 1.1 shard_map.96
  (15 shorter events, 0.1 us)
Async XLA Ops:
  4.6 25.5 %collective-permute-start.2 = (bf16[2304,128]{1,0:T(8,128)(2,1)}, bf16[2304,128]{1,0:T(8,128)(2,1)S(1)}, u32[]{:S(2)}, u32[]{:S(2)}) collective-permute-start(bf16[2304,128]{1,0:T(8,128)(2,1)} %get-tuple-element.24), channel_id=1, source_target_pairs={{0,8},{1,9},{2,10},{3,11},{4,12},{5,13},{6,14},{7,15},{8,0},{9,1},... | collective-permute-start | bytes 1769480 | tf_op jit(solution)/shard_map/ppermute | solution.py:370
  8.6 50.5 %all-to-all-start = ((bf16[768,4,128]{2,1,0:T(4,128)(2,1)}), bf16[768,4,128]{2,1,0:T(4,128)(2,1)S(1)}, u32[]{:S(2)}, u32[]{:S(2)}) async-start(bf16[768,4,128]{2,1,0:T(4,128)(2,1)} %bitcast.19), calls=%async_computation | async-start | bytes 1572864 | tf_op jit(solution)/shard_map/all_to_all | solution.py:374
  30.2 43.5 %copy-start.8 = (bf16[2304,128]{1,0:T(8,128)(2,1)}, bf16[2304,128]{1,0:T(8,128)(2,1)S(1)}, u32[]{:S(2)}) copy-start(bf16[2304,128]{1,0:T(8,128)(2,1)S(1)} %collective-permute-done.2.early) | copy-start | bytes 1769476
  30.2 43.5 %collective-permute-start.3 = (bf16[5888,128]{1,0:T(8,128)(2,1)}, bf16[5888,128]{1,0:T(8,128)(2,1)S(1)}, u32[]{:S(2)}, u32[]{:S(2)}) collective-permute-start(bf16[5888,128]{1,0:T(8,128)(2,1)} %get-tuple-element.27), channel_id=1, source_target_pairs={{0,8},{1,9},{2,10},{3,11},{4,12},{5,13},{6,14},{7,15},{8,0},{9,1},... | collective-permute-start | bytes 4521992 | tf_op jit(solution)/shard_map/ppermute | solution.py:370
  59.1 14.6 %copy-start.6 = (bf16[768,4,128]{2,1,0:T(4,128)(2,1)}, bf16[768,4,128]{2,1,0:T(4,128)(2,1)S(1)}, u32[]{:S(2)}) copy-start(bf16[768,4,128]{2,1,0:T(4,128)(2,1)S(1)} %all-to-all-done) | copy-start | bytes 2359300
  60.1 15.1 %collective-permute-start = (bf16[2,768,128]{2,1,0:T(8,128)(2,1)}, bf16[2,768,128]{2,1,0:T(8,128)(2,1)}, u32[]{:S(2)}, u32[]{:S(2)}) collective-permute-start(bf16[2,768,128]{2,1,0:T(8,128)(2,1)} %bitcast.7), channel_id=1, source_target_pairs={{0,1},{1,2},{2,3},{3,4},{4,5},{5,6},{6,7},{7,0},{8,9},{9,10},{10,1... | collective-permute-start | bytes 1179656 | tf_op jit(solution)/shard_map/ppermute | solution.py:418
  62.9 12.3 %collective-permute-start.1 = (bf16[2,768,128]{2,1,0:T(8,128)(2,1)S(1)}, bf16[2,768,128]{2,1,0:T(8,128)(2,1)}, u32[]{:S(2)}, u32[]{:S(2)}) collective-permute-start(bf16[2,768,128]{2,1,0:T(8,128)(2,1)S(1)} %bitcast.20), channel_id=1, source_target_pairs={{1,0},{2,1},{3,2},{4,3},{5,4},{6,5},{7,6},{0,7},{9,8},{10,9},{11,1... | collective-permute-start | bytes 1179656 | tf_op jit(solution)/shard_map/ppermute | solution.py:419
  73.7 1.6 %copy-start.7 = (bf16[5888,128]{1,0:T(8,128)(2,1)}, bf16[5888,128]{1,0:T(8,128)(2,1)S(1)}, u32[]{:S(2)}) copy-start(bf16[5888,128]{1,0:T(8,128)(2,1)S(1)} %collective-permute-done.3.late) | copy-start | bytes 4521988
  84.7 15.3 %collective-permute-start.4 = (bf16[2,768,128]{2,1,0:T(8,128)(2,1)}, bf16[2,768,128]{2,1,0:T(8,128)(2,1)S(1)}, u32[]{:S(2)}, u32[]{:S(2)}) collective-permute-start(bf16[2,768,128]{2,1,0:T(8,128)(2,1)} %get-tuple-element.29), channel_id=1, source_target_pairs={{0,1},{1,2},{2,3},{3,4},{4,5},{5,6},{6,7},{7,0},{8,9},{9,10},{10,1... | collective-permute-start | bytes 1179656 | tf_op jit(solution)/shard_map/ppermute | solution.py:462
  87.1 13.9 %collective-permute-start.5 = (bf16[2,768,128]{2,1,0:T(8,128)(2,1)}, bf16[2,768,128]{2,1,0:T(8,128)(2,1)S(1)}, u32[]{:S(2)}, u32[]{:S(2)}) collective-permute-start(bf16[2,768,128]{2,1,0:T(8,128)(2,1)} %get-tuple-element.30), channel_id=1, source_target_pairs={{1,0},{2,1},{3,2},{4,3},{5,4},{6,5},{7,6},{0,7},{9,8},{10,9},{11,1... | collective-permute-start | bytes 1179656 | tf_op jit(solution)/shard_map/ppermute | solution.py:463
  92.9 27.1 %collective-permute-start.6 = (bf16[192,2048]{1,0:T(8,128)(2,1)}, bf16[192,2048]{1,0:T(8,128)(2,1)S(1)}, u32[]{:S(2)}, u32[]{:S(2)}) collective-permute-start(bf16[192,2048]{1,0:T(8,128)(2,1)} %get-tuple-element.33.x_ref), channel_id=1, source_target_pairs={{0,8},{1,9},{2,10},{3,11},{4,12},{5,13},{6,14},{7,15},{8,0},{9,1},... | collective-permute-start | bytes 2359304 | tf_op jit(solution)/shard_map/ppermute | solution.py:370
  101.0 1.1 copy-start
  102.1 17.9 %copy-start.2 = (bf16[192,2560]{1,0:T(8,128)(2,1)S(1)}, bf16[192,2560]{1,0:T(8,128)(2,1)}, u32[]{:S(2)}) copy-start(bf16[192,2560]{1,0:T(8,128)(2,1)} %get-tuple-element.36.g_ref) | copy-start | bytes 2949124
  102.1 49.8 %copy-start.3 = (bf16[192,2048]{1,0:T(8,128)(2,1)S(1)}, bf16[192,2048]{1,0:T(8,128)(2,1)}, u32[]{:S(2)}) copy-start(bf16[192,2048]{1,0:T(8,128)(2,1)} %get-tuple-element.33.x_ref) | copy-start | bytes 2359300
  102.1 49.8 %copy-start.4 = (bf16[2,192,256]{2,1,0:T(8,128)(2,1)S(1)}, bf16[2,192,256]{2,1,0:T(8,128)(2,1)}, u32[]{:S(2)}) copy-start(bf16[2,192,256]{2,1,0:T(8,128)(2,1)} %get-tuple-element.37.own_ref) | copy-start | bytes 589828
  103.2 51.4 %all-to-all-start.1 = ((bf16[768,4,128]{2,1,0:T(4,128)(2,1)}), bf16[768,4,128]{2,1,0:T(4,128)(2,1)S(1)}, u32[]{:S(2)}, u32[]{:S(2)}) async-start(bf16[768,4,128]{2,1,0:T(4,128)(2,1)} %bitcast.9), calls=%async_computation.1 | async-start | bytes 1572864 | tf_op jit(solution)/shard_map/all_to_all | solution.py:374
  120.0 31.9 %collective-permute-start.7 = (bf16[192,2560]{1,0:T(8,128)(2,1)S(1)}, bf16[192,2560]{1,0:T(8,128)(2,1)S(1)}, u32[]{:S(2)}, u32[]{:S(2)}) collective-permute-start(bf16[192,2560]{1,0:T(8,128)(2,1)S(1)} %copy-done.2), channel_id=1, source_target_pairs={{0,8},{1,9},{2,10},{3,11},{4,12},{5,13},{6,14},{7,15},{8,0},{9,1},... | collective-permute-start | bytes 2949128 | tf_op jit(solution)/shard_map/ppermute | solution.py:370
  151.9 2.7 %copy-start.1 = (f32[128,2]{0,1:T(2,128)S(1)}, f32[128,2]{0,1:T(2,128)}, u32[]{:S(2)}) copy-start(f32[128,2]{0,1:T(2,128)} %param.8) | copy-start | bytes 3076
  151.9 2.7 %copy-start.5 = (s32[2,128]{1,0:T(2,128)S(1)}, s32[2,128]{1,0:T(2,128)}, u32[]{:S(2)}) copy-start(s32[2,128]{1,0:T(2,128)} %get-tuple-element.22.rows_ref) | copy-start | bytes 3076

commit v11 on v10

--- a/solution.py
+++ b/solution.py
@@ -11,7 +11,7 @@
 BF16 = jnp.bfloat16
 F32 = jnp.float32
 HALVES = 2
-EARLY = (1, 1)
+EARLY = (1, 3)
 PIECES = 4
 GROUP = 8
 FOUR = 4
@@ -151,9 +151,9 @@
 
 
 def expert_kernel(used, odd_ref, own, low, high, in_own, out_own, in_other, early, late, *rest):
-    ret_own, ret_low, ret_high, x_out, g_out, own_ref = rest[:6]
-    recv_ref, x_ref, g_ref, in0, in1, out0, out1, held_ref, ret_ref, other_ref = rest[6:16]
-    recv_sems, weight_sems, ret_sems, kept_sems = rest[16:]
+    ret_own, ret_low, ret_high, rows_out, own_ref = rest[:5]
+    recv_ref, x_ref, g_ref, in0, in1, out0, out1, held_ref, ret_ref, other_ref = rest[5:15]
+    recv_sems, weight_sems, ret_sems, kept_sems = rest[15:]
     classes, all_rows, width = own.shape
     peers = 2 * classes
     rows = all_rows // 4
@@ -210,16 +210,16 @@
     kept = [
         pltpu.make_async_copy(
             ref.at[:, pl.ds(at, model // PIECES)],
-            out.at[:, pl.ds(at, model // PIECES)],
+            rows_out.at[kind, :, pl.ds(at, model // PIECES)],
             kept_sems.at[kind, at * PIECES // model],
         )
-        for kind, (ref, out) in enumerate(((x_ref, x_out), (g_ref, g_out)))
+        for kind, ref in enumerate((x_ref, g_ref))
         for at in range(0, model, model // PIECES)
     ]
     kept += [
         pltpu.make_async_copy(
             other_ref.at[kind],
-            g_out.at[:, pl.ds(model + kind * hidden, hidden)],
+            rows_out.at[kind, :, pl.ds(model, hidden)],
             kept_sems.at[kind, PIECES],
         )
         for kind in range(2)
@@ -276,18 +276,18 @@
         copy.wait()
 
 
-def gradient_kernel(x_ref, g_ref, other_x_ref, other_g_ref, own_ref, grad_in_ref, grad_out_ref):
+def gradient_kernel(rows_ref, other_ref, own_ref, grad_in_ref, grad_out_ref):
     over_rows = ((0,), (0,))
-    model, hidden = x_ref.shape[1], own_ref.shape[2]
-    act = other_g_ref[:, model : model + hidden]
-    dpre = other_g_ref[:, model + hidden :]
+    hidden = own_ref.shape[2]
+    model = rows_ref.shape[2] - hidden
+    units = slice(model, model + hidden)
     for at in range(0, model, hidden):
         cols = slice(at, at + hidden)
-        part = dot(x_ref[:, cols], own_ref[1], over_rows)
-        part = part + dot(other_x_ref[:, cols], dpre, over_rows)
+        part = dot(rows_ref[0, :, cols], own_ref[1], over_rows)
+        part = part + dot(other_ref[0, :, cols], other_ref[1, :, units], over_rows)
         grad_in_ref[0, cols, :] = part.astype(BF16)
-        part = dot(own_ref[0], g_ref[:, cols], over_rows)
-        part = part + dot(act, other_g_ref[:, cols], over_rows)
+        part = dot(own_ref[0], rows_ref[1, :, cols], over_rows)
+        part = part + dot(other_ref[0, :, units], other_ref[1, :, cols], over_rows)
         grad_out_ref[0, :, cols] = part.astype(BF16)
 
 
@@ -420,18 +420,17 @@
     early_in = early[: EARLY[0] * model].reshape(EARLY[0], model, width)
     late_in = late[: (hidden // width - EARLY[0]) * model].reshape(-1, model, width)
     in_other = jnp.concatenate([*early_in, *late_in], axis=1)
-    ret_own, ret_low, ret_high, held_x, held_g, own_units = call(
+    ret_own, ret_low, ret_high, held_rows, own_units = call(
         functools.partial(expert_kernel, used),
         (
             struct(classes, all_rows, width),
             struct(side, all_rows, width),
             struct(classes - side, all_rows, width),
-            struct(rows, model),
-            struct(rows, model + 2 * hidden),
+            struct(2, rows, model + hidden),
             struct(2, rows, hidden),
         ),
         (16 * rows * model * hidden, 12 * rows * model + 8 * model * hidden),
-        ([pltpu.SMEM] + [far] * 8, [far] * 5 + [near]),
+        ([pltpu.SMEM] + [far] * 8, [far] * 4 + [near]),
         60,
         [
             pltpu.VMEM((all_rows, peers * width), BF16),
@@ -461,8 +460,7 @@
     )
     from_low = lax.ppermute(ret_low, "cuts", up)
     from_high = lax.ppermute(ret_high, "cuts", down)
-    partner_x, sent_g = lax.optimization_barrier((to_partner(held_x), held_g))
-    partner_g = to_partner(sent_g)
+    partner_rows = to_partner(held_rows)
     summed = call(
         add_kernel,
         (struct(classes, all_rows, width),),
@@ -479,13 +477,11 @@
         gradient_kernel,
         (struct(1, model, hidden), struct(1, hidden, model)),
         (16 * rows * model * hidden, 16 * model * hidden),
-        ([near] * 5, [near] * 2),
+        ([near] * 3, [near] * 2),
         32,
         [],
-        held_x,
-        held_g,
-        partner_x,
-        partner_g,
+        held_rows,
+        partner_rows,
         own_units,
     )
     mixed, token_grad = call(

time: 158 us -> 148 us (0.937); the launches traced: 156 us -> 147 us
  starting transfers between devices: 66.4 us -> 61 us
  waiting for transfers between devices: 66.6 us -> 62.4 us
    ppermute x4 -> x3, waiting for transfers between devices: 35.6 us -> 27.2 us  [to_partner(): return lax.ppermute(value, 'cuts', swap)]
    ppermute x4 -> x3, starting transfers between devices: 13.3 us -> 9.75 us  [to_partner(): return lax.ppermute(value, 'cuts', swap)]
    all_to_all x2, waiting for transfers between devices: 25.6 us -> 27.7 us  [over_spread(): lax.all_to_all(pieces, ('dp', 'cuts'), 0, 0, tiled=True, axis_index_group...]
    ppermute x1, waiting for transfers between devices: 0.01 us -> 1.88 us  [body(): low = lax.ppermute(recv[:side], 'cuts', up)]
  transfers between devices with their start and end apart: 10 -> 9, of which waited for: 5 -> 8; matrix products, arithmetic and copies ran while one was open for 1% -> 2% of each run, Pallas kernels for 2% -> 4%
where the time goes in v11:
time: 148 us; the launch traced here: 147 us
  waiting for transfers between devices  62.4 us (42%)
  starting transfers between devices  61 us (41%)
  Pallas kernels  19.8 us (13%)
  local copies, waits for them, and re-layouts  2.24 us (2%)
    all_to_all x2, starting transfers between devices, over_spread(): lax.all_to_all(pieces, ('dp', 'cuts'), 0, 0, tiled=True, axis_index_group...  37.7 us
    all_to_all x2, waiting for transfers between devices, over_spread(): lax.all_to_all(pieces, ('dp', 'cuts'), 0, 0, tiled=True, axis_index_group...  27.7 us
    ppermute x3, waiting for transfers between devices, to_partner(): return lax.ppermute(value, 'cuts', swap)  27.2 us
    pallas_call x5, Pallas kernels, call(): pl.pallas_call(kernel, out_shape=shapes, in_specs=[pl.BlockSpec(memory_sp...  19.8 us
    ppermute x3, starting transfers between devices, to_partner(): return lax.ppermute(value, 'cuts', swap)  9.75 us
    ppermute x1, starting transfers between devices, body(): from_high = lax.ppermute(ret_high, 'cuts', down)  4.44 us
    ppermute x1, waiting for transfers between devices, body(): from_low = lax.ppermute(ret_low, 'cuts', up)  3.8 us
    ppermute x1, starting transfers between devices, body(): high = lax.ppermute(recv[side:], 'cuts', down)  3.73 us
  transfers between devices with their start and end apart: 9, of which 8 were waited for; matrix products, arithmetic and copies ran while one was open for 2% of the time, Pallas kernels for 4%

profile of v11, /device:TPU:1, one launch (start us, length us, event | category | flops | bytes accessed | tf_op | source)
XLA Modules:
  0.0 147.5 jit_solution(2179167713808751061)
XLA Ops:
  0.6 4.0 %shard_map.93 = (bf16[4,768,128]{2,1,0:T(8,128)(2,1)}, s32[2,128]{1,0:T(2,128)}, bf16[2816,128]{1,0:T(8,128)(2,1)}, bf16[5376,128]{1,0:T(8,128)(2,1)}) custom-call(s32[2,128]{1,0:T(2,128)} %bitcast.21, f32[2,128]{1,0:T(2,128)} %bitcast.12, bf16[128,128]{1,0:T(8,128)(2,1)} %tok_in.1, bf16[128,128]{1,0:T(8,128)(2,1)} %cot_in.1, bf16[2048,256]{1,0:T(8,128)(2,1)} %bitcast.15, ...), custom_call_target="tpu_custom_call" | custom-call | flops 50331648 | bytes 1572864 | tf_op jit(solution)/shard_map/pallas_call | solution.py:331
  4.6 3.9 %collective-permute-start.2 = (bf16[2816,128]{1,0:T(8,128)(2,1)}, bf16[2816,128]{1,0:T(8,128)(2,1)S(1)}, u32[]{:S(2)}, u32[]{:S(2)}) collective-permute-start(bf16[2816,128]{1,0:T(8,128)(2,1)} %get-tuple-element.21), channel_id=1, source_target_pairs={{0,8},{1,9},{2,10},{3,11},{4,12},{5,13},{6,14},{7,15},{8,0},{9,1},... | collective-permute-start | bytes 2162696 | tf_op jit(solution)/shard_map/ppermute | solution.py:370
  8.6 21.6 %all-to-all-start = ((bf16[768,4,128]{2,1,0:T(4,128)(2,1)}), bf16[768,4,128]{2,1,0:T(4,128)(2,1)S(1)}, u32[]{:S(2)}, u32[]{:S(2)}) async-start(bf16[768,4,128]{2,1,0:T(4,128)(2,1)} %bitcast.19), calls=%async_computation | async-start | bytes 1572864 | tf_op jit(solution)/shard_map/all_to_all | solution.py:374
  30.2 0.0 collective-permute-done.2.early
  30.2 0.0 copy-start.7
  30.2 3.3 %collective-permute-start.3 = (bf16[5376,128]{1,0:T(8,128)(2,1)}, bf16[5376,128]{1,0:T(8,128)(2,1)S(1)}, u32[]{:S(2)}, u32[]{:S(2)}) collective-permute-start(bf16[5376,128]{1,0:T(8,128)(2,1)} %get-tuple-element.24), channel_id=1, source_target_pairs={{0,8},{1,9},{2,10},{3,11},{4,12},{5,13},{6,14},{7,15},{8,0},{9,1},... | collective-permute-start | bytes 4128776 | tf_op jit(solution)/shard_map/ppermute | solution.py:370
  33.5 25.6 %all-to-all-done = bf16[768,4,128]{2,1,0:T(4,128)(2,1)S(1)} async-done(((bf16[768,4,128]{2,1,0:T(4,128)(2,1)}), bf16[768,4,128]{2,1,0:T(4,128)(2,1)S(1)}, u32[]{:S(2)}, u32[]{:S(2)}) %all-to-all-start) | async-done | bytes 786464 | tf_op jit(solution)/shard_map/all_to_all | solution.py:374
  59.1 1.0 fusion
  60.1 2.8 %collective-permute-start = (bf16[2,768,128]{2,1,0:T(8,128)(2,1)}, bf16[2,768,128]{2,1,0:T(8,128)(2,1)}, u32[]{:S(2)}, u32[]{:S(2)}) collective-permute-start(bf16[2,768,128]{2,1,0:T(8,128)(2,1)} %bitcast.7), channel_id=1, source_target_pairs={{0,1},{1,2},{2,3},{3,4},{4,5},{5,6},{6,7},{7,0},{8,9},{9,10},{10,1... | collective-permute-start | bytes 1179656 | tf_op jit(solution)/shard_map/ppermute | solution.py:418
  62.9 3.7 %collective-permute-start.1 = (bf16[2,768,128]{2,1,0:T(8,128)(2,1)S(1)}, bf16[2,768,128]{2,1,0:T(8,128)(2,1)}, u32[]{:S(2)}, u32[]{:S(2)}) collective-permute-start(bf16[2,768,128]{2,1,0:T(8,128)(2,1)S(1)} %bitcast.20), channel_id=1, source_target_pairs={{1,0},{2,1},{3,2},{4,3},{5,4},{6,5},{7,6},{0,7},{9,8},{10,9},{11,1... | collective-permute-start | bytes 1179656 | tf_op jit(solution)/shard_map/ppermute | solution.py:419
  66.7 4.2 %collective-permute-done.3.late = bf16[5376,128]{1,0:T(8,128)(2,1)S(1)} collective-permute-done((bf16[5376,128]{1,0:T(8,128)(2,1)}, bf16[5376,128]{1,0:T(8,128)(2,1)S(1)}, u32[]{:S(2)}, u32[]{:S(2)}) %collective-permute-start.3) | collective-permute-done | bytes 1376288 | tf_op jit(solution)/shard_map/ppermute | solution.py:370
  70.9 0.0 copy-done.7
  70.9 0.0 copy-done.5
  70.9 1.2 pad_maximum_fusion.in_other
  72.1 1.9 %collective-permute-done.low = bf16[2,768,128]{2,1,0:T(8,128)(2,1)} collective-permute-done((bf16[2,768,128]{2,1,0:T(8,128)(2,1)}, bf16[2,768,128]{2,1,0:T(8,128)(2,1)}, u32[]{:S(2)}, u32[]{:S(2)}) %collective-permute-start) | collective-permute-done | bytes 393248 | tf_op jit(solution)/shard_map/ppermute | solution.py:418
  74.0 0.8 collective-permute-done.1.high
  74.8 0.0 copy-done.6
  74.8 9.5 %shard_map.94 = (bf16[4,768,128]{2,1,0:T(8,128)(2,1)}, bf16[2,768,128]{2,1,0:T(8,128)(2,1)}, bf16[2,768,128]{2,1,0:T(8,128)(2,1)}, bf16[2,192,2304]{2,1,0:T(8,128)(2,1)}, bf16[2,192,256]{2,1,0:T(8,128)(2,1)}) custom-call(s32[1]{0:T(128)} %bitcast.4.odd_ref, bf16[4,768,128]{2,1,0:T(8,128)(2,1)} %bitcast.14, bf16[2,768,128]{2,1,0:T(8,128)(2,1)} %collective-permute-done.low, ...), custom_call_target="tpu_custom_call" | custom-call | flops 1610612736 | bytes 8912896 | tf_op jit(solution)/shard_map/pallas_call | solution.py:331
  84.3 2.6 %collective-permute-start.4 = (bf16[2,768,128]{2,1,0:T(8,128)(2,1)}, bf16[2,768,128]{2,1,0:T(8,128)(2,1)S(1)}, u32[]{:S(2)}, u32[]{:S(2)}) collective-permute-start(bf16[2,768,128]{2,1,0:T(8,128)(2,1)} %get-tuple-element.26), channel_id=1, source_target_pairs={{0,1},{1,2},{2,3},{3,4},{4,5},{5,6},{6,7},{7,0},{8,9},{9,10},{10,1... | collective-permute-start | bytes 1179656 | tf_op jit(solution)/shard_map/ppermute | solution.py:461
  87.0 4.4 %collective-permute-start.5 = (bf16[2,768,128]{2,1,0:T(8,128)(2,1)}, bf16[2,768,128]{2,1,0:T(8,128)(2,1)S(1)}, u32[]{:S(2)}, u32[]{:S(2)}) collective-permute-start(bf16[2,768,128]{2,1,0:T(8,128)(2,1)} %get-tuple-element.27), channel_id=1, source_target_pairs={{1,0},{2,1},{3,2},{4,3},{5,4},{6,5},{7,6},{0,7},{9,8},{10,9},{11,1... | collective-permute-start | bytes 1179656 | tf_op jit(solution)/shard_map/ppermute | solution.py:462
  91.4 2.5 %collective-permute-start.6 = (bf16[2,192,2304]{2,1,0:T(8,128)(2,1)}, bf16[2,192,2304]{2,1,0:T(8,128)(2,1)}, u32[]{:S(2)}, u32[]{:S(2)}) collective-permute-start(bf16[2,192,2304]{2,1,0:T(8,128)(2,1)} %get-tuple-element.30.rows_ref), channel_id=1, source_target_pairs={{0,8},{1,9},{2,10},{3,11},{4,12},{5,13},{6,14},{7,15},{8,0},{9,1},... | collective-permute-start | bytes 5308424 | tf_op jit(solution)/shard_map/ppermute | solution.py:370
  93.9 3.8 %collective-permute-done.4.low_ref = bf16[2,768,128]{2,1,0:T(8,128)(2,1)S(1)} collective-permute-done((bf16[2,768,128]{2,1,0:T(8,128)(2,1)}, bf16[2,768,128]{2,1,0:T(8,128)(2,1)S(1)}, u32[]{:S(2)}, u32[]{:S(2)}) %collective-permute-start.4) | collective-permute-done | bytes 393248 | tf_op jit(solution)/shard_map/ppermute | solution.py:461
  97.7 1.0 collective-permute-done.5.high_ref
  98.8 1.1 copy-done
  99.9 1.1 shard_map.95
  101.0 16.1 %all-to-all-start.1 = ((bf16[768,4,128]{2,1,0:T(4,128)(2,1)}), bf16[768,4,128]{2,1,0:T(4,128)(2,1)S(1)}, u32[]{:S(2)}, u32[]{:S(2)}) async-start(bf16[768,4,128]{2,1,0:T(4,128)(2,1)} %bitcast.9), calls=%async_computation.1 | async-start | bytes 1572864 | tf_op jit(solution)/shard_map/all_to_all | solution.py:374
  117.1 23.0 %collective-permute-done.6.other_ref = bf16[2,192,2304]{2,1,0:T(8,128)(2,1)} collective-permute-done((bf16[2,192,2304]{2,1,0:T(8,128)(2,1)}, bf16[2,192,2304]{2,1,0:T(8,128)(2,1)}, u32[]{:S(2)}, u32[]{:S(2)}) %collective-permute-start.6) | collective-permute-done | bytes 1769504 | tf_op jit(solution)/shard_map/ppermute | solution.py:370
  140.1 0.0 copy-done.2
  140.1 4.2 %shard_map.97 = (bf16[1,2048,256]{2,1,0:T(8,128)(2,1)}, bf16[1,256,2048]{2,1,0:T(8,128)(2,1)}) custom-call(bf16[2,192,2304]{2,1,0:T(8,128)(2,1)S(1)} %copy-done.2, bf16[2,192,2304]{2,1,0:T(8,128)(2,1)} %collective-permute-done.6.other_ref, bf16[2,192,256]{2,1,0:T(8,128)(2,1)S(1)} %copy-done.3), custom_call_target="tpu_custom_call" | custom-call | flops 1610612736 | bytes 8388608 | tf_op jit(solution)/shard_map/pallas_call | solution.py:331
  144.3 2.0 %all-to-all-done.1 = bf16[768,4,128]{2,1,0:T(4,128)(2,1)S(1)} async-done(((bf16[768,4,128]{2,1,0:T(4,128)(2,1)}), bf16[768,4,128]{2,1,0:T(4,128)(2,1)S(1)}, u32[]{:S(2)}, u32[]{:S(2)}) %all-to-all-start.1) | async-done | bytes 786464 | tf_op jit(solution)/shard_map/all_to_all | solution.py:374
  146.3 0.0 copy-done.1
  146.3 1.1 shard_map.96
  (11 shorter events, 0.1 us)
Async XLA Ops:
  4.6 25.5 %collective-permute-start.2 = (bf16[2816,128]{1,0:T(8,128)(2,1)}, bf16[2816,128]{1,0:T(8,128)(2,1)S(1)}, u32[]{:S(2)}, u32[]{:S(2)}) collective-permute-start(bf16[2816,128]{1,0:T(8,128)(2,1)} %get-tuple-element.21), channel_id=1, source_target_pairs={{0,8},{1,9},{2,10},{3,11},{4,12},{5,13},{6,14},{7,15},{8,0},{9,1},... | collective-permute-start | bytes 2162696 | tf_op jit(solution)/shard_map/ppermute | solution.py:370
  8.6 50.5 %all-to-all-start = ((bf16[768,4,128]{2,1,0:T(4,128)(2,1)}), bf16[768,4,128]{2,1,0:T(4,128)(2,1)S(1)}, u32[]{:S(2)}, u32[]{:S(2)}) async-start(bf16[768,4,128]{2,1,0:T(4,128)(2,1)} %bitcast.19), calls=%async_computation | async-start | bytes 1572864 | tf_op jit(solution)/shard_map/all_to_all | solution.py:374
  30.2 40.7 %copy-start.7 = (bf16[2816,128]{1,0:T(8,128)(2,1)}, bf16[2816,128]{1,0:T(8,128)(2,1)S(1)}, u32[]{:S(2)}) copy-start(bf16[2816,128]{1,0:T(8,128)(2,1)S(1)} %collective-permute-done.2.early) | copy-start | bytes 2162692
  30.2 40.7 %collective-permute-start.3 = (bf16[5376,128]{1,0:T(8,128)(2,1)}, bf16[5376,128]{1,0:T(8,128)(2,1)S(1)}, u32[]{:S(2)}, u32[]{:S(2)}) collective-permute-start(bf16[5376,128]{1,0:T(8,128)(2,1)} %get-tuple-element.24), channel_id=1, source_target_pairs={{0,8},{1,9},{2,10},{3,11},{4,12},{5,13},{6,14},{7,15},{8,0},{9,1},... | collective-permute-start | bytes 4128776 | tf_op jit(solution)/shard_map/ppermute | solution.py:370
  59.1 11.8 %copy-start.5 = (bf16[768,4,128]{2,1,0:T(4,128)(2,1)}, bf16[768,4,128]{2,1,0:T(4,128)(2,1)S(1)}, u32[]{:S(2)}) copy-start(bf16[768,4,128]{2,1,0:T(4,128)(2,1)S(1)} %all-to-all-done) | copy-start | bytes 2359300
  60.1 13.9 %collective-permute-start = (bf16[2,768,128]{2,1,0:T(8,128)(2,1)}, bf16[2,768,128]{2,1,0:T(8,128)(2,1)}, u32[]{:S(2)}, u32[]{:S(2)}) collective-permute-start(bf16[2,768,128]{2,1,0:T(8,128)(2,1)} %bitcast.7), channel_id=1, source_target_pairs={{0,1},{1,2},{2,3},{3,4},{4,5},{5,6},{6,7},{7,0},{8,9},{9,10},{10,1... | collective-permute-start | bytes 1179656 | tf_op jit(solution)/shard_map/ppermute | solution.py:418
  62.9 11.9 %collective-permute-start.1 = (bf16[2,768,128]{2,1,0:T(8,128)(2,1)S(1)}, bf16[2,768,128]{2,1,0:T(8,128)(2,1)}, u32[]{:S(2)}, u32[]{:S(2)}) collective-permute-start(bf16[2,768,128]{2,1,0:T(8,128)(2,1)S(1)} %bitcast.20), channel_id=1, source_target_pairs={{1,0},{2,1},{3,2},{4,3},{5,4},{6,5},{7,6},{0,7},{9,8},{10,9},{11,1... | collective-permute-start | bytes 1179656 | tf_op jit(solution)/shard_map/ppermute | solution.py:419
  70.9 4.0 %copy-start.6 = (bf16[5376,128]{1,0:T(8,128)(2,1)}, bf16[5376,128]{1,0:T(8,128)(2,1)S(1)}, u32[]{:S(2)}) copy-start(bf16[5376,128]{1,0:T(8,128)(2,1)S(1)} %collective-permute-done.3.late) | copy-start | bytes 4128772
  84.3 13.4 %collective-permute-start.4 = (bf16[2,768,128]{2,1,0:T(8,128)(2,1)}, bf16[2,768,128]{2,1,0:T(8,128)(2,1)S(1)}, u32[]{:S(2)}, u32[]{:S(2)}) collective-permute-start(bf16[2,768,128]{2,1,0:T(8,128)(2,1)} %get-tuple-element.26), channel_id=1, source_target_pairs={{0,1},{1,2},{2,3},{3,4},{4,5},{5,6},{6,7},{7,0},{8,9},{9,10},{10,1... | collective-permute-start | bytes 1179656 | tf_op jit(solution)/shard_map/ppermute | solution.py:461
  87.0 11.8 %collective-permute-start.5 = (bf16[2,768,128]{2,1,0:T(8,128)(2,1)}, bf16[2,768,128]{2,1,0:T(8,128)(2,1)S(1)}, u32[]{:S(2)}, u32[]{:S(2)}) collective-permute-start(bf16[2,768,128]{2,1,0:T(8,128)(2,1)} %get-tuple-element.27), channel_id=1, source_target_pairs={{1,0},{2,1},{3,2},{4,3},{5,4},{6,5},{7,6},{0,7},{9,8},{10,9},{11,1... | collective-permute-start | bytes 1179656 | tf_op jit(solution)/shard_map/ppermute | solution.py:462
  91.4 48.7 %collective-permute-start.6 = (bf16[2,192,2304]{2,1,0:T(8,128)(2,1)}, bf16[2,192,2304]{2,1,0:T(8,128)(2,1)}, u32[]{:S(2)}, u32[]{:S(2)}) collective-permute-start(bf16[2,192,2304]{2,1,0:T(8,128)(2,1)} %get-tuple-element.30.rows_ref), channel_id=1, source_target_pairs={{0,8},{1,9},{2,10},{3,11},{4,12},{5,13},{6,14},{7,15},{8,0},{9,1},... | collective-permute-start | bytes 5308424 | tf_op jit(solution)/shard_map/ppermute | solution.py:370
  98.8 1.1 copy-start
  99.9 40.2 %copy-start.2 = (bf16[2,192,2304]{2,1,0:T(8,128)(2,1)S(1)}, bf16[2,192,2304]{2,1,0:T(8,128)(2,1)}, u32[]{:S(2)}) copy-start(bf16[2,192,2304]{2,1,0:T(8,128)(2,1)} %get-tuple-element.30.rows_ref) | copy-start | bytes 5308420
  99.9 40.2 %copy-start.3 = (bf16[2,192,256]{2,1,0:T(8,128)(2,1)S(1)}, bf16[2,192,256]{2,1,0:T(8,128)(2,1)}, u32[]{:S(2)}) copy-start(bf16[2,192,256]{2,1,0:T(8,128)(2,1)} %get-tuple-element.31.own_ref) | copy-start | bytes 589828
  101.0 45.4 %all-to-all-start.1 = ((bf16[768,4,128]{2,1,0:T(4,128)(2,1)}), bf16[768,4,128]{2,1,0:T(4,128)(2,1)S(1)}, u32[]{:S(2)}, u32[]{:S(2)}) async-start(bf16[768,4,128]{2,1,0:T(4,128)(2,1)} %bitcast.9), calls=%async_computation.1 | async-start | bytes 1572864 | tf_op jit(solution)/shard_map/all_to_all | solution.py:374
  140.1 6.2 %copy-start.1 = (f32[128,2]{0,1:T(2,128)S(1)}, f32[128,2]{0,1:T(2,128)}, u32[]{:S(2)}) copy-start(f32[128,2]{0,1:T(2,128)} %param.8) | copy-start | bytes 3076
  140.1 6.2 %copy-start.4 = (s32[2,128]{1,0:T(2,128)S(1)}, s32[2,128]{1,0:T(2,128)}, u32[]{:S(2)}) copy-start(s32[2,128]{1,0:T(2,128)} %get-tuple-element.19.rows_ref) | copy-start | bytes 3076
